TPU v7x, 512 devices: a whole 4x8x8 slice. The times are simulated.
512 devices in a mesh: seq: 32 (over x, z), tensor: 16 (over y, core).
Axes of the slice: x: 4, y: 8, z: 8, core: 2. Of those that a mesh axis runs over, the one named last changes fastest.
Arguments:
- text_hidden: bfloat16 [4096, 8192], P('seq', 'tensor'), may hold values from -1500 to 1500
- patches: bfloat16 [4096, 8192], P('seq', 'tensor'), may hold values from -1500 to 1500
- norm_gain: float32 [8192], replicated, may hold values from 0.5 to 1.5
- head_weight: bfloat16 [152064, 8192], P(('seq', 'tensor')), may hold values from -2 to 2
- image_rows: int32 [4096], P('seq'), may hold values from -1 to 4095, as said below
- patch_owner: int32 [4096], P('seq'), may hold values from -1 to 4095, as said below
- nucleus: int32 [4096, 32], P('seq'), may hold values from 0 to 511, as said below
- sampled_code: int32 [4096], P('seq'), may hold values from 0 to 9503
Outputs:
- logprob: float32 [4096], P('seq')
Inputs may be any that keep to these rules, and one draw needn't show every extreme that they name: `image_rows`: image tokens come in aligned blocks of 64 positions, filled in order by 64 consecutive patch rows that start at a multiple of 64 within one encoder shard's 128 rows; the images of one sequence shard come from different encoder shards; some sequence shard is all image tokens. The inverse of image_rows: patch row q fills token patch_owner[q], or none for -1. `nucleus`: A token's 32 blocks are distinct. Among the rows of one sequence shard (aligned blocks of 128 rows) no block appears more than 10 times, and some block appears exactly 10 times in every shard.
All inputs are finite; a program needn't handle non-finite values.
Results may differ from a plain program's by a relative error of at most 0.00078.
Values may be sent and summed in bfloat16 or wider, within the bound.
No kernel may reach another device: no remote copies, remote signals or barrier semaphores. Data moves between devices by JAX's collectives and lax.ppermute only.
A program may use at most 64 MiB of HBM per device.

v0:
```python
import jax
import jax.numpy as jnp
from jax import lax
from jax.sharding import PartitionSpec as P

D = 8192
VB = 297
IMG = 64


sharpness_divisor = 0.7
epsilon = 1e-06
floor_value = -1e30


def block_scores(input_rows, offsets_in, coefficient_matrix):
    unnormalized_energies = jnp.einsum(
        "ujl,al->uja", input_rows, coefficient_matrix, preferred_element_type=jnp.float32
    )
    rating_numbers = unnormalized_energies / sharpness_divisor
    peak = jnp.max(rating_numbers, axis=-1)
    total = jnp.sum(jnp.exp(rating_numbers - peak[..., None]), axis=-1)
    column = lax.broadcasted_iota(jnp.int32, rating_numbers.shape, 2)
    picked = jnp.sum(jnp.where(column == offsets_in[..., None], rating_numbers, 0.0), axis=-1)
    return (peak, total, picked)


def per_device(
    text_hidden, patches, norm_gain, head_weight, image_rows, patch_owner, nucleus, sampled_code
):
    shards = lax.axis_size("seq")
    tensor_count = lax.axis_size("tensor")
    column_here = lax.axis_index("tensor")
    tok_rows = text_hidden.shape[0]
    width = text_hidden.shape[1]
    image_blocks = tok_rows // IMG
    shard_ids = jnp.arange(shards, dtype=jnp.int32)
    owners = patch_owner.reshape(image_blocks, IMG)[:, 0]
    target_shard = jnp.where(owners >= 0, owners // tok_rows, -1)
    sending = (target_shard[None, :] == shard_ids[:, None]).astype(jnp.bfloat16)
    outgoing = jnp.dot(
        sending, patches.reshape(image_blocks, IMG * width), preferred_element_type=jnp.float32
    ).astype(jnp.bfloat16)
    arrived = lax.all_to_all(
        outgoing.reshape(shards, IMG, width), "seq", split_axis=0, concat_axis=0, tiled=True
    )
    firsts = image_rows.reshape(image_blocks, IMG)[:, 0]
    sender_partition = jnp.where(firsts >= 0, firsts // tok_rows, -1)
    taking = (sender_partition[:, None] == shard_ids[None, :]).astype(jnp.bfloat16)
    placed = jnp.dot(
        taking, arrived.reshape(shards, IMG * width), preferred_element_type=jnp.float32
    ).astype(jnp.bfloat16)
    merged = jnp.where(image_rows[:, None] >= 0, placed.reshape(tok_rows, width), text_hidden)
    values = merged.astype(jnp.float32)
    squares = lax.psum(jnp.sum(values * values, axis=-1), "tensor")
    gain_part = lax.dynamic_slice_in_dim(norm_gain, column_here * width, width, 0)
    normed_part = (values * lax.rsqrt(squares / D + epsilon)[:, None] * gain_part[None, :]).astype(
        jnp.bfloat16
    )
    embedding_lines = lax.all_gather(normed_part, "tensor", axis=1, tiled=True)
    blocks_flat = nucleus.reshape(-1)
    pairs = blocks_flat.shape[0]
    per_token = nucleus.shape[1]
    room = 5 * tok_rows // (4 * tensor_count)
    mine = blocks_flat % tensor_count == column_here
    keyed = jnp.where(mine, blocks_flat // tensor_count, shards)
    order = jnp.argsort(keyed, stable=True)
    ordered = keyed[order]
    first = jnp.searchsorted(ordered, ordered, side="left")
    counting = jnp.arange(pairs, dtype=jnp.int32)
    rank = jnp.zeros((pairs,), jnp.int32).at[order].set(counting - first)
    slot = jnp.where(mine, keyed * room + rank, shards * room)
    slot_pair = jnp.full((shards * room,), pairs, jnp.int32).at[slot].set(counting, mode="drop")
    filled = slot_pair < pairs
    safe = jnp.minimum(slot_pair, pairs - 1)
    token_of = safe // per_token
    entry_of = safe % per_token
    code = sampled_code[token_of]
    offsets = jnp.where(filled & (entry_of == code // VB), code % VB, -1).reshape(shards, room)
    outgoing_rows = embedding_lines[token_of].reshape(shards, room, embedding_lines.shape[1])
    peak, total, picked = block_scores(
        lax.all_to_all(outgoing_rows, "seq", split_axis=0, concat_axis=0, tiled=True),
        lax.all_to_all(offsets, "seq", split_axis=0, concat_axis=0, tiled=True),
        head_weight,
    )
    peak, total, picked = (
        lax.all_to_all(peak, "seq", split_axis=0, concat_axis=0, tiled=True),
        lax.all_to_all(total, "seq", split_axis=0, concat_axis=0, tiled=True),
        lax.all_to_all(picked, "seq", split_axis=0, concat_axis=0, tiled=True),
    )
    peak = peak.reshape(-1)
    total = total.reshape(-1)
    picked = picked.reshape(-1)
    member = (token_of[:, None] == jnp.arange(tok_rows, dtype=jnp.int32)[None, :]) & filled[:, None]
    local_peak = jnp.max(jnp.where(member, peak[:, None], floor_value), axis=0)
    scaled = jnp.exp(jnp.where(member, peak[:, None] - local_peak[None, :], floor_value))
    partial_total_sum = jnp.sum(scaled * total[:, None], axis=0)
    local_pick = jnp.sum(jnp.where(member, picked[:, None], 0.0), axis=0)
    top = lax.pmax(local_peak, "tensor")
    summed, chosen = lax.psum((partial_total_sum * jnp.exp(local_peak - top), local_pick), "tensor")
    return chosen - top - jnp.log(summed)


def solution(mesh):
    return jax.shard_map(
        per_device,
        mesh=mesh,
        in_specs=(
            P("seq", "tensor"),
            P("seq", "tensor"),
            P(),
            P(("seq", "tensor"), None),
            P("seq"),
            P("seq"),
            P("seq", None),
            P("seq"),
        ),
        out_specs=P("seq"),
        check_vma=False,
    )
```

profile of v0, /device:TPU:1, one launch (start us, length us, event | category | flops | bytes accessed | tf_op | source)
XLA Modules:
  0.0 781.8 jit_solution(9819206307973891304)
XLA Ops:
  11.2 13.7 %all-to-all-start.1 = ((bf16[32,64,512]{2,1,0:T(8,128)(2,1)}), bf16[32,64,512]{2,1,0:T(8,128)(2,1)S(1)}, u32[]{:S(2)}, u32[]{:S(2)}) async-start(bf16[32,64,512]{2,1,0:T(8,128)(2,1)} %bitcast.19), calls=%async_computation.1 | async-start | bytes 4194304 | tf_op jit(solution)/shard_map/all_to_all | solution.py:44
  31.1 23.0 %gather_fusion.1 = s32[4096]{0:T(1024)S(1)} fusion(s32[4096]{0:T(1024)S(1)} %fusion.13, s32[4096]{0:T(1024)S(1)} %get-tuple-element.108), kind=kCustom, calls=%fused_computation.1 | custom fusion | bytes 49152 | tf_op jit(solution)/shard_map/gather | solution.py:68
  55.1 18.8 %all-to-all-done.1 = bf16[32,64,512]{2,1,0:T(8,128)(2,1)S(1)} async-done(((bf16[32,64,512]{2,1,0:T(8,128)(2,1)}), bf16[32,64,512]{2,1,0:T(8,128)(2,1)S(1)}, u32[]{:S(2)}, u32[]{:S(2)}) %all-to-all-start.1) | async-done | bytes 2097184 | tf_op jit(solution)/shard_map/all_to_all | solution.py:44
  75.7 25.6 %psum.21 = f32[128]{0:T(128)S(1)} all-reduce(f32[128]{0:T(128)S(1)} %fusion.8), channel_id=1, replica_groups=mesh['seq'=32,'tensor'=16] {'tensor'}, use_global_device_ids=true, to_apply=%region_6.7 | all-reduce | flops 128 | bytes 1024 | tf_op jit(solution)/shard_map/psum | solution.py:55
  102.2 300.6 %while.25 = (s32[]{:T(128)}, u32[4096]{0:T(1024)S(1)}, u32[4096]{0:T(1024)S(1)}, s32[4096]{0:T(1024)S(1)}, s32[]{:T(128)}, /*index=5*/s32[]{:T(128)}, s32[]{}) while((s32[]{:T(128)}, u32[4096]{0:T(1024)S(1)}, u32[4096]{0:T(1024)S(1)}, s32[4096]{0:T(1024)S(1)}, s32[]{:T(128)}, /*index=5*/s32[]{:T(128)}, s32[]{}) %tuple.41), condition=%wide.region_2.3_spmd.clone, body=%wide.region_1.2_spmd.clone.sunk | while | flops 77828 | bytes 270445 | solution.py:69
  102.2 23.0 %gather_fusion = s32[4096]{0:T(1024)S(1)} fusion(s32[4096]{0:T(1024)S(1)} %get-tuple-element.158, u32[4096]{0:T(1024)S(1)} %broadcast_clamp_fusion.3), kind=kCustom, calls=%fused_computation.clone.clone.1 | custom fusion | bytes 49152 | tf_op jit(solution)/shard_map/jit(searchsorted)/jit(_searchsorted_scan_impl)/vmap(jit(_searchsorted_scan_impl))/while/body/eval_jaxpr/gather | solution.py:69
  125.4 23.0 %gather_fusion = s32[4096]{0:T(1024)S(1)} fusion(s32[4096]{0:T(1024)S(1)} %get-tuple-element.158, u32[4096]{0:T(1024)S(1)} %broadcast_clamp_fusion.3), kind=kCustom, calls=%fused_computation.clone.clone.1 | custom fusion | bytes 49152 | tf_op jit(solution)/shard_map/jit(searchsorted)/jit(_searchsorted_scan_impl)/vmap(jit(_searchsorted_scan_impl))/while/body/eval_jaxpr/gather | solution.py:69
  148.5 23.0 %gather_fusion = s32[4096]{0:T(1024)S(1)} fusion(s32[4096]{0:T(1024)S(1)} %get-tuple-element.158, u32[4096]{0:T(1024)S(1)} %broadcast_clamp_fusion.3), kind=kCustom, calls=%fused_computation.clone.clone.1 | custom fusion | bytes 49152 | tf_op jit(solution)/shard_map/jit(searchsorted)/jit(_searchsorted_scan_impl)/vmap(jit(_searchsorted_scan_impl))/while/body/eval_jaxpr/gather | solution.py:69
  171.6 23.0 %gather_fusion = s32[4096]{0:T(1024)S(1)} fusion(s32[4096]{0:T(1024)S(1)} %get-tuple-element.158, u32[4096]{0:T(1024)S(1)} %broadcast_clamp_fusion.3), kind=kCustom, calls=%fused_computation.clone.clone.1 | custom fusion | bytes 49152 | tf_op jit(solution)/shard_map/jit(searchsorted)/jit(_searchsorted_scan_impl)/vmap(jit(_searchsorted_scan_impl))/while/body/eval_jaxpr/gather | solution.py:69
  194.7 23.0 %gather_fusion = s32[4096]{0:T(1024)S(1)} fusion(s32[4096]{0:T(1024)S(1)} %get-tuple-element.158, u32[4096]{0:T(1024)S(1)} %broadcast_clamp_fusion.3), kind=kCustom, calls=%fused_computation.clone.clone.1 | custom fusion | bytes 49152 | tf_op jit(solution)/shard_map/jit(searchsorted)/jit(_searchsorted_scan_impl)/vmap(jit(_searchsorted_scan_impl))/while/body/eval_jaxpr/gather | solution.py:69
  217.9 23.0 %gather_fusion = s32[4096]{0:T(1024)S(1)} fusion(s32[4096]{0:T(1024)S(1)} %get-tuple-element.158, u32[4096]{0:T(1024)S(1)} %broadcast_clamp_fusion.3), kind=kCustom, calls=%fused_computation.clone.clone.1 | custom fusion | bytes 49152 | tf_op jit(solution)/shard_map/jit(searchsorted)/jit(_searchsorted_scan_impl)/vmap(jit(_searchsorted_scan_impl))/while/body/eval_jaxpr/gather | solution.py:69
  241.0 23.0 %gather_fusion = s32[4096]{0:T(1024)S(1)} fusion(s32[4096]{0:T(1024)S(1)} %get-tuple-element.158, u32[4096]{0:T(1024)S(1)} %broadcast_clamp_fusion.3), kind=kCustom, calls=%fused_computation.clone.clone.1 | custom fusion | bytes 49152 | tf_op jit(solution)/shard_map/jit(searchsorted)/jit(_searchsorted_scan_impl)/vmap(jit(_searchsorted_scan_impl))/while/body/eval_jaxpr/gather | solution.py:69
  264.1 23.0 %gather_fusion = s32[4096]{0:T(1024)S(1)} fusion(s32[4096]{0:T(1024)S(1)} %get-tuple-element.158, u32[4096]{0:T(1024)S(1)} %broadcast_clamp_fusion.3), kind=kCustom, calls=%fused_computation.clone.clone.1 | custom fusion | bytes 49152 | tf_op jit(solution)/shard_map/jit(searchsorted)/jit(_searchsorted_scan_impl)/vmap(jit(_searchsorted_scan_impl))/while/body/eval_jaxpr/gather | solution.py:69
  287.2 23.0 %gather_fusion = s32[4096]{0:T(1024)S(1)} fusion(s32[4096]{0:T(1024)S(1)} %get-tuple-element.158, u32[4096]{0:T(1024)S(1)} %broadcast_clamp_fusion.3), kind=kCustom, calls=%fused_computation.clone.clone.1 | custom fusion | bytes 49152 | tf_op jit(solution)/shard_map/jit(searchsorted)/jit(_searchsorted_scan_impl)/vmap(jit(_searchsorted_scan_impl))/while/body/eval_jaxpr/gather | solution.py:69
  310.4 23.0 %gather_fusion = s32[4096]{0:T(1024)S(1)} fusion(s32[4096]{0:T(1024)S(1)} %get-tuple-element.158, u32[4096]{0:T(1024)S(1)} %broadcast_clamp_fusion.3), kind=kCustom, calls=%fused_computation.clone.clone.1 | custom fusion | bytes 49152 | tf_op jit(solution)/shard_map/jit(searchsorted)/jit(_searchsorted_scan_impl)/vmap(jit(_searchsorted_scan_impl))/while/body/eval_jaxpr/gather | solution.py:69
  333.5 23.0 %gather_fusion = s32[4096]{0:T(1024)S(1)} fusion(s32[4096]{0:T(1024)S(1)} %get-tuple-element.158, u32[4096]{0:T(1024)S(1)} %broadcast_clamp_fusion.3), kind=kCustom, calls=%fused_computation.clone.clone.1 | custom fusion | bytes 49152 | tf_op jit(solution)/shard_map/jit(searchsorted)/jit(_searchsorted_scan_impl)/vmap(jit(_searchsorted_scan_impl))/while/body/eval_jaxpr/gather | solution.py:69
  356.6 23.0 %gather_fusion = s32[4096]{0:T(1024)S(1)} fusion(s32[4096]{0:T(1024)S(1)} %get-tuple-element.158, u32[4096]{0:T(1024)S(1)} %broadcast_clamp_fusion.3), kind=kCustom, calls=%fused_computation.clone.clone.1 | custom fusion | bytes 49152 | tf_op jit(solution)/shard_map/jit(searchsorted)/jit(_searchsorted_scan_impl)/vmap(jit(_searchsorted_scan_impl))/while/body/eval_jaxpr/gather | solution.py:69
  379.7 23.0 %gather_fusion = s32[4096]{0:T(1024)S(1)} fusion(s32[4096]{0:T(1024)S(1)} %get-tuple-element.158, u32[4096]{0:T(1024)S(1)} %broadcast_clamp_fusion.3), kind=kCustom, calls=%fused_computation.clone.clone.1 | custom fusion | bytes 49152 | tf_op jit(solution)/shard_map/jit(searchsorted)/jit(_searchsorted_scan_impl)/vmap(jit(_searchsorted_scan_impl))/while/body/eval_jaxpr/gather | solution.py:69
  402.9 15.5 %scatter_custom_fusion = s32[4096]{0:T(1024)S(1)} fusion(s32[4096]{0:T(1024)S(1)} %get-tuple-element.109, s32[4096]{0:T(1024)S(1)} %convert_subtract_fusion, s32[]{:T(128)} %constant.131.clone.1), kind=kCustom, calls=%fused_computation.46 | custom fusion | bytes 16388 | tf_op jit(solution)/shard_map/scatter | solution.py:71
  418.4 15.5 %scatter_custom_fusion.1 = s32[320]{0:T(512)S(1)} fusion(s32[4096]{0:T(1024)S(1)} %compare_select_fusion, s32[4096]{0:T(1024)S(1)} %iota.27, s32[]{:T(128)} %constant.130.clone.1), kind=kCustom, calls=%fused_computation.79 | custom fusion | bytes 1284 | tf_op jit(solution)/shard_map/scatter | solution.py:73
  443.1 16.4 %gather_fusion.3 = bf16[320,8192]{1,0:T(8,128)(2,1)} fusion(bf16[128,8192]{1,0:T(8,128)(2,1)} %all-gather.2.cloned.1.call-done, s32[1024]{0:T(1024)S(1)} %pad_clamp_fusion), kind=kCustom, calls=%fused_computation.3 | custom fusion | bytes 10487040 | tf_op jit(solution)/shard_map/gather | solution.py:80
  477.1 182.0 %all-to-all-done.2 = bf16[32,10,8192]{2,1,0:T(8,128)(2,1)} async-done(((bf16[32,10,8192]{2,1,0:T(8,128)(2,1)}), bf16[32,10,8192]{2,1,0:T(8,128)(2,1)}, u32[]{:S(2)}, u32[]{:S(2)}) %all-to-all-start.2) | async-done | bytes 5242912 | tf_op jit(solution)/shard_map/all_to_all | solution.py:82
  715.1 36.0 %pmax.7 = f32[128]{0:T(128)S(1)} all-reduce(f32[128]{0:T(128)S(1)} %get-tuple-element.93), channel_id=1, replica_groups=mesh['seq'=32,'tensor'=16] {'tensor'}, use_global_device_ids=true, to_apply=%region_12.13 | all-reduce | flops 128 | bytes 1024 | tf_op jit(solution)/shard_map/pmax | solution.py:99
  751.3 23.1 %all-reduce = (f32[128]{0:T(128)S(1)}, f32[128]{0:T(128)S(1)}) all-reduce(f32[128]{0:T(128)S(1)} %exponential_multiply_fusion, f32[128]{0:T(128)S(1)} %get-tuple-element.92), channel_id=1, replica_groups=mesh['seq'=32,'tensor'=16] {'tensor'}, use_global_device_ids=true, to_apply=%region_15.16 | all-reduce | flops 256 | bytes 2048 | tf_op jit(solution)/shard_map/psum | solution.py:100
  (123 shorter events, 98.3 us)
Async XLA Ops:
  6.5 427.4 %copy-start = (s32[128]{0:T(128)S(1)}, s32[128]{0:T(128)}, u32[]{:S(2)}) copy-start(s32[128]{0:T(128)} %param.17) | copy-start | bytes 1540
  8.4 16.6 %copy-start.3 = (s32[128]{0:T(128)S(1)}, s32[128]{0:T(128)}, u32[]{:S(2)}) copy-start(s32[128]{0:T(128)} %param.14) | copy-start | bytes 1540
  8.4 16.7 %copy-start.2 = (s32[128,32]{0,1:T(8,128)S(1)}, s32[128,32]{0,1:T(8,128)}, u32[]{:S(2)}) copy-start(s32[128,32]{0,1:T(8,128)} %param.16) | copy-start | bytes 49156
  11.2 62.6 %all-to-all-start.1 = ((bf16[32,64,512]{2,1,0:T(8,128)(2,1)}), bf16[32,64,512]{2,1,0:T(8,128)(2,1)S(1)}, u32[]{:S(2)}, u32[]{:S(2)}) async-start(bf16[32,64,512]{2,1,0:T(8,128)(2,1)} %bitcast.19), calls=%async_computation.1 | async-start | bytes 4194304 | tf_op jit(solution)/shard_map/all_to_all | solution.py:44
  24.9 418.2 %all-gather.2.cloned.1.call-start = ((), (), s32[]{:S(2)}) async-start(), calls=%async_computation.6 | async-start | bytes 2228224 | tf_op jit(solution)/shard_map/all_gather | solution.py:60
  54.1 21.4 %copy-start.1 = (bf16[128,512]{1,0:T(8,128)(2,1)S(1)}, bf16[128,512]{1,0:T(8,128)(2,1)}, u32[]{:S(2)}) copy-start(bf16[128,512]{1,0:T(8,128)(2,1)} %param.10) | copy-start | bytes 393220
  437.1 30.8 %all-to-all-start = ((s32[32,1,10]{2,1,0:T(1,128)}), s32[32,1,10]{2,1,0:T(1,128)S(1)}, u32[]{:S(2)}, u32[]{:S(2)}) async-start(s32[32,1,10]{2,1,0:T(1,128)} %bitcast), calls=%async_computation | async-start | bytes 32768 | tf_op jit(solution)/shard_map/all_to_all | solution.py:83
  467.9 191.2 %all-to-all-start.2 = ((bf16[32,10,8192]{2,1,0:T(8,128)(2,1)}), bf16[32,10,8192]{2,1,0:T(8,128)(2,1)}, u32[]{:S(2)}, u32[]{:S(2)}) async-start(bf16[32,10,8192]{2,1,0:T(8,128)(2,1)} %reshape.90), calls=%async_computation.2 | async-start | bytes 16777216 | tf_op jit(solution)/shard_map/all_to_all | solution.py:82
  668.6 20.6 %all-to-all-start.5 = ((f32[32,1,10]{2,1,0:T(1,128)}), f32[32,1,10]{2,1,0:T(1,128)S(1)}, u32[]{:S(2)}, u32[]{:S(2)}) async-start(f32[32,1,10]{2,1,0:T(1,128)} %copy.26), calls=%async_computation.5 | async-start | bytes 32768 | tf_op jit(solution)/shard_map/all_to_all | solution.py:88
  689.1 12.5 %all-to-all-start.3 = ((f32[32,1,10]{2,1,0:T(1,128)}), f32[32,1,10]{2,1,0:T(1,128)S(1)}, u32[]{:S(2)}, u32[]{:S(2)}) async-start(f32[32,1,10]{2,1,0:T(1,128)} %copy.24), calls=%async_computation.3 | async-start | bytes 32768 | tf_op jit(solution)/shard_map/all_to_all | solution.py:89
  701.6 12.4 %all-to-all-start.4 = ((f32[32,1,10]{2,1,0:T(1,128)}), f32[32,1,10]{2,1,0:T(1,128)S(1)}, u32[]{:S(2)}, u32[]{:S(2)}) async-start(f32[32,1,10]{2,1,0:T(1,128)} %copy.25), calls=%async_computation.4 | async-start | bytes 32768 | tf_op jit(solution)/shard_map/all_to_all | solution.py:87
Sparse Core Ops, SparseCore 0:
  102.3 39.3 all-gather.1
where the time goes:
time: 783 us; the launch traced here: 782 us
  local copies, waits for them, and re-layouts  391 us (50%)
  waiting for transfers between devices  223 us (28%)
  blocking collectives  84.7 us (11%)
  starting transfers between devices  48.5 us (6%)
  between operations  13.7 us (2%)
  other arithmetic  10.9 us (1%)
  matrix products  9.59 us (1%)
    gather x13, local copies, waits for them, and re-layouts, per_device(): first = jnp.searchsorted(ordered, ordered, side='left')  299 us
    all_to_all x1, waiting for transfers between devices, per_device(): lax.all_to_all(outgoing_rows, 'seq', split_axis=0, concat_axis=0, tiled=T...  182 us
    pmax x1, blocking collectives, per_device(): top = lax.pmax(local_peak, 'tensor')  36 us
    psum x1, blocking collectives, per_device(): squares = lax.psum(jnp.sum(values * values, axis=-1), 'tensor')  25.6 us
    psum x1, blocking collectives, per_device(): lax.psum((partial_total_sum * jnp.exp(local_peak - top), local_pick), 'te...  23.1 us
    gather x1, local copies, waits for them, and re-layouts, per_device(): ordered = keyed[order]  23 us
    all_to_all x1, waiting for transfers between devices, per_device(): lax.all_to_all(outgoing.reshape(shards, IMG, width), 'seq', split_axis=0,...  18.8 us
    gather x1, local copies, waits for them, and re-layouts, per_device(): embedding_lines[token_of].reshape(shards, room, embedding_lines.shape[1])  16.4 us
  transfers between devices with their start and end apart: 7, of which 5 were waited for; matrix products, arithmetic and copies ran while one was open for 50% of the time, Pallas kernels for 0%

commit v1 on v0

v1 whole, which is shorter than its diff:
```python
import jax
import jax.numpy as jnp
from jax import lax
from jax.sharding import Mesh
from jax.sharding import PartitionSpec as P

D = 8192
VB = 297
VP = 304
IMG = 64
CAP = 10
GROUP = 4

sharpness_divisor = 0.7
epsilon = 1e-06
floor_value = -1e30

SEQ = ("x", "z")
TEN = ("core", "y")


def exchange(value, axis):
    return lax.all_to_all(value, axis, split_axis=0, concat_axis=0, tiled=True)


def pack(scores):
    tail = scores[..., 256:]
    tail = jnp.concatenate([tail[..., : VP // 2, :], tail[..., VP // 2 :, :]], axis=-1)
    return jnp.concatenate([scores[..., :128], scores[..., 128:256], tail], axis=-2)


def unpack(packed):
    tail = packed[..., 2 * VP :, :]
    tail = jnp.concatenate([tail[..., :64], tail[..., 64:]], axis=-2)
    return jnp.concatenate([packed[..., :VP, :], packed[..., VP : 2 * VP, :], tail], axis=-1)


def per_device(text, patches, norm_gain, head, image_rows, patch_owner, nucleus, code):
    del patch_owner
    shards = lax.axis_size(SEQ)
    columns = lax.axis_size(TEN)
    cores, chips = lax.axis_size("core"), lax.axis_size("y")
    y, core = lax.axis_index("y"), lax.axis_index("core")
    place = y * cores + core
    number = core * chips + y
    tokens, width = text.shape
    slots = tokens // IMG
    blocks = shards * columns
    members = shards * CAP

    pieces = head.reshape(VB, chips, cores, width).transpose(2, 1, 0, 3).reshape(columns, VB, width)
    head_here = exchange(pieces, TEN)

    both = jnp.concatenate([text, patches], axis=0)
    everyone = lax.all_gather(both, SEQ, axis=0, tiled=True)

    with jax.named_scope("routing"):
        ids = jnp.arange(blocks, dtype=jnp.int32)
        named = jnp.any(nucleus[:, :, None] == ids[None, None, :], axis=1)
        lower = (jnp.arange(tokens)[:, None] > jnp.arange(tokens)[None, :]).astype(jnp.bfloat16)
        rank = jnp.dot(lower, named.astype(jnp.bfloat16), preferred_element_type=jnp.float32).astype(jnp.int32)
        entry = jnp.arange(nucleus.shape[1], dtype=jnp.int32)
        target = jnp.sum(jnp.where(entry[None, :] == (code // VB)[:, None], nucleus, 0), axis=1)
        mark = jnp.where(target[:, None] == ids[None, :], (code % VB + 1)[:, None], 0)
        value = (jnp.arange(tokens, dtype=jnp.int32)[:, None] + 1) * 512 + mark
        rank = jnp.where(named, rank, -1)
        slot = jnp.arange(CAP, dtype=jnp.int32)
        lists = jnp.sum(jnp.where(rank[None] == slot[:, None, None], value[None], 0), axis=1)
        lists = lists.reshape(CAP, shards, chips, cores).transpose(1, 3, 2, 0).reshape(shards, columns, CAP)

    squares = jnp.sum(jnp.square(both.astype(jnp.float32)), axis=1)
    squares = lax.psum(squares, TEN)
    firsts = image_rows.reshape(slots, IMG)[:, 0].astype(jnp.float32)
    common = jnp.concatenate([squares, firsts])
    message = jnp.concatenate(
        [
            lists.reshape(shards, columns * CAP).astype(jnp.float32),
            jnp.broadcast_to(common[None, :], (shards, common.shape[0])),
        ],
        axis=1,
    )
    told = exchange(message, SEQ)
    told_lists = told[:, : columns * CAP].astype(jnp.int32).reshape(shards, columns, CAP)
    told_squares = told[:, columns * CAP : columns * CAP + 2 * tokens]
    told_firsts = told[:, columns * CAP + 2 * tokens :].astype(jnp.int32)

    with jax.named_scope("merge"):
        own_unit = jnp.arange(shards, dtype=jnp.int32)[:, None] * (2 * slots) + jnp.arange(slots, dtype=jnp.int32)[None, :]
        patch_unit = (told_firsts // tokens) * (2 * slots) + slots + (told_firsts % tokens) // IMG
        unit = jnp.where(told_firsts >= 0, patch_unit, own_unit).reshape(-1)
        pick = unit[:, None] == jnp.arange(shards * 2 * slots, dtype=jnp.int32)[None, :]
        units = everyone.reshape(shards * 2 * slots, IMG * width)
        merged = jnp.dot(pick.astype(jnp.bfloat16), units, preferred_element_type=jnp.float32)
        unit_squares = told_squares.reshape(1, shards * 2 * slots, IMG)
        row_squares = jnp.sum(jnp.where(pick[:, :, None], unit_squares, 0.0), axis=1)
        scale = lax.rsqrt(row_squares / D + epsilon)
        gain = lax.dynamic_slice_in_dim(norm_gain, place * width, width, 0)
        normed = (merged.reshape(shards * slots, IMG, width) * scale[:, :, None] * gain).astype(jnp.bfloat16)

    with jax.named_scope("partial"):
        groups = shards // GROUP
        token_of = told_lists // 512 - 1 + (jnp.arange(shards, dtype=jnp.int32) % GROUP * tokens)[:, None, None]
        token_of = jnp.where(told_lists > 0, token_of, -1)
        token_of = token_of.reshape(groups, GROUP, columns, CAP).transpose(0, 2, 1, 3).reshape(groups, columns * GROUP * CAP)
        hot = (token_of[:, :, None] == jnp.arange(GROUP * tokens, dtype=jnp.int32)).astype(jnp.bfloat16)
        rows = jnp.einsum(
            "gpt,gtk->gpk", hot, normed.reshape(groups, GROUP * tokens, width), preferred_element_type=jnp.float32
        ).astype(jnp.bfloat16)
        rows = rows.reshape(groups, columns, GROUP * CAP, width).transpose(1, 0, 2, 3).reshape(columns, members, width)
        partial = jnp.einsum("cvk,cpk->cvp", head_here, rows, preferred_element_type=jnp.float32)
        partial = jnp.pad(partial, ((0, 0), (0, VP - VB), (0, 0)))
        packed = pack(partial).astype(jnp.float16)

    packed = packed.reshape((cores, chips) + packed.shape[1:])
    halves = exchange(packed, "core")
    halves = jnp.sum(halves.astype(jnp.float32), axis=0).astype(jnp.float16)
    parts = exchange(halves, "y")
    scores = unpack(jnp.sum(parts.astype(jnp.float32), axis=0))[:VB] / sharpness_divisor

    with jax.named_scope("softmax"):
        mine = lax.dynamic_index_in_dim(told_lists, number, 1, keepdims=False).reshape(members)
        offset = mine % 512 - 1
        peak = jnp.max(scores, axis=0)
        total = jnp.sum(jnp.exp(scores - peak[None, :]), axis=0)
        entry_id = lax.broadcasted_iota(jnp.int32, scores.shape, 0)
        picked = jnp.sum(jnp.where(entry_id == offset[None, :], scores, 0.0), axis=0)
    answer = jnp.stack([peak, total, picked]).reshape(3, shards, CAP).transpose(1, 0, 2)
    answer = exchange(answer.reshape(shards, 3 * CAP), SEQ).reshape(shards, 3, CAP).transpose(1, 0, 2)
    peak, total, picked = answer.reshape(3, members)
    with jax.named_scope("combine"):
        sent = lax.dynamic_index_in_dim(lists, number, 1, keepdims=False).reshape(members)
        token = jnp.where(sent > 0, sent // 512 - 1, -1)
        member = token[:, None] == jnp.arange(tokens, dtype=jnp.int32)[None, :]
        local_peak = jnp.max(jnp.where(member, peak[:, None], floor_value), axis=0)
        scaled = jnp.exp(jnp.where(member, peak[:, None] - local_peak[None, :], floor_value))
        local_total = jnp.sum(scaled * total[:, None], axis=0)
        local_pick = jnp.sum(jnp.where(member, picked[:, None], 0.0), axis=0)
        local = jnp.stack([local_peak, local_total, local_pick])
    every = lax.all_gather(local, TEN, axis=0)
    top = jnp.max(every[:, 0], axis=0)
    summed = jnp.sum(every[:, 1] * jnp.exp(every[:, 0] - top[None, :]), axis=0)
    chosen = jnp.sum(every[:, 2], axis=0)
    return chosen - top - jnp.log(summed)


def solution(mesh):
    fine = Mesh(mesh.devices.reshape(4, 8, 8, 2), ("x", "z", "y", "core"))
    seq, tensor = ("x", "z"), ("y", "core")
    return jax.shard_map(
        per_device,
        mesh=fine,
        in_specs=(
            P(seq, tensor),
            P(seq, tensor),
            P(),
            P(seq + tensor, None),
            P(seq),
            P(seq),
            P(seq, None),
            P(seq),
        ),
        out_specs=P(seq),
        check_vma=False,
    )
```

time: 783 us -> 315 us (0.40)
  local copies, waits for them, and re-layouts: 391 us -> 60.5 us
  waiting for transfers between devices: 223 us -> 110 us
  blocking collectives: 84.7 us -> 63.2 us
  starting transfers between devices: 48.5 us -> 34.5 us
  matrix products: 9.59 us -> 20.4 us
    gather x16 -> x0, local copies, waits for them, and re-layouts: 341 us -> none  [the longest x13 299 us: per_device(): first = jnp.searchsorted(ordered, ordered, side='left')]
    all_to_all x6 -> x4, waiting for transfers between devices: 223 us -> 77.9 us  [exchange(): return lax.all_to_all(value, axis, split_axis=0, concat_axis=0, tiled=True)]
    reshape x6 -> x11, local copies, waits for them, and re-layouts: 10.3 us -> 46.4 us  [the longest x2 25.4 us: per_device(): units = everyone.reshape(shards * 2 * slots, IMG * width)]
    pmax x1 -> x0, blocking collectives: 36 us -> none  [per_device(): top = lax.pmax(local_peak, 'tensor')]
    all_gather x1, waiting for transfers between devices: 0.02 us -> 32 us  [per_device(): everyone = lax.all_gather(both, SEQ, axis=0, tiled=True)]
    scatter x2 -> x0, local copies, waits for them, and re-layouts: 31 us -> none  [the longest x1 15.5 us: per_device(): rank = jnp.zeros((pairs,), jnp.int32).at[order].set(counting - first)]
    all_gather x0 -> x1, blocking collectives: none -> 27.6 us  [per_device(): every = lax.all_gather(local, TEN, axis=0)]
    psum x2 -> x1, blocking collectives: 48.7 us -> 29.6 us  [per_device(): squares = lax.psum(squares, TEN)]
  transfers between devices with their start and end apart: 7 -> 5, of which waited for: 5 -> 4; matrix products, arithmetic and copies ran while one was open for 50% -> 23% of each run, Pallas kernels for 0% -> 0%
where the time goes in v1:
time: 315 us; the launch traced here: 313 us
  waiting for transfers between devices  110 us (35%)
  blocking collectives  63.2 us (20%)
  local copies, waits for them, and re-layouts  60.5 us (19%)
  starting transfers between devices  34.5 us (11%)
  matrix products  20.4 us (6%)
  between operations  13.8 us (4%)
  other arithmetic  10.9 us (3%)
    all_to_all x4, waiting for transfers between devices, exchange(): return lax.all_to_all(value, axis, split_axis=0, concat_axis=0, tiled=True)  77.9 us
    all_to_all x4, starting transfers between devices, exchange(): return lax.all_to_all(value, axis, split_axis=0, concat_axis=0, tiled=True)  34.5 us
    all_gather x1, waiting for transfers between devices, per_device(): everyone = lax.all_gather(both, SEQ, axis=0, tiled=True)  32 us
    psum x1, blocking collectives, per_device(): squares = lax.psum(squares, TEN)  29.6 us
    all_gather x1, blocking collectives, per_device(): every = lax.all_gather(local, TEN, axis=0)  27.6 us
    reshape x2, local copies, waits for them, and re-layouts, per_device(): units = everyone.reshape(shards * 2 * slots, IMG * width)  25.4 us
    reshape x2, local copies, waits for them, and re-layouts, per_device(): head.reshape(VB, chips, cores, width).transpose(2, 1, 0, 3)  19.7 us
    dot_general x1, matrix products, per_device(): jnp.dot(pick.astype(jnp.bfloat16), units, preferred_element_type=jnp.floa...  9.33 us
  transfers between devices with their start and end apart: 5, of which 4 were waited for; matrix products, arithmetic and copies ran while one was open for 23% of the time, Pallas kernels for 0%

profile of v1, /device:TPU:1, one launch (start us, length us, event | category | flops | bytes accessed | tf_op | source)
XLA Modules:
  0.0 313.1 jit_solution(14797176754203129599)
XLA Ops:
  12.1 1.1 fusion.1
  14.3 1.1 multiply_reduce_fusion
  15.4 29.6 %psum.7 = f32[256]{0:T(256)S(1)} all-reduce(f32[256]{0:T(256)S(1)} %multiply_reduce_fusion), channel_id=1, replica_groups=mesh['x'=4,'z'=8,'y'=8,'core'=2] {'core','y'}, use_global_device_ids=true, to_apply=%region_4.5 | all-reduce | flops 256 | bytes 2048 | tf_op jit(solution)/shard_map/psum | solution.py:72
  45.8 13.2 %all-to-all-start = ((f32[32,1,418]{2,1,0:T(1,128)}), f32[32,1,418]{2,1,0:T(1,128)S(1)}, u32[]{:S(2)}, u32[]{:S(2)}) async-start(f32[32,1,418]{2,1,0:T(1,128)} %all_to_all.23), calls=%async_computation | async-start | bytes 131072 | tf_op jit(solution)/shard_map/all_to_all | solution.py:23
  59.0 12.0 %reshape.255 = bf16[297,8,2,512]{3,2,1,0:T(2,128)(2,1)} reshape(bf16[297,8192]{1,0:T(8,128)(2,1)} %param.11) | data formatting | bytes 9732096 | tf_op jit(solution)/shard_map/reshape | solution.py:51
  71.0 7.8 %copy.107 = bf16[297,8,2,512]{3,0,1,2:T(8,128)(2,1)} copy(bf16[297,8,2,512]{3,2,1,0:T(2,128)(2,1)} %reshape.255) | data formatting | bytes 9732096 | tf_op jit(solution)/shard_map/reshape | solution.py:51
  78.7 6.7 %all-to-all-start.1 = ((bf16[16,297,512]{2,1,0:T(8,128)(2,1)}), bf16[16,297,512]{2,1,0:T(8,128)(2,1)}, u32[]{:S(2)}, u32[]{:S(2)}) async-start(bf16[16,297,512]{2,1,0:T(8,128)(2,1)} %bitcast.61), calls=%async_computation.1 | async-start | bytes 9961472 | tf_op jit(solution)/shard_map/all_to_all | solution.py:23
  88.2 32.0 %all-gather.4.cloned.1.call-done = bf16[8192,512]{1,0:T(8,128)(2,1)} async-done(((bf16[256,512]{1,0:T(8,128)(2,1)}), bf16[8192,512]{1,0:T(8,128)(2,1)}) %all-gather.4.cloned.1.call-update) | async-done | bytes 8388624 | tf_op jit(solution)/shard_map/all_gather | solution.py:55
  120.2 13.5 %reshape.251 = bf16[128,32768]{1,0:T(8,128)(2,1)} reshape(bf16[8192,512]{1,0:T(8,128)(2,1)} %all-gather.4.cloned.1.call-done) | data formatting | bytes 16777216 | tf_op jit(solution)/shard_map/merge/reshape | solution.py:92
  133.6 11.9 %copy.102 = bf16[128,32768]{0,1:T(8,128)(2,1)} copy(bf16[128,32768]{1,0:T(8,128)(2,1)} %reshape.251) | data formatting | bytes 16777216 | tf_op jit(solution)/shard_map/merge/reshape | solution.py:92
  145.6 9.3 %multiply_convert_fusion = bf16[64,64,512]{2,0,1:T(8,128)(2,1)S(1)} fusion(f32[512]{0:T(512)S(1)} %dynamic_slice.11, f32[64,64]{0,1:T(8,128)S(1)} %copy.104, bf16[64,512,128]{2,1,0:T(8,128)(2,1)} %bitcast.59, s32[64]{0:T(128)S(1)} %eq.138), kind=kOutput, calls=%fused_computation.2 | convolution fusion | flops 543170560 | bytes 12601600 | tf_op jit(solution)/shard_map/merge/dot_general | solution.py:93
  154.9 2.4 copy.105
  157.3 3.5 %fusion.3 = bf16[8,640,512]{2,1,0:T(8,128)(2,1)S(1)} fusion(bf16[8,512,512]{2,1,0:T(8,128)(2,1)S(1)} %bitcast.65, s32[8,640]{1,0:T(8,128)S(1)} %eq.134), kind=kOutput, calls=%fused_computation.10 | convolution fusion | flops 2689597440 | bytes 9457664 | tf_op jit(solution)/shard_map/partial/gpt,gtk->gpk/dot_general | solution.py:106
  160.8 2.9 copy.106
  163.7 32.0 %all-to-all-done.1 = bf16[16,297,512]{2,1,0:T(8,128)(2,1)} async-done(((bf16[16,297,512]{2,1,0:T(8,128)(2,1)}), bf16[16,297,512]{2,1,0:T(8,128)(2,1)}, u32[]{:S(2)}, u32[]{:S(2)}) %all-to-all-start.1) | async-done | bytes 4866080 | tf_op jit(solution)/shard_map/all_to_all | solution.py:23
  195.7 7.4 %convolution_bitcast_fusion = f32[16,297,320]{2,1,0:T(8,128)S(1)} fusion(bf16[16,320,512]{2,1,0:T(8,128)(2,1)} %bitcast.60, bf16[16,297,512]{2,1,0:T(8,128)(2,1)} %all-to-all-done.1), kind=kOutput, calls=%fused_computation.11 | convolution fusion | flops 1557135360 | bytes 16191488 | tf_op jit(solution)/shard_map/partial/cvk,cpk->cvp/dot_general | solution.py:110
  204.8 1.0 pad_maximum_fusion
  205.8 6.1 %all_to_all.36 = f16[2,8,760,128]{3,2,1,0:T(8,128)(2,1)S(1)} all-to-all(f16[2,8,760,128]{3,2,1,0:T(8,128)(2,1)S(1)} %pad_maximum_fusion), channel_id=1, replica_groups=mesh['x'=4,'z'=8,'y'=8,'core'=2] {'core'}, dimensions={0} | all-to-all | bytes 6225920 | tf_op jit(solution)/shard_map/all_to_all | solution.py:23
  212.5 1.4 convert_element_type.58
  213.8 5.3 %all-to-all-start.3 = ((f16[8,760,128]{2,1,0:T(8,128)(2,1)}), f16[8,760,128]{2,1,0:T(8,128)(2,1)S(1)}, u32[]{:S(2)}, u32[]{:S(2)}) async-start(f16[8,760,128]{2,1,0:T(8,128)(2,1)} %convert_element_type.58), calls=%async_computation.3 | async-start | bytes 3112960 | tf_op jit(solution)/shard_map/all_to_all | solution.py:23
  219.9 37.2 %all-to-all-done.3 = f16[8,760,128]{2,1,0:T(8,128)(2,1)S(1)} async-done(((f16[8,760,128]{2,1,0:T(8,128)(2,1)}), f16[8,760,128]{2,1,0:T(8,128)(2,1)S(1)}, u32[]{:S(2)}, u32[]{:S(2)}) %all-to-all-start.3) | async-done | bytes 1556512 | tf_op jit(solution)/shard_map/all_to_all | solution.py:23
  259.0 9.4 %all-to-all-start.4 = ((f32[32,1,30]{2,1,0:T(1,128)}), f32[32,1,30]{2,1,0:T(1,128)S(1)}, u32[]{:S(2)}, u32[]{:S(2)}) async-start(f32[32,1,30]{2,1,0:T(1,128)} %copy.114), calls=%async_computation.4 | async-start | bytes 32768 | tf_op jit(solution)/shard_map/all_to_all | solution.py:23
  268.4 8.6 %all-to-all-done.4 = f32[32,1,30]{2,1,0:T(1,128)S(1)} async-done(((f32[32,1,30]{2,1,0:T(1,128)}), f32[32,1,30]{2,1,0:T(1,128)S(1)}, u32[]{:S(2)}, u32[]{:S(2)}) %all-to-all-start.4) | async-done | bytes 3872 | tf_op jit(solution)/shard_map/all_to_all | solution.py:23
  278.1 27.6 %all-gather.1 = f32[16,3,128]{2,1,0:T(4,128)S(1)} all-gather(f32[1,3,128]{2,1,0:T(4,128)S(1)} %maximum_bitcast_fusion.1), channel_id=2, replica_groups=mesh['x'=4,'z'=8,'y'=8,'core'=2] {'core','y'}, dimensions={0}, use_global_device_ids=true | all-gather | bytes 26112 | tf_op jit(solution)/shard_map/all_gather | solution.py:139
  (88 shorter events, 16.7 us)
Async XLA Ops:
  6.5 113.6 %all-gather.4.cloned.1.call-start = ((), (), s32[]{:S(2)}) async-start(), calls=%async_computation.5 | async-start | bytes 8650752 | tf_op jit(solution)/shard_map/all_gather | solution.py:55
  8.4 0.7 copy-start
  45.8 32.9 %all-to-all-start = ((f32[32,1,418]{2,1,0:T(1,128)}), f32[32,1,418]{2,1,0:T(1,128)S(1)}, u32[]{:S(2)}, u32[]{:S(2)}) async-start(f32[32,1,418]{2,1,0:T(1,128)} %all_to_all.23), calls=%async_computation | async-start | bytes 131072 | tf_op jit(solution)/shard_map/all_to_all | solution.py:23
  78.7 117.0 %all-to-all-start.1 = ((bf16[16,297,512]{2,1,0:T(8,128)(2,1)}), bf16[16,297,512]{2,1,0:T(8,128)(2,1)}, u32[]{:S(2)}, u32[]{:S(2)}) async-start(bf16[16,297,512]{2,1,0:T(8,128)(2,1)} %bitcast.61), calls=%async_computation.1 | async-start | bytes 9961472 | tf_op jit(solution)/shard_map/all_to_all | solution.py:23
  213.8 43.2 %all-to-all-start.3 = ((f16[8,760,128]{2,1,0:T(8,128)(2,1)}), f16[8,760,128]{2,1,0:T(8,128)(2,1)S(1)}, u32[]{:S(2)}, u32[]{:S(2)}) async-start(f16[8,760,128]{2,1,0:T(8,128)(2,1)} %convert_element_type.58), calls=%async_computation.3 | async-start | bytes 3112960 | tf_op jit(solution)/shard_map/all_to_all | solution.py:23
  259.0 18.0 %all-to-all-start.4 = ((f32[32,1,30]{2,1,0:T(1,128)}), f32[32,1,30]{2,1,0:T(1,128)S(1)}, u32[]{:S(2)}, u32[]{:S(2)}) async-start(f32[32,1,30]{2,1,0:T(1,128)} %copy.114), calls=%async_computation.4 | async-start | bytes 32768 | tf_op jit(solution)/shard_map/all_to_all | solution.py:23
Sparse Core Ops, SparseCore 0:
  10.5 109.5 all-gather.3

commit v2 on v1

--- a/solution.py
+++ b/solution.py
@@ -1,6 +1,8 @@
 import jax
 import jax.numpy as jnp
 from jax import lax
+from jax.experimental import pallas as pl
+from jax.experimental.pallas import tpu as pltpu
 from jax.sharding import Mesh
 from jax.sharding import PartitionSpec as P
 
@@ -9,7 +11,9 @@
 VP = 304
 IMG = 64
 CAP = 10
-GROUP = 4
+GROUP = 8
+TALL = 760
+VMEM = 48 * 2**20
 
 sharpness_divisor = 0.7
 epsilon = 1e-06
@@ -23,10 +27,95 @@
     return lax.all_to_all(value, axis, split_axis=0, concat_axis=0, tiled=True)
 
 
-def pack(scores):
-    tail = scores[..., 256:]
-    tail = jnp.concatenate([tail[..., : VP // 2, :], tail[..., VP // 2 :, :]], axis=-1)
-    return jnp.concatenate([scores[..., :128], scores[..., 128:256], tail], axis=-2)
+def share(value, axis):
+    return exchange(jnp.broadcast_to(value[None], (lax.axis_size(axis),) + value.shape), axis)
+
+
+def split_kernel(head_ref, out_ref):
+    rows = lax.broadcasted_iota(jnp.int32, out_ref.shape[1:], 0)
+    out_ref[0] = jnp.where(rows < VB, head_ref[...].astype(jnp.float32), 0.0).astype(jnp.bfloat16)
+
+
+def split_head(head, chips, cores):
+    width = head.shape[1] // (chips * cores)
+    return pl.pallas_call(
+        split_kernel,
+        grid=(chips * cores,),
+        in_specs=[pl.BlockSpec((VP, width), lambda i: (0, i % chips * cores + i // chips))],
+        out_specs=pl.BlockSpec((1, VP, width), lambda i: (i, 0, 0)),
+        out_shape=jax.ShapeDtypeStruct((chips * cores, VP, width), jnp.bfloat16),
+        compiler_params=pltpu.CompilerParams(vmem_limit_bytes=VMEM),
+        name="split_head",
+    )(head)
+
+
+def rows_kernel(unit_ref, *refs):
+    del unit_ref
+    *pieces, scale_ref, gain_ref, token_ref, out_ref, normed_ref = refs
+    for i, piece in enumerate(pieces):
+        here = pl.ds(i * IMG, IMG)
+        values = piece[...].astype(jnp.float32)
+        normed_ref[here, :] = (values * scale_ref[here, :] * gain_ref[...]).astype(jnp.bfloat16)
+    token = token_ref[0]
+    shape = (token.shape[0], normed_ref.shape[0])
+    hot = (token == lax.broadcasted_iota(jnp.int32, shape, 1)).astype(jnp.float32).astype(jnp.bfloat16)
+    rows = jnp.dot(hot, normed_ref[...], preferred_element_type=jnp.float32)
+    out_ref[...] = rows.astype(jnp.bfloat16).reshape(out_ref.shape)
+
+
+def pick_rows(unit, everyone, scale, gain, token_of, columns):
+    groups, pairs, _ = token_of.shape
+    width = everyone.shape[1]
+    units = unit.shape[0] // groups
+    piece = [
+        pl.BlockSpec((IMG, width), lambda g, unit_ref, i=i: (unit_ref[g * units + i], 0)) for i in range(units)
+    ]
+    return pl.pallas_call(
+        rows_kernel,
+        grid_spec=pltpu.PrefetchScalarGridSpec(
+            num_scalar_prefetch=1,
+            grid=(groups,),
+            in_specs=piece
+            + [
+                pl.BlockSpec((units * IMG, 1), lambda g, unit_ref: (g, 0)),
+                pl.BlockSpec((1, width), lambda g, unit_ref: (0, 0)),
+                pl.BlockSpec((1, pairs, 1), lambda g, unit_ref: (g, 0, 0)),
+            ],
+            out_specs=pl.BlockSpec((columns, pairs // columns, width), lambda g, unit_ref: (0, g, 0)),
+            scratch_shapes=[pltpu.VMEM((units * IMG, width), jnp.bfloat16)],
+        ),
+        out_shape=jax.ShapeDtypeStruct((columns, groups * pairs // columns, width), jnp.bfloat16),
+        compiler_params=pltpu.CompilerParams(vmem_limit_bytes=VMEM),
+        cost_estimate=pl.CostEstimate(flops=1000, bytes_accessed=1000, transcendentals=0),
+        name="pick_rows",
+    )(unit, *([everyone] * units), scale, gain, token_of)
+
+
+def partial_kernel(head_ref, rows_ref, out_ref):
+    scores = lax.dot_general(
+        head_ref[0], rows_ref[0], (((1,), (1,)), ((), ())), preferred_element_type=jnp.float32
+    )
+    half = VP // 2
+    tail = jnp.concatenate([scores[:half, 256:320], scores[half:, 256:320]], axis=1)
+    out_ref[0, :VP, :] = scores[:, :128].astype(out_ref.dtype)
+    out_ref[0, VP : 2 * VP, :] = scores[:, 128:256].astype(out_ref.dtype)
+    out_ref[0, 2 * VP :, :] = tail.astype(out_ref.dtype)
+
+
+def partial_scores(head, rows):
+    columns, _, width = head.shape
+    return pl.pallas_call(
+        partial_kernel,
+        grid=(columns,),
+        in_specs=[
+            pl.BlockSpec((1, VP, width), lambda i: (i, 0, 0)),
+            pl.BlockSpec((1, rows.shape[1], width), lambda i: (i, 0, 0)),
+        ],
+        out_specs=pl.BlockSpec((1, TALL, 128), lambda i: (i, 0, 0)),
+        out_shape=jax.ShapeDtypeStruct((columns, TALL, 128), jnp.float32),
+        compiler_params=pltpu.CompilerParams(vmem_limit_bytes=VMEM),
+        name="partial_scores",
+    )(head, rows)
 
 
 def unpack(packed):
@@ -48,9 +137,7 @@
     blocks = shards * columns
     members = shards * CAP
 
-    pieces = head.reshape(VB, chips, cores, width).transpose(2, 1, 0, 3).reshape(columns, VB, width)
-    head_here = exchange(pieces, TEN)
-
+    pieces = split_head(head, chips, cores)
     both = jnp.concatenate([text, patches], axis=0)
     everyone = lax.all_gather(both, SEQ, axis=0, tiled=True)
 
@@ -69,7 +156,6 @@
         lists = lists.reshape(CAP, shards, chips, cores).transpose(1, 3, 2, 0).reshape(shards, columns, CAP)
 
     squares = jnp.sum(jnp.square(both.astype(jnp.float32)), axis=1)
-    squares = lax.psum(squares, TEN)
     firsts = image_rows.reshape(slots, IMG)[:, 0].astype(jnp.float32)
     common = jnp.concatenate([squares, firsts])
     message = jnp.concatenate(
@@ -80,6 +166,8 @@
         axis=1,
     )
     told = exchange(message, SEQ)
+    told, pieces = lax.optimization_barrier((told, pieces))
+    head_here = exchange(pieces, TEN)
     told_lists = told[:, : columns * CAP].astype(jnp.int32).reshape(shards, columns, CAP)
     told_squares = told[:, columns * CAP : columns * CAP + 2 * tokens]
     told_firsts = told[:, columns * CAP + 2 * tokens :].astype(jnp.int32)
@@ -89,31 +177,24 @@
         patch_unit = (told_firsts // tokens) * (2 * slots) + slots + (told_firsts % tokens) // IMG
         unit = jnp.where(told_firsts >= 0, patch_unit, own_unit).reshape(-1)
         pick = unit[:, None] == jnp.arange(shards * 2 * slots, dtype=jnp.int32)[None, :]
-        units = everyone.reshape(shards * 2 * slots, IMG * width)
-        merged = jnp.dot(pick.astype(jnp.bfloat16), units, preferred_element_type=jnp.float32)
         unit_squares = told_squares.reshape(1, shards * 2 * slots, IMG)
         row_squares = jnp.sum(jnp.where(pick[:, :, None], unit_squares, 0.0), axis=1)
+        row_squares = lax.psum(row_squares, TEN)
         scale = lax.rsqrt(row_squares / D + epsilon)
         gain = lax.dynamic_slice_in_dim(norm_gain, place * width, width, 0)
-        normed = (merged.reshape(shards * slots, IMG, width) * scale[:, :, None] * gain).astype(jnp.bfloat16)
 
     with jax.named_scope("partial"):
         groups = shards // GROUP
         token_of = told_lists // 512 - 1 + (jnp.arange(shards, dtype=jnp.int32) % GROUP * tokens)[:, None, None]
         token_of = jnp.where(told_lists > 0, token_of, -1)
-        token_of = token_of.reshape(groups, GROUP, columns, CAP).transpose(0, 2, 1, 3).reshape(groups, columns * GROUP * CAP)
-        hot = (token_of[:, :, None] == jnp.arange(GROUP * tokens, dtype=jnp.int32)).astype(jnp.bfloat16)
-        rows = jnp.einsum(
-            "gpt,gtk->gpk", hot, normed.reshape(groups, GROUP * tokens, width), preferred_element_type=jnp.float32
-        ).astype(jnp.bfloat16)
-        rows = rows.reshape(groups, columns, GROUP * CAP, width).transpose(1, 0, 2, 3).reshape(columns, members, width)
-        partial = jnp.einsum("cvk,cpk->cvp", head_here, rows, preferred_element_type=jnp.float32)
-        partial = jnp.pad(partial, ((0, 0), (0, VP - VB), (0, 0)))
-        packed = pack(partial).astype(jnp.float16)
+        token_of = token_of.reshape(groups, GROUP, columns, CAP).transpose(0, 2, 1, 3)
+        token_of = token_of.reshape(groups, columns * GROUP * CAP, 1)
+        rows = pick_rows(unit, everyone, scale.reshape(-1, 1), gain[None, :], token_of, columns)
+        packed = partial_scores(head_here, rows)
 
     packed = packed.reshape((cores, chips) + packed.shape[1:])
     halves = exchange(packed, "core")
-    halves = jnp.sum(halves.astype(jnp.float32), axis=0).astype(jnp.float16)
+    halves = jnp.sum(halves, axis=0).astype(jnp.float16)
     parts = exchange(halves, "y")
     scores = unpack(jnp.sum(parts.astype(jnp.float32), axis=0))[:VB] / sharpness_divisor
 
@@ -136,7 +217,7 @@
         local_total = jnp.sum(scaled * total[:, None], axis=0)
         local_pick = jnp.sum(jnp.where(member, picked[:, None], 0.0), axis=0)
         local = jnp.stack([local_peak, local_total, local_pick])
-    every = lax.all_gather(local, TEN, axis=0)
+    every = share(local, TEN)
     top = jnp.max(every[:, 0], axis=0)
     summed = jnp.sum(every[:, 1] * jnp.exp(every[:, 0] - top[None, :]), axis=0)
     chosen = jnp.sum(every[:, 2], axis=0)

time: 315 us -> 344 us (1.092)
  blocking collectives: 63.2 us -> 184 us
  waiting for transfers between devices: 110 us -> 45.9 us
  local copies, waits for them, and re-layouts: 60.5 us -> 17.3 us
  Pallas kernels: 0 us -> 33.2 us
  matrix products: 20.4 us -> 0.19 us
    psum x1, blocking collectives: 29.6 us -> 156 us  [per_device(): row_squares = lax.psum(row_squares, TEN)]
    reshape x4 -> x3, local copies, waits for them, and re-layouts: 45.1 us -> 4.26 us  [the longest x1 3.48 us: per_device(): scale.reshape(-1, 1)]
    pallas_call x0 -> x3, Pallas kernels: none -> 33.2 us  [the longest x1 14.2 us: partial_scores(): pl.pallas_call(partial_kernel, grid=(columns,), in_specs=[pl.BlockSpec((1...]
    all_to_all x4, waiting for transfers between devices: 77.9 us -> 45.8 us  [exchange(): return lax.all_to_all(value, axis, split_axis=0, concat_axis=0, tiled=True)]
    all_gather x1, waiting for transfers between devices: 32 us -> 0.02 us  [per_device(): everyone = lax.all_gather(both, SEQ, axis=0, tiled=True)]
    all_gather x1 -> x0, blocking collectives: 27.6 us -> none  [per_device(): every = lax.all_gather(local, TEN, axis=0)]
    all_to_all x1 -> x2, blocking collectives: 6.07 us -> 28.1 us  [exchange(): return lax.all_to_all(value, axis, split_axis=0, concat_axis=0, tiled=True)]
    dot_general x3 -> x0, matrix products: 20.2 us -> none  [the longest x1 9.33 us: per_device(): jnp.dot(pick.astype(jnp.bfloat16), units, preferred_element_type=jnp.floa...]
  transfers between devices with their start and end apart: 5 -> 5, of which waited for: 4 -> 2; matrix products, arithmetic and copies ran while one was open for 23% -> 4% of each run, Pallas kernels for 0% -> 6%
where the time goes in v2:
time: 344 us; the launch traced here: 343 us
  blocking collectives  184 us (53%)
  waiting for transfers between devices  45.9 us (13%)
  starting transfers between devices  37.8 us (11%)
  Pallas kernels  33.2 us (10%)
  local copies, waits for them, and re-layouts  17.3 us (5%)
  between operations  13.7 us (4%)
  other arithmetic  10.7 us (3%)
    psum x1, blocking collectives, per_device(): row_squares = lax.psum(row_squares, TEN)  156 us
    all_to_all x4, waiting for transfers between devices, exchange(): return lax.all_to_all(value, axis, split_axis=0, concat_axis=0, tiled=True)  45.8 us
    all_to_all x4, starting transfers between devices, exchange(): return lax.all_to_all(value, axis, split_axis=0, concat_axis=0, tiled=True)  37.8 us
    all_to_all x2, blocking collectives, exchange(): return lax.all_to_all(value, axis, split_axis=0, concat_axis=0, tiled=True)  28.1 us
    pallas_call x1, Pallas kernels, partial_scores(): pl.pallas_call(partial_kernel, grid=(columns,), in_specs=[pl.BlockSpec((1...  14.2 us
    pallas_call x1, Pallas kernels, pick_rows(): pl.pallas_call(rows_kernel, grid_spec=pltpu.PrefetchScalarGridSpec(num_sc...  10.7 us
    pallas_call x1, Pallas kernels, split_head(): pl.pallas_call(split_kernel, grid=(chips * cores,), in_specs=[pl.BlockSpe...  8.37 us
  transfers between devices with their start and end apart: 5, of which 2 were waited for; matrix products, arithmetic and copies ran while one was open for 4% of the time, Pallas kernels for 6%

profile of v2, /device:TPU:1, one launch (start us, length us, event | category | flops | bytes accessed | tf_op | source)
XLA Modules:
  0.0 342.8 jit_solution(4055650319210549085)
XLA Ops:
  6.5 0.9 constant_dynamic-update-slice_fusion.1
  7.5 0.9 constant_dynamic-update-slice_fusion
  9.1 0.8 reshape.227
  9.9 0.8 copy.109
  11.4 0.7 select_reduce_fusion.5
  12.1 1.1 fusion
  15.4 13.7 %all-to-all-start = ((f32[32,1,418]{2,1,0:T(1,128)}), f32[32,1,418]{2,1,0:T(1,128)S(1)}, u32[]{:S(2)}, u32[]{:S(2)}) async-start(f32[32,1,418]{2,1,0:T(1,128)} %all_to_all.26), calls=%async_computation | async-start | bytes 131072 | tf_op jit(solution)/shard_map/all_to_all | solution.py:27
  29.1 8.4 %split_head.1 = bf16[16,304,512]{2,1,0:T(8,128)(2,1)S(1)} custom-call(bf16[297,8192]{1,0:T(8,128)(2,1)} %head_ref.1), custom_call_target="tpu_custom_call" | custom-call | tf_op jit(solution)/shard_map/split_head/pallas_call | solution.py:41
  37.5 2.2 copy-done
  39.7 8.1 %all-to-all-start.1 = ((bf16[16,304,512]{2,1,0:T(8,128)(2,1)}), bf16[16,304,512]{2,1,0:T(8,128)(2,1)}, u32[]{:S(2)}, u32[]{:S(2)}) async-start(bf16[16,304,512]{2,1,0:T(8,128)(2,1)} %copy-done), calls=%async_computation.1 | async-start | bytes 9961472 | tf_op jit(solution)/shard_map/all_to_all | solution.py:27
  47.8 0.8 dynamic_slice.11
  50.2 155.8 %psum.7 = f32[64,64]{1,0:T(8,128)S(1)} all-reduce(f32[64,64]{1,0:T(8,128)S(1)} %select_reduce_fusion.1), channel_id=1, replica_groups=mesh['x'=4,'z'=8,'y'=8,'core'=2] {'core','y'}, use_global_device_ids=true, to_apply=%region_5.6 | all-reduce | flops 4096 | bytes 32768 | tf_op jit(solution)/shard_map/merge/psum | solution.py:182
  206.1 3.5 %reshape.236.refs_16_ = f32[4096,1]{1,0:T(8,128)} reshape(f32[64,64]{1,0:T(8,128)S(1)} %add_rsqrt_fusion) | data formatting | bytes 32768 | tf_op jit(solution)/shard_map/partial/reshape | solution.py:192
  210.3 1.6 copy-done.1
  211.9 10.7 %pick_rows.1.rows_ref = bf16[16,320,512]{2,1,0:T(8,128)(2,1)} custom-call(s32[64]{0:T(128)S(1)} %reshape.228.unit_ref, bf16[8192,512]{1,0:T(8,128)(2,1)} %all-gather.2.cloned.1.call-done.refs_0_.refs_1_.refs_2_.refs_3_.refs_4_.refs_5_.refs_6_.refs_7_.refs_8_.refs_9_.refs_10_.refs_11_.refs_12_.refs_13_.refs_14_.refs_15_, ...), custom_call_target="tpu_custom_call" | custom-call | flops 1000 | bytes 1000 | tf_op jit(solution)/shard_map/partial/pick_rows/pallas_call | solution.py:73
  222.5 14.2 %partial_scores.1 = f32[16,760,128]{2,1,0:T(8,128)} custom-call(bf16[16,304,512]{2,1,0:T(8,128)(2,1)} %all-to-all-done.1.head_ref, bf16[16,320,512]{2,1,0:T(8,128)(2,1)} %pick_rows.1.rows_ref), custom_call_target="tpu_custom_call" | custom-call | tf_op jit(solution)/shard_map/partial/partial_scores/pallas_call | solution.py:107
  236.7 14.6 %all_to_all.41 = f32[2,8,760,128]{3,2,1,0:T(8,128)} all-to-all(f32[2,8,760,128]{3,2,1,0:T(8,128)} %bitcast.40), channel_id=1, replica_groups=mesh['x'=4,'z'=8,'y'=8,'core'=2] {'core'}, dimensions={0} | all-to-all | bytes 12451840 | tf_op jit(solution)/shard_map/all_to_all | solution.py:27
  251.3 3.5 %reduce_sum.112 = f32[8,760,128]{2,1,0:T(8,128)S(1)} reduce(f32[2,8,760,128]{3,2,1,0:T(8,128)} %all_to_all.41, f32[]{:T(128)} %constant.144.clone.1), dimensions={0}, to_apply=%region_6.7 | reduce | flops 778240 | bytes 9338884 | tf_op jit(solution)/shard_map/reduce_sum | solution.py:197
  254.9 1.4 convert_element_type.40
  256.2 6.5 %all-to-all-start.3 = ((f16[8,760,128]{2,1,0:T(8,128)(2,1)}), f16[8,760,128]{2,1,0:T(8,128)(2,1)S(1)}, u32[]{:S(2)}, u32[]{:S(2)}) async-start(f16[8,760,128]{2,1,0:T(8,128)(2,1)} %convert_element_type.40), calls=%async_computation.3 | async-start | bytes 3112960 | tf_op jit(solution)/shard_map/all_to_all | solution.py:27
  263.5 37.2 %all-to-all-done.3 = f16[8,760,128]{2,1,0:T(8,128)(2,1)S(1)} async-done(((f16[8,760,128]{2,1,0:T(8,128)(2,1)}), f16[8,760,128]{2,1,0:T(8,128)(2,1)S(1)}, u32[]{:S(2)}, u32[]{:S(2)}) %all-to-all-start.3) | async-done | bytes 1556512 | tf_op jit(solution)/shard_map/all_to_all | solution.py:27
  302.6 9.4 %all-to-all-start.4 = ((f32[32,1,30]{2,1,0:T(1,128)}), f32[32,1,30]{2,1,0:T(1,128)S(1)}, u32[]{:S(2)}, u32[]{:S(2)}) async-start(f32[32,1,30]{2,1,0:T(1,128)} %copy.126), calls=%async_computation.4 | async-start | bytes 32768 | tf_op jit(solution)/shard_map/all_to_all | solution.py:27
  312.1 8.6 %all-to-all-done.4 = f32[32,1,30]{2,1,0:T(1,128)S(1)} async-done(((f32[32,1,30]{2,1,0:T(1,128)}), f32[32,1,30]{2,1,0:T(1,128)S(1)}, u32[]{:S(2)}, u32[]{:S(2)}) %all-to-all-start.4) | async-done | bytes 3872 | tf_op jit(solution)/shard_map/all_to_all | solution.py:27
  321.8 13.5 %all_to_all.42 = f32[16,3,128]{2,1,0:T(4,128)S(1)} all-to-all(f32[16,3,128]{2,1,0:T(4,128)S(1)} %broadcast_in_dim.146), channel_id=1, replica_groups=mesh['x'=4,'z'=8,'y'=8,'core'=2] {'core','y'}, dimensions={0} | all-to-all | bytes 49152 | tf_op jit(solution)/shard_map/all_to_all | solution.py:27
  (86 shorter events, 10.0 us)
Async XLA Ops:
  6.5 203.7 %all-gather.2.cloned.1.call-start = ((), (), s32[]{:S(2)}) async-start(), calls=%async_computation.6 | async-start | bytes 8650752 | tf_op jit(solution)/shard_map/all_gather | solution.py:142
  8.4 0.7 copy-start.2
  9.1 5.3 %copy-start.3 = (bf16[256,512]{1,0:T(8,128)(2,1)S(1)}, bf16[256,512]{1,0:T(8,128)(2,1)}, u32[]{:S(2)}) copy-start(bf16[256,512]{1,0:T(8,128)(2,1)} %copy-done.2) | copy-start | bytes 786436
  15.4 24.3 %all-to-all-start = ((f32[32,1,418]{2,1,0:T(1,128)}), f32[32,1,418]{2,1,0:T(1,128)S(1)}, u32[]{:S(2)}, u32[]{:S(2)}) async-start(f32[32,1,418]{2,1,0:T(1,128)} %all_to_all.26), calls=%async_computation | async-start | bytes 131072 | tf_op jit(solution)/shard_map/all_to_all | solution.py:27
  37.5 2.2 copy-start
  39.7 182.8 %all-to-all-start.1 = ((bf16[16,304,512]{2,1,0:T(8,128)(2,1)}), bf16[16,304,512]{2,1,0:T(8,128)(2,1)}, u32[]{:S(2)}, u32[]{:S(2)}) async-start(bf16[16,304,512]{2,1,0:T(8,128)(2,1)} %copy-done), calls=%async_computation.1 | async-start | bytes 9961472 | tf_op jit(solution)/shard_map/all_to_all | solution.py:27
  210.3 1.6 copy-start.1
  256.2 44.5 %all-to-all-start.3 = ((f16[8,760,128]{2,1,0:T(8,128)(2,1)}), f16[8,760,128]{2,1,0:T(8,128)(2,1)S(1)}, u32[]{:S(2)}, u32[]{:S(2)}) async-start(f16[8,760,128]{2,1,0:T(8,128)(2,1)} %convert_element_type.40), calls=%async_computation.3 | async-start | bytes 3112960 | tf_op jit(solution)/shard_map/all_to_all | solution.py:27
  302.6 18.1 %all-to-all-start.4 = ((f32[32,1,30]{2,1,0:T(1,128)}), f32[32,1,30]{2,1,0:T(1,128)S(1)}, u32[]{:S(2)}, u32[]{:S(2)}) async-start(f32[32,1,30]{2,1,0:T(1,128)} %copy.126), calls=%async_computation.4 | async-start | bytes 32768 | tf_op jit(solution)/shard_map/all_to_all | solution.py:27
Sparse Core Ops, SparseCore 0:
  10.5 109.5 all-gather.1

commit v3 on v2

--- a/solution.py
+++ b/solution.py
@@ -13,7 +13,7 @@
 CAP = 10
 GROUP = 8
 TALL = 760
-VMEM = 48 * 2**20
+VMEM = 60 * 2**20
 
 sharpness_divisor = 0.7
 epsilon = 1e-06
@@ -31,19 +31,31 @@
     return exchange(jnp.broadcast_to(value[None], (lax.axis_size(axis),) + value.shape), axis)
 
 
+def by_steps(value, axis):
+    count, me = lax.axis_size(axis), lax.axis_index(axis)
+    twice = jnp.concatenate([value, value], axis=0)
+    turned = lax.dynamic_slice_in_dim(twice, me, count, 0)
+    came = [turned[0]]
+    for step in range(1, count):
+        came.append(lax.ppermute(turned[step], axis, [(i, (i + step) % count) for i in range(count)]))
+    back = jnp.stack(came[::-1])
+    twice = jnp.concatenate([back, back], axis=0)
+    return lax.dynamic_slice_in_dim(twice, count - 1 - me, count, 0)
+
+
 def split_kernel(head_ref, out_ref):
     rows = lax.broadcasted_iota(jnp.int32, out_ref.shape[1:], 0)
     out_ref[0] = jnp.where(rows < VB, head_ref[...].astype(jnp.float32), 0.0).astype(jnp.bfloat16)
 
 
-def split_head(head, chips, cores):
-    width = head.shape[1] // (chips * cores)
+def split_head(head, chips):
+    part = head.shape[1] // chips
     return pl.pallas_call(
         split_kernel,
-        grid=(chips * cores,),
-        in_specs=[pl.BlockSpec((VP, width), lambda i: (0, i % chips * cores + i // chips))],
-        out_specs=pl.BlockSpec((1, VP, width), lambda i: (i, 0, 0)),
-        out_shape=jax.ShapeDtypeStruct((chips * cores, VP, width), jnp.bfloat16),
+        grid=(chips,),
+        in_specs=[pl.BlockSpec((VP, part), lambda i: (0, i))],
+        out_specs=pl.BlockSpec((1, VP, part), lambda i: (i, 0, 0)),
+        out_shape=jax.ShapeDtypeStruct((chips, VP, part), jnp.bfloat16),
         compiler_params=pltpu.CompilerParams(vmem_limit_bytes=VMEM),
         name="split_head",
     )(head)
@@ -51,22 +63,26 @@
 
 def rows_kernel(unit_ref, *refs):
     del unit_ref
-    *pieces, scale_ref, gain_ref, token_ref, out_ref, normed_ref = refs
+    *pieces, scale_ref, gain_ref, token_ref, away_ref, here_ref, normed_ref = refs
     for i, piece in enumerate(pieces):
-        here = pl.ds(i * IMG, IMG)
+        span = pl.ds(i * IMG, IMG)
         values = piece[...].astype(jnp.float32)
-        normed_ref[here, :] = (values * scale_ref[here, :] * gain_ref[...]).astype(jnp.bfloat16)
+        normed_ref[span, :] = (values * scale_ref[span, :] * gain_ref[...]).astype(jnp.bfloat16)
     token = token_ref[0]
-    shape = (token.shape[0], normed_ref.shape[0])
-    hot = (token == lax.broadcasted_iota(jnp.int32, shape, 1)).astype(jnp.float32).astype(jnp.bfloat16)
-    rows = jnp.dot(hot, normed_ref[...], preferred_element_type=jnp.float32)
-    out_ref[...] = rows.astype(jnp.bfloat16).reshape(out_ref.shape)
-
-
-def pick_rows(unit, everyone, scale, gain, token_of, columns):
+    half = token.shape[0] // 2
+    for part, out_ref in enumerate((away_ref, here_ref)):
+        wanted = token[part * half : (part + 1) * half]
+        shape = (half, normed_ref.shape[0])
+        hot = (wanted == lax.broadcasted_iota(jnp.int32, shape, 1)).astype(jnp.float32).astype(jnp.bfloat16)
+        rows = jnp.dot(hot, normed_ref[...], preferred_element_type=jnp.float32)
+        out_ref[...] = rows.astype(jnp.bfloat16).reshape(out_ref.shape)
+
+
+def pick_rows(unit, everyone, scale, gain, token_of, chips):
     groups, pairs, _ = token_of.shape
     width = everyone.shape[1]
     units = unit.shape[0] // groups
+    each = pairs // (2 * chips)
     piece = [
         pl.BlockSpec((IMG, width), lambda g, unit_ref, i=i: (unit_ref[g * units + i], 0)) for i in range(units)
     ]
@@ -81,41 +97,47 @@
                 pl.BlockSpec((1, width), lambda g, unit_ref: (0, 0)),
                 pl.BlockSpec((1, pairs, 1), lambda g, unit_ref: (g, 0, 0)),
             ],
-            out_specs=pl.BlockSpec((columns, pairs // columns, width), lambda g, unit_ref: (0, g, 0)),
+            out_specs=[pl.BlockSpec((chips, each, width), lambda g, unit_ref: (0, g, 0))] * 2,
             scratch_shapes=[pltpu.VMEM((units * IMG, width), jnp.bfloat16)],
         ),
-        out_shape=jax.ShapeDtypeStruct((columns, groups * pairs // columns, width), jnp.bfloat16),
+        out_shape=[jax.ShapeDtypeStruct((chips, groups * each, width), jnp.bfloat16)] * 2,
         compiler_params=pltpu.CompilerParams(vmem_limit_bytes=VMEM),
-        cost_estimate=pl.CostEstimate(flops=1000, bytes_accessed=1000, transcendentals=0),
         name="pick_rows",
     )(unit, *([everyone] * units), scale, gain, token_of)
 
 
-def partial_kernel(head_ref, rows_ref, out_ref):
-    scores = lax.dot_general(
-        head_ref[0], rows_ref[0], (((1,), (1,)), ((), ())), preferred_element_type=jnp.float32
-    )
+def partial_kernel(core_ref, head_here_ref, head_away_ref, here_ref, came_ref, out_ref):
+    del core_ref
+    across = (((1,), (1,)), ((), ()))
+    scores = lax.dot_general(head_here_ref[0], here_ref[0], across, preferred_element_type=jnp.float32)
+    scores += lax.dot_general(head_away_ref[0], came_ref[0], across, preferred_element_type=jnp.float32)
     half = VP // 2
     tail = jnp.concatenate([scores[:half, 256:320], scores[half:, 256:320]], axis=1)
-    out_ref[0, :VP, :] = scores[:, :128].astype(out_ref.dtype)
-    out_ref[0, VP : 2 * VP, :] = scores[:, 128:256].astype(out_ref.dtype)
-    out_ref[0, 2 * VP :, :] = tail.astype(out_ref.dtype)
-
-
-def partial_scores(head, rows):
-    columns, _, width = head.shape
+    out_ref[0, :VP, :] = scores[:, :128]
+    out_ref[0, VP : 2 * VP, :] = scores[:, 128:256]
+    out_ref[0, 2 * VP :, :] = tail
+
+
+def partial_scores(core, head, here, came):
+    chips = head.shape[0]
+    members, width = here.shape[1:]
     return pl.pallas_call(
         partial_kernel,
-        grid=(columns,),
-        in_specs=[
-            pl.BlockSpec((1, VP, width), lambda i: (i, 0, 0)),
-            pl.BlockSpec((1, rows.shape[1], width), lambda i: (i, 0, 0)),
-        ],
-        out_specs=pl.BlockSpec((1, TALL, 128), lambda i: (i, 0, 0)),
-        out_shape=jax.ShapeDtypeStruct((columns, TALL, 128), jnp.float32),
+        grid_spec=pltpu.PrefetchScalarGridSpec(
+            num_scalar_prefetch=1,
+            grid=(chips,),
+            in_specs=[
+                pl.BlockSpec((1, VP, width), lambda i, core_ref: (i, 0, core_ref[0])),
+                pl.BlockSpec((1, VP, width), lambda i, core_ref: (i, 0, 1 - core_ref[0])),
+                pl.BlockSpec((1, members, width), lambda i, core_ref: (i, 0, 0)),
+                pl.BlockSpec((1, members, width), lambda i, core_ref: (i, 0, 0)),
+            ],
+            out_specs=pl.BlockSpec((1, TALL, 128), lambda i, core_ref: (i, 0, 0)),
+        ),
+        out_shape=jax.ShapeDtypeStruct((chips, TALL, 128), jnp.float32),
         compiler_params=pltpu.CompilerParams(vmem_limit_bytes=VMEM),
         name="partial_scores",
-    )(head, rows)
+    )(core[None], head, head, here, came)
 
 
 def unpack(packed):
@@ -137,9 +159,12 @@
     blocks = shards * columns
     members = shards * CAP
 
-    pieces = split_head(head, chips, cores)
     both = jnp.concatenate([text, patches], axis=0)
     everyone = lax.all_gather(both, SEQ, axis=0, tiled=True)
+    squares = jnp.sum(share(jnp.sum(jnp.square(both.astype(jnp.float32)), axis=1), TEN), axis=0)
+
+    pieces, squares = lax.optimization_barrier((split_head(head, chips), squares))
+    head_here = exchange(pieces, "y")
 
     with jax.named_scope("routing"):
         ids = jnp.arange(blocks, dtype=jnp.int32)
@@ -155,7 +180,6 @@
         lists = jnp.sum(jnp.where(rank[None] == slot[:, None, None], value[None], 0), axis=1)
         lists = lists.reshape(CAP, shards, chips, cores).transpose(1, 3, 2, 0).reshape(shards, columns, CAP)
 
-    squares = jnp.sum(jnp.square(both.astype(jnp.float32)), axis=1)
     firsts = image_rows.reshape(slots, IMG)[:, 0].astype(jnp.float32)
     common = jnp.concatenate([squares, firsts])
     message = jnp.concatenate(
@@ -165,9 +189,8 @@
         ],
         axis=1,
     )
-    told = exchange(message, SEQ)
-    told, pieces = lax.optimization_barrier((told, pieces))
-    head_here = exchange(pieces, TEN)
+    told = by_steps(message.reshape(lax.axis_size("x"), lax.axis_size("z"), -1).swapaxes(0, 1), "z")
+    told = by_steps(told.swapaxes(0, 1), "x").reshape(shards, -1)
     told_lists = told[:, : columns * CAP].astype(jnp.int32).reshape(shards, columns, CAP)
     told_squares = told[:, columns * CAP : columns * CAP + 2 * tokens]
     told_firsts = told[:, columns * CAP + 2 * tokens :].astype(jnp.int32)
@@ -179,7 +202,6 @@
         pick = unit[:, None] == jnp.arange(shards * 2 * slots, dtype=jnp.int32)[None, :]
         unit_squares = told_squares.reshape(1, shards * 2 * slots, IMG)
         row_squares = jnp.sum(jnp.where(pick[:, :, None], unit_squares, 0.0), axis=1)
-        row_squares = lax.psum(row_squares, TEN)
         scale = lax.rsqrt(row_squares / D + epsilon)
         gain = lax.dynamic_slice_in_dim(norm_gain, place * width, width, 0)
 
@@ -187,20 +209,22 @@
         groups = shards // GROUP
         token_of = told_lists // 512 - 1 + (jnp.arange(shards, dtype=jnp.int32) % GROUP * tokens)[:, None, None]
         token_of = jnp.where(told_lists > 0, token_of, -1)
-        token_of = token_of.reshape(groups, GROUP, columns, CAP).transpose(0, 2, 1, 3)
+        token_of = token_of.reshape(groups, GROUP, cores, chips, CAP).transpose(0, 2, 3, 1, 4)
+        token_of = jnp.where(core == 0, token_of[:, ::-1], token_of)
         token_of = token_of.reshape(groups, columns * GROUP * CAP, 1)
-        rows = pick_rows(unit, everyone, scale.reshape(-1, 1), gain[None, :], token_of, columns)
-        packed = partial_scores(head_here, rows)
-
-    packed = packed.reshape((cores, chips) + packed.shape[1:])
-    halves = exchange(packed, "core")
-    halves = jnp.sum(halves, axis=0).astype(jnp.float16)
-    parts = exchange(halves, "y")
+        away, here = pick_rows(unit, everyone, scale.reshape(-1, 1), gain[None, :], token_of, chips)
+        came = lax.ppermute(away, "core", [(0, 1), (1, 0)])
+        packed = partial_scores(core, head_here, here, came).astype(jnp.float16)
+
+    mine = lax.dynamic_index_in_dim(told_lists, number, 1, keepdims=False).reshape(members)
+    offset = mine % 512 - 1
+    sent = lax.dynamic_index_in_dim(lists, number, 1, keepdims=False).reshape(members)
+    token = jnp.where(sent > 0, sent // 512 - 1, -1)
+    packed, offset, token = lax.optimization_barrier((packed, offset, token))
+    parts = exchange(packed, "y")
     scores = unpack(jnp.sum(parts.astype(jnp.float32), axis=0))[:VB] / sharpness_divisor
 
     with jax.named_scope("softmax"):
-        mine = lax.dynamic_index_in_dim(told_lists, number, 1, keepdims=False).reshape(members)
-        offset = mine % 512 - 1
         peak = jnp.max(scores, axis=0)
         total = jnp.sum(jnp.exp(scores - peak[None, :]), axis=0)
         entry_id = lax.broadcasted_iota(jnp.int32, scores.shape, 0)
@@ -209,8 +233,6 @@
     answer = exchange(answer.reshape(shards, 3 * CAP), SEQ).reshape(shards, 3, CAP).transpose(1, 0, 2)
     peak, total, picked = answer.reshape(3, members)
     with jax.named_scope("combine"):
-        sent = lax.dynamic_index_in_dim(lists, number, 1, keepdims=False).reshape(members)
-        token = jnp.where(sent > 0, sent // 512 - 1, -1)
         member = token[:, None] == jnp.arange(tokens, dtype=jnp.int32)[None, :]
         local_peak = jnp.max(jnp.where(member, peak[:, None], floor_value), axis=0)
         scaled = jnp.exp(jnp.where(member, peak[:, None] - local_peak[None, :], floor_value))

time: 344 us -> 252 us (0.73)
  blocking collectives: 184 us -> 73.7 us
  starting transfers between devices: 37.8 us -> 60.7 us
  Pallas kernels: 33.2 us -> 27.7 us
    psum x1 -> x0, blocking collectives: 156 us -> none  [per_device(): row_squares = lax.psum(row_squares, TEN)]
    all_to_all x2 -> x3, blocking collectives: 28.1 us -> 73.7 us  [exchange(): return lax.all_to_all(value, axis, split_axis=0, concat_axis=0, tiled=True)]
    ppermute x0 -> x11, starting transfers between devices: none -> 44 us  [the longest x10 41 us: by_steps(): lax.ppermute(turned[step], axis, [(i, (i + step) % count) for i in range(...]
    all_to_all x4 -> x2, waiting for transfers between devices: 45.8 us -> 18.1 us  [exchange(): return lax.all_to_all(value, axis, split_axis=0, concat_axis=0, tiled=True)]
    all_gather x1, waiting for transfers between devices: 0.02 us -> 23.9 us  [per_device(): everyone = lax.all_gather(both, SEQ, axis=0, tiled=True)]
    all_to_all x4 -> x2, starting transfers between devices: 37.8 us -> 16.7 us  [exchange(): return lax.all_to_all(value, axis, split_axis=0, concat_axis=0, tiled=True)]
    pallas_call x2, Pallas kernels: 22.5 us -> 16.4 us  [the longest x1 9.3 us: partial_scores(): pl.pallas_call(partial_kernel, grid_spec=pltpu.PrefetchScalarGridSpec(num...]
    ppermute x0 -> x11, waiting for transfers between devices: none -> 6.12 us  [the longest x10 6.11 us: by_steps(): lax.ppermute(turned[step], axis, [(i, (i + step) % count) for i in range(...]
  transfers between devices with their start and end apart: 5 -> 14, of which waited for: 2 -> 6; matrix products, arithmetic and copies ran while one was open for 4% -> 7% of each run, Pallas kernels for 6% -> 7%
where the time goes in v3:
time: 252 us; the launch traced here: 250 us
  blocking collectives  73.7 us (29%)
  starting transfers between devices  60.7 us (24%)
  waiting for transfers between devices  48.2 us (19%)
  Pallas kernels  27.7 us (11%)
  local copies, waits for them, and re-layouts  17 us (7%)
  between operations  14 us (6%)
  other arithmetic  9.02 us (4%)
    all_to_all x3, blocking collectives, exchange(): return lax.all_to_all(value, axis, split_axis=0, concat_axis=0, tiled=True)  73.7 us
    ppermute x10, starting transfers between devices, by_steps(): lax.ppermute(turned[step], axis, [(i, (i + step) % count) for i in range(...  41 us
    all_gather x1, waiting for transfers between devices, per_device(): everyone = lax.all_gather(both, SEQ, axis=0, tiled=True)  23.9 us
    all_to_all x2, waiting for transfers between devices, exchange(): return lax.all_to_all(value, axis, split_axis=0, concat_axis=0, tiled=True)  18.1 us
    all_to_all x2, starting transfers between devices, exchange(): return lax.all_to_all(value, axis, split_axis=0, concat_axis=0, tiled=True)  16.7 us
    pallas_call x1, Pallas kernels, pick_rows(): pl.pallas_call(rows_kernel, grid_spec=pltpu.PrefetchScalarGridSpec(num_sc...  11.3 us
    pallas_call x1, Pallas kernels, partial_scores(): pl.pallas_call(partial_kernel, grid_spec=pltpu.PrefetchScalarGridSpec(num...  9.3 us
    pallas_call x1, Pallas kernels, split_head(): pl.pallas_call(split_kernel, grid=(chips,), in_specs=[pl.BlockSpec((VP, p...  7.08 us
  transfers between devices with their start and end apart: 14, of which 6 were waited for; matrix products, arithmetic and copies ran while one was open for 7% of the time, Pallas kernels for 7%

profile of v3, /device:TPU:1, one launch (start us, length us, event | category | flops | bytes accessed | tf_op | source)
XLA Modules:
  0.0 250.4 jit_solution(1109709866635238709)
XLA Ops:
  10.8 10.1 %all-to-all-start = ((f32[16,1,256]{2,1,0:T(1,128)}), f32[16,1,256]{2,1,0:T(1,128)S(1)}, u32[]{:S(2)}, u32[]{:S(2)}) async-start(f32[16,1,256]{2,1,0:T(1,128)} %broadcast_in_dim.137), calls=%async_computation | async-start | bytes 32768 | tf_op jit(solution)/shard_map/all_to_all | solution.py:27
  26.5 7.1 %split_head.1 = bf16[8,304,1024]{2,1,0:T(8,128)(2,1)} custom-call(bf16[297,8192]{1,0:T(8,128)(2,1)} %head_ref.1), custom_call_target="tpu_custom_call" | custom-call | tf_op jit(solution)/shard_map/split_head/pallas_call | solution.py:53
  33.6 6.6 %all-to-all-start.1 = ((bf16[8,304,1024]{2,1,0:T(8,128)(2,1)}), bf16[8,304,1024]{2,1,0:T(8,128)(2,1)}, u32[]{:S(2)}, u32[]{:S(2)}) async-start(bf16[8,304,1024]{2,1,0:T(8,128)(2,1)} %split_head.1), calls=%async_computation.1 | async-start | bytes 9961472 | tf_op jit(solution)/shard_map/all_to_all | solution.py:27
  40.3 9.1 %collective-permute-start = (f32[4,418]{1,0:T(4,128)S(1)}, f32[4,418]{1,0:T(4,128)S(1)}, u32[]{:S(2)}, u32[]{:S(2)}) collective-permute-start(f32[4,418]{1,0:T(4,128)S(1)} %get-tuple-element.37), channel_id=1, source_target_pairs={{0,112},{16,0},{32,16},{48,32},{64,48},{80,64},{96,80},{112,96},{1... | collective-permute-start | bytes 20072 | tf_op jit(solution)/shard_map/ppermute | solution.py:40
  53.4 4.5 %collective-permute-start.4 = (f32[4,418]{1,0:T(4,128)S(1)}, f32[4,418]{1,0:T(4,128)S(1)}, u32[]{:S(2)}, u32[]{:S(2)}) collective-permute-start(f32[4,418]{1,0:T(4,128)S(1)} %get-tuple-element.33), channel_id=1, source_target_pairs={{0,48},{16,64},{32,80},{48,96},{64,112},{80,0},{96,16},{112,32},{1... | collective-permute-start | bytes 20072 | tf_op jit(solution)/shard_map/ppermute | solution.py:40
  57.9 5.0 %collective-permute-start.3 = (f32[4,418]{1,0:T(4,128)S(1)}, f32[4,418]{1,0:T(4,128)S(1)}, u32[]{:S(2)}, u32[]{:S(2)}) collective-permute-start(f32[4,418]{1,0:T(4,128)S(1)} %get-tuple-element.34), channel_id=1, source_target_pairs={{0,64},{16,80},{32,96},{48,112},{64,0},{80,16},{96,32},{112,48},{1... | collective-permute-start | bytes 20072 | tf_op jit(solution)/shard_map/ppermute | solution.py:40
  62.9 5.5 %collective-permute-start.1 = (f32[4,418]{1,0:T(4,128)S(1)}, f32[4,418]{1,0:T(4,128)S(1)}, u32[]{:S(2)}, u32[]{:S(2)}) collective-permute-start(f32[4,418]{1,0:T(4,128)S(1)} %get-tuple-element.36), channel_id=1, source_target_pairs={{0,96},{16,112},{32,0},{48,16},{64,32},{80,48},{96,64},{112,80},{1... | collective-permute-start | bytes 20072 | tf_op jit(solution)/shard_map/ppermute | solution.py:40
  69.1 3.7 %collective-permute-start.2 = (f32[4,418]{1,0:T(4,128)S(1)}, f32[4,418]{1,0:T(4,128)S(1)}, u32[]{:S(2)}, u32[]{:S(2)}) collective-permute-start(f32[4,418]{1,0:T(4,128)S(1)} %get-tuple-element.35), channel_id=1, source_target_pairs={{0,80},{16,96},{32,112},{48,0},{64,16},{80,32},{96,48},{112,64},{1... | collective-permute-start | bytes 20072 | tf_op jit(solution)/shard_map/ppermute | solution.py:40
  72.8 2.8 %collective-permute-done.2 = f32[4,418]{1,0:T(4,128)S(1)} collective-permute-done((f32[4,418]{1,0:T(4,128)S(1)}, f32[4,418]{1,0:T(4,128)S(1)}, u32[]{:S(2)}, u32[]{:S(2)}) %collective-permute-start.2) | collective-permute-done | bytes 6720 | tf_op jit(solution)/shard_map/ppermute | solution.py:40
  76.1 4.4 %collective-permute-start.7 = (f32[8,418]{1,0:T(8,128)S(1)}, f32[8,418]{1,0:T(8,128)S(1)}, u32[]{:S(2)}, u32[]{:S(2)}) collective-permute-start(f32[8,418]{1,0:T(8,128)S(1)} %bitcast.100), channel_id=1, source_target_pairs={{0,384},{128,0},{256,128},{384,256},{1,385},{129,1},{257,129},{385... | collective-permute-start | bytes 40136 | tf_op jit(solution)/shard_map/ppermute | solution.py:40
  80.5 2.4 collective-permute-start.8
  82.9 2.5 collective-permute-start.9
  87.0 2.3 collective-permute-done.9
  91.3 3.4 %rsqrt.15.refs_16_ = f32[4096,1]{1,0:T(8,128)} reshape(f32[64,64]{1,0:T(8,128)S(1)} %add_rsqrt_fusion) | data formatting | bytes 32768 | tf_op jit(solution)/shard_map/merge/rsqrt | solution.py:205
  94.7 2.2 reshape.211.refs_18_
  96.9 23.9 %all-gather.2.cloned.1.call-done.refs_0_.refs_1_.refs_2_.refs_3_.refs_4_.refs_5_.refs_6_.refs_7_.refs_8_.refs_9_.refs_10_.refs_11_.refs_12_.refs_13_.refs_14_.refs_15_ = bf16[8192,512]{1,0:T(8,128)(2,1)} async-done(((bf16[256,512]{1,0:T(8,128)(2,1)}), bf16[8192,512]{1,0:T(8,128)(2,1)}) %all-gather.2.cloned.1.call-update) | async-done | bytes 8388624 | tf_op jit(solution)/shard_map/all_gather | solution.py:163
  120.8 11.3 %pick_rows.1 = (bf16[8,320,512]{2,1,0:T(8,128)(2,1)}, bf16[8,320,512]{2,1,0:T(8,128)(2,1)}) custom-call(s32[64]{0:T(128)} %copy-done.2, bf16[8192,512]{1,0:T(8,128)(2,1)} %all-gather.2.cloned.1.call-done.refs_0_.refs_1_.refs_2_.refs_3_.refs_4_.refs_5_.refs_6_.refs_7_.refs_8_.refs_9_.refs_10_.refs_11_.refs_12_.refs_13_.refs_14_.refs_15_, ...), custom_call_target="tpu_custom_call" | custom-call | tf_op jit(solution)/shard_map/partial/pick_rows/pallas_call | solution.py:89
  132.1 3.0 %collective-permute-start.10 = (bf16[8,320,512]{2,1,0:T(8,128)(2,1)}, bf16[8,320,512]{2,1,0:T(8,128)(2,1)S(1)}, u32[]{:S(2)}, u32[]{:S(2)}) collective-permute-start(bf16[8,320,512]{2,1,0:T(8,128)(2,1)} %get-tuple-element.15), channel_id=1, source_target_pairs={{0,1},{1,0},{2,3},{3,2},{4,5},{5,4},{6,7},{7,6},{8,9},{9,8},{10,11... | collective-permute-start | bytes 7864328 | tf_op jit(solution)/shard_map/partial/ppermute | solution.py:216
  135.9 18.1 %all-to-all-done.1.head_here_ref.head_away_ref = bf16[8,304,1024]{2,1,0:T(8,128)(2,1)} async-done(((bf16[8,304,1024]{2,1,0:T(8,128)(2,1)}), bf16[8,304,1024]{2,1,0:T(8,128)(2,1)}, u32[]{:S(2)}, u32[]{:S(2)}) %all-to-all-start.1) | async-done | bytes 4980768 | tf_op jit(solution)/shard_map/all_to_all | solution.py:27
  155.4 9.3 %partial_scores.1 = f32[8,760,128]{2,1,0:T(8,128)} custom-call(s32[1]{0:T(128)} %bitcast.core_ref, bf16[8,304,1024]{2,1,0:T(8,128)(2,1)} %all-to-all-done.1.head_here_ref.head_away_ref, bf16[8,304,1024]{2,1,0:T(8,128)(2,1)} %all-to-all-done.1.head_here_ref.head_away_ref, bf16[8,320,512]{2,1,0:T(8,128)(2,1)} %get-tuple-element.14.here_ref, ...), custom_call_target="tpu_custom_call" | custom-call | tf_op jit(solution)/shard_map/partial/partial_scores/pallas_call | solution.py:124
  164.8 2.1 convert_element_type.41
  166.8 42.3 %all_to_all.30 = f16[8,760,128]{2,1,0:T(8,128)(2,1)S(1)} all-to-all(f16[8,760,128]{2,1,0:T(8,128)(2,1)S(1)} %convert_element_type.41), channel_id=1, replica_groups=mesh['x'=4,'z'=8,'y'=8,'core'=2] {'y'}, dimensions={0} | all-to-all | bytes 3112960 | tf_op jit(solution)/shard_map/all_to_all | solution.py:27
  210.4 19.9 %all_to_all.31 = f32[32,1,30]{2,1,0:T(1,128)S(1)} all-to-all(f32[32,1,30]{2,1,0:T(1,128)S(1)} %copy.170), channel_id=1, replica_groups=mesh['x'=4,'z'=8,'y'=8,'core'=2] {'x','z'}, dimensions={0} | all-to-all | bytes 7680 | tf_op jit(solution)/shard_map/all_to_all | solution.py:27
  231.5 11.5 %all_to_all.32 = f32[16,3,128]{2,1,0:T(4,128)S(1)} all-to-all(f32[16,3,128]{2,1,0:T(4,128)S(1)} %broadcast_in_dim.157), channel_id=1, replica_groups=mesh['x'=4,'z'=8,'y'=8,'core'=2] {'core','y'}, dimensions={0} | all-to-all | bytes 49152 | tf_op jit(solution)/shard_map/all_to_all | solution.py:27
  (132 shorter events, 23.4 us)
Async XLA Ops:
  6.5 114.3 %all-gather.2.cloned.1.call-start = ((), (), s32[]{:S(2)}) async-start(), calls=%async_computation.5 | async-start | bytes 8650752 | tf_op jit(solution)/shard_map/all_gather | solution.py:163
  8.4 0.7 copy-start.1
  10.8 22.8 %all-to-all-start = ((f32[16,1,256]{2,1,0:T(1,128)}), f32[16,1,256]{2,1,0:T(1,128)S(1)}, u32[]{:S(2)}, u32[]{:S(2)}) async-start(f32[16,1,256]{2,1,0:T(1,128)} %broadcast_in_dim.137), calls=%async_computation | async-start | bytes 32768 | tf_op jit(solution)/shard_map/all_to_all | solution.py:27
  33.6 120.4 %all-to-all-start.1 = ((bf16[8,304,1024]{2,1,0:T(8,128)(2,1)}), bf16[8,304,1024]{2,1,0:T(8,128)(2,1)}, u32[]{:S(2)}, u32[]{:S(2)}) async-start(bf16[8,304,1024]{2,1,0:T(8,128)(2,1)} %split_head.1), calls=%async_computation.1 | async-start | bytes 9961472 | tf_op jit(solution)/shard_map/all_to_all | solution.py:27
  40.3 22.5 %collective-permute-start = (f32[4,418]{1,0:T(4,128)S(1)}, f32[4,418]{1,0:T(4,128)S(1)}, u32[]{:S(2)}, u32[]{:S(2)}) collective-permute-start(f32[4,418]{1,0:T(4,128)S(1)} %get-tuple-element.37), channel_id=1, source_target_pairs={{0,112},{16,0},{32,16},{48,32},{64,48},{80,64},{96,80},{112,96},{1... | collective-permute-start | bytes 20072 | tf_op jit(solution)/shard_map/ppermute | solution.py:40
  49.5 26.2 %collective-permute-start.6 = (f32[4,418]{1,0:T(4,128)S(1)}, f32[4,418]{1,0:T(4,128)S(1)}, u32[]{:S(2)}, u32[]{:S(2)}) collective-permute-start(f32[4,418]{1,0:T(4,128)S(1)} %get-tuple-element.31), channel_id=1, source_target_pairs={{0,16},{16,32},{32,48},{48,64},{64,80},{80,96},{96,112},{112,0},{1... | collective-permute-start | bytes 20072 | tf_op jit(solution)/shard_map/ppermute | solution.py:40
  51.4 24.3 %collective-permute-start.5 = (f32[4,418]{1,0:T(4,128)S(1)}, f32[4,418]{1,0:T(4,128)S(1)}, u32[]{:S(2)}, u32[]{:S(2)}) collective-permute-start(f32[4,418]{1,0:T(4,128)S(1)} %get-tuple-element.32), channel_id=1, source_target_pairs={{0,32},{16,48},{32,64},{48,80},{64,96},{80,112},{96,0},{112,16},{1... | collective-permute-start | bytes 20072 | tf_op jit(solution)/shard_map/ppermute | solution.py:40
  53.4 22.3 %collective-permute-start.4 = (f32[4,418]{1,0:T(4,128)S(1)}, f32[4,418]{1,0:T(4,128)S(1)}, u32[]{:S(2)}, u32[]{:S(2)}) collective-permute-start(f32[4,418]{1,0:T(4,128)S(1)} %get-tuple-element.33), channel_id=1, source_target_pairs={{0,48},{16,64},{32,80},{48,96},{64,112},{80,0},{96,16},{112,32},{1... | collective-permute-start | bytes 20072 | tf_op jit(solution)/shard_map/ppermute | solution.py:40
  57.9 17.8 %collective-permute-start.3 = (f32[4,418]{1,0:T(4,128)S(1)}, f32[4,418]{1,0:T(4,128)S(1)}, u32[]{:S(2)}, u32[]{:S(2)}) collective-permute-start(f32[4,418]{1,0:T(4,128)S(1)} %get-tuple-element.34), channel_id=1, source_target_pairs={{0,64},{16,80},{32,96},{48,112},{64,0},{80,16},{96,32},{112,48},{1... | collective-permute-start | bytes 20072 | tf_op jit(solution)/shard_map/ppermute | solution.py:40
  62.9 6.3 %collective-permute-start.1 = (f32[4,418]{1,0:T(4,128)S(1)}, f32[4,418]{1,0:T(4,128)S(1)}, u32[]{:S(2)}, u32[]{:S(2)}) collective-permute-start(f32[4,418]{1,0:T(4,128)S(1)} %get-tuple-element.36), channel_id=1, source_target_pairs={{0,96},{16,112},{32,0},{48,16},{64,32},{80,48},{96,64},{112,80},{1... | collective-permute-start | bytes 20072 | tf_op jit(solution)/shard_map/ppermute | solution.py:40
  69.1 6.6 %collective-permute-start.2 = (f32[4,418]{1,0:T(4,128)S(1)}, f32[4,418]{1,0:T(4,128)S(1)}, u32[]{:S(2)}, u32[]{:S(2)}) collective-permute-start(f32[4,418]{1,0:T(4,128)S(1)} %get-tuple-element.35), channel_id=1, source_target_pairs={{0,80},{16,96},{32,112},{48,0},{64,16},{80,32},{96,48},{112,64},{1... | collective-permute-start | bytes 20072 | tf_op jit(solution)/shard_map/ppermute | solution.py:40
  76.1 10.7 %collective-permute-start.7 = (f32[8,418]{1,0:T(8,128)S(1)}, f32[8,418]{1,0:T(8,128)S(1)}, u32[]{:S(2)}, u32[]{:S(2)}) collective-permute-start(f32[8,418]{1,0:T(8,128)S(1)} %bitcast.100), channel_id=1, source_target_pairs={{0,384},{128,0},{256,128},{384,256},{1,385},{129,1},{257,129},{385... | collective-permute-start | bytes 40136 | tf_op jit(solution)/shard_map/ppermute | solution.py:40
  80.5 6.6 %collective-permute-start.8 = (f32[8,418]{1,0:T(8,128)S(1)}, f32[8,418]{1,0:T(8,128)S(1)}, u32[]{:S(2)}, u32[]{:S(2)}) collective-permute-start(f32[8,418]{1,0:T(8,128)S(1)} %bitcast.99), channel_id=1, source_target_pairs={{0,256},{128,384},{256,0},{384,128},{1,257},{129,385},{257,1},{385... | collective-permute-start | bytes 40136 | tf_op jit(solution)/shard_map/ppermute | solution.py:40
  82.9 6.4 %collective-permute-start.9 = (f32[8,418]{1,0:T(8,128)S(1)}, f32[8,418]{1,0:T(8,128)S(1)}, u32[]{:S(2)}, u32[]{:S(2)}) collective-permute-start(f32[8,418]{1,0:T(8,128)S(1)} %bitcast.98), channel_id=1, source_target_pairs={{0,128},{128,256},{256,384},{384,0},{1,129},{129,257},{257,385},{3... | collective-permute-start | bytes 40136 | tf_op jit(solution)/shard_map/ppermute | solution.py:40
  89.9 7.0 %copy-start.2 = (s32[64]{0:T(128)}, s32[64]{0:T(128)S(1)}, u32[]{:S(2)}) copy-start(s32[64]{0:T(128)S(1)} %reshape.203.unit_ref) | copy-start | bytes 772
  132.1 21.9 %collective-permute-start.10 = (bf16[8,320,512]{2,1,0:T(8,128)(2,1)}, bf16[8,320,512]{2,1,0:T(8,128)(2,1)S(1)}, u32[]{:S(2)}, u32[]{:S(2)}) collective-permute-start(bf16[8,320,512]{2,1,0:T(8,128)(2,1)} %get-tuple-element.15), channel_id=1, source_target_pairs={{0,1},{1,0},{2,3},{3,2},{4,5},{5,4},{6,7},{7,6},{8,9},{9,8},{10,11... | collective-permute-start | bytes 7864328 | tf_op jit(solution)/shard_map/partial/ppermute | solution.py:216
  154.0 1.5 copy-start
Sparse Core Ops, SparseCore 0:
  10.5 110.2 all-gather.1

commit v4 on v3

--- a/solution.py
+++ b/solution.py
@@ -13,6 +13,7 @@
 CAP = 10
 GROUP = 8
 TALL = 760
+STEPS = ((4, 3, 5), (2, 6, 1, 7, 0))
 VMEM = 60 * 2**20
 
 sharpness_divisor = 0.7
@@ -43,9 +44,35 @@
     return lax.dynamic_slice_in_dim(twice, count - 1 - me, count, 0)
 
 
+def front_kernel(text_ref, patches_ref, both_ref, squares_ref):
+    tokens = text_ref.shape[0]
+    for i, ref in enumerate((text_ref, patches_ref)):
+        rows = ref[...]
+        both_ref[pl.ds(i * tokens, tokens), :] = rows
+        square = jnp.square(rows.astype(jnp.float32))
+        square = sum(square[:, k : k + 128] for k in range(0, square.shape[1], 128))
+        total = jnp.sum(square.T, axis=0, keepdims=True)
+        squares_ref[:, i, :] = jnp.broadcast_to(total, (squares_ref.shape[0], tokens))
+
+
+def front(text, patches, copies):
+    tokens, width = text.shape
+    return pl.pallas_call(
+        front_kernel,
+        out_shape=[
+            jax.ShapeDtypeStruct((2 * tokens, width), jnp.bfloat16),
+            jax.ShapeDtypeStruct((copies, 2, tokens), jnp.float32),
+        ],
+        name="front",
+    )(text, patches)
+
+
 def split_kernel(head_ref, out_ref):
-    rows = lax.broadcasted_iota(jnp.int32, out_ref.shape[1:], 0)
-    out_ref[0] = jnp.where(rows < VB, head_ref[...].astype(jnp.float32), 0.0).astype(jnp.bfloat16)
+    whole = VP - 16
+    out_ref[0, :whole] = head_ref[:whole]
+    last = head_ref[whole:].astype(jnp.float32)
+    rows = lax.broadcasted_iota(jnp.int32, last.shape, 0) + whole
+    out_ref[0, whole:] = jnp.where(rows < VB, last, 0.0).astype(jnp.bfloat16)
 
 
 def split_head(head, chips):
@@ -61,25 +88,37 @@
     )(head)
 
 
+def column(row):
+    return jnp.broadcast_to(row, (128, 128)).T
+
+
 def rows_kernel(unit_ref, *refs):
     del unit_ref
-    *pieces, scale_ref, gain_ref, token_ref, away_ref, here_ref, normed_ref = refs
-    for i, piece in enumerate(pieces):
-        span = pl.ds(i * IMG, IMG)
-        values = piece[...].astype(jnp.float32)
-        normed_ref[span, :] = (values * scale_ref[span, :] * gain_ref[...]).astype(jnp.bfloat16)
-    token = token_ref[0]
-    half = token.shape[0] // 2
+    *pieces, scale_ref, gain_ref, token_ref, away_ref, here_ref, normed_ref, hot_ref = refs
+    shards, tokens = scale_ref.shape[1:]
+    per = tokens // IMG
+    for shard in range(shards):
+        scale = column(scale_ref[0, shard : shard + 1])
+        scale = jnp.concatenate([scale] * (normed_ref.shape[1] // 128), axis=1)
+        for slot in range(per):
+            values = pieces[shard * per + slot][...].astype(jnp.float32)
+            rows = values * scale[slot * IMG : (slot + 1) * IMG] * gain_ref[...]
+            normed_ref[pl.ds(shard * tokens + slot * IMG, IMG), :] = rows.astype(jnp.bfloat16)
+    lane = lax.broadcasted_iota(jnp.int32, (128, 128), 1)
+    for chunk in range(token_ref.shape[1]):
+        token = column(token_ref[0, chunk : chunk + 1])
+        for shard in range(shards):
+            hot = (token == lane + shard * tokens).astype(jnp.float32).astype(jnp.bfloat16)
+            hot_ref[pl.ds(chunk * 128, 128), pl.ds(shard * tokens, tokens)] = hot
+    half = hot_ref.shape[0] // 2
     for part, out_ref in enumerate((away_ref, here_ref)):
-        wanted = token[part * half : (part + 1) * half]
-        shape = (half, normed_ref.shape[0])
-        hot = (wanted == lax.broadcasted_iota(jnp.int32, shape, 1)).astype(jnp.float32).astype(jnp.bfloat16)
-        rows = jnp.dot(hot, normed_ref[...], preferred_element_type=jnp.float32)
+        rows = jnp.dot(hot_ref[pl.ds(part * half, half), :], normed_ref[...], preferred_element_type=jnp.float32)
         out_ref[...] = rows.astype(jnp.bfloat16).reshape(out_ref.shape)
 
 
 def pick_rows(unit, everyone, scale, gain, token_of, chips):
-    groups, pairs, _ = token_of.shape
+    groups, chunks, _ = token_of.shape
+    pairs = chunks * 128
     width = everyone.shape[1]
     units = unit.shape[0] // groups
     each = pairs // (2 * chips)
@@ -93,21 +132,24 @@
             grid=(groups,),
             in_specs=piece
             + [
-                pl.BlockSpec((units * IMG, 1), lambda g, unit_ref: (g, 0)),
+                pl.BlockSpec((1,) + scale.shape[1:], lambda g, unit_ref: (g, 0, 0)),
                 pl.BlockSpec((1, width), lambda g, unit_ref: (0, 0)),
-                pl.BlockSpec((1, pairs, 1), lambda g, unit_ref: (g, 0, 0)),
+                pl.BlockSpec((1, chunks, 128), lambda g, unit_ref: (g, 0, 0)),
             ],
             out_specs=[pl.BlockSpec((chips, each, width), lambda g, unit_ref: (0, g, 0))] * 2,
-            scratch_shapes=[pltpu.VMEM((units * IMG, width), jnp.bfloat16)],
+            scratch_shapes=[
+                pltpu.VMEM((units * IMG, width), jnp.bfloat16),
+                pltpu.VMEM((pairs, units * IMG), jnp.bfloat16),
+            ],
         ),
         out_shape=[jax.ShapeDtypeStruct((chips, groups * each, width), jnp.bfloat16)] * 2,
-        compiler_params=pltpu.CompilerParams(vmem_limit_bytes=VMEM),
+        compiler_params=pltpu.CompilerParams(vmem_limit_bytes=56 * 2**20),
         name="pick_rows",
     )(unit, *([everyone] * units), scale, gain, token_of)
 
 
-def partial_kernel(core_ref, head_here_ref, head_away_ref, here_ref, came_ref, out_ref):
-    del core_ref
+def partial_kernel(order_ref, head_here_ref, head_away_ref, here_ref, came_ref, out_ref):
+    del order_ref
     across = (((1,), (1,)), ((), ()))
     scores = lax.dot_general(head_here_ref[0], here_ref[0], across, preferred_element_type=jnp.float32)
     scores += lax.dot_general(head_away_ref[0], came_ref[0], across, preferred_element_type=jnp.float32)
@@ -118,8 +160,9 @@
     out_ref[0, 2 * VP :, :] = tail
 
 
-def partial_scores(core, head, here, came):
-    chips = head.shape[0]
+def partial_scores(core, order, head, here, came):
+    chips = order.shape[0]
+    order = jnp.append(order, core)
     members, width = here.shape[1:]
     return pl.pallas_call(
         partial_kernel,
@@ -127,17 +170,17 @@
             num_scalar_prefetch=1,
             grid=(chips,),
             in_specs=[
-                pl.BlockSpec((1, VP, width), lambda i, core_ref: (i, 0, core_ref[0])),
-                pl.BlockSpec((1, VP, width), lambda i, core_ref: (i, 0, 1 - core_ref[0])),
-                pl.BlockSpec((1, members, width), lambda i, core_ref: (i, 0, 0)),
-                pl.BlockSpec((1, members, width), lambda i, core_ref: (i, 0, 0)),
+                pl.BlockSpec((1, VP, width), lambda i, order_ref: (order_ref[i], 0, order_ref[chips])),
+                pl.BlockSpec((1, VP, width), lambda i, order_ref: (order_ref[i], 0, 1 - order_ref[chips])),
+                pl.BlockSpec((1, members, width), lambda i, order_ref: (order_ref[i], 0, 0)),
+                pl.BlockSpec((1, members, width), lambda i, order_ref: (order_ref[i], 0, 0)),
             ],
-            out_specs=pl.BlockSpec((1, TALL, 128), lambda i, core_ref: (i, 0, 0)),
+            out_specs=pl.BlockSpec((1, TALL, 128), lambda i, order_ref: (i, 0, 0)),
         ),
         out_shape=jax.ShapeDtypeStruct((chips, TALL, 128), jnp.float32),
-        compiler_params=pltpu.CompilerParams(vmem_limit_bytes=VMEM),
+        compiler_params=pltpu.CompilerParams(vmem_limit_bytes=16 * 2**20),
         name="partial_scores",
-    )(core[None], head, head, here, came)
+    )(order, head, head, here, came)
 
 
 def unpack(packed):
@@ -159,11 +202,11 @@
     blocks = shards * columns
     members = shards * CAP
 
-    both = jnp.concatenate([text, patches], axis=0)
+    both, squares = front(text, patches, columns)
     everyone = lax.all_gather(both, SEQ, axis=0, tiled=True)
-    squares = jnp.sum(share(jnp.sum(jnp.square(both.astype(jnp.float32)), axis=1), TEN), axis=0)
-
-    pieces, squares = lax.optimization_barrier((split_head(head, chips), squares))
+    squares = jnp.sum(exchange(squares, TEN), axis=0).reshape(-1)
+
+    pieces, squares, nucleus, code = lax.optimization_barrier((split_head(head, chips), squares, nucleus, code))
     head_here = exchange(pieces, "y")
 
     with jax.named_scope("routing"):
@@ -211,18 +254,27 @@
         token_of = jnp.where(told_lists > 0, token_of, -1)
         token_of = token_of.reshape(groups, GROUP, cores, chips, CAP).transpose(0, 2, 3, 1, 4)
         token_of = jnp.where(core == 0, token_of[:, ::-1], token_of)
-        token_of = token_of.reshape(groups, columns * GROUP * CAP, 1)
-        away, here = pick_rows(unit, everyone, scale.reshape(-1, 1), gain[None, :], token_of, chips)
+        token_of = token_of.reshape(groups, columns * GROUP * CAP // 128, 128)
+        away, here = pick_rows(unit, everyone, scale.reshape(groups, GROUP, tokens), gain[None, :], token_of, chips)
         came = lax.ppermute(away, "core", [(0, 1), (1, 0)])
-        packed = partial_scores(core, head_here, here, came).astype(jnp.float16)
+        packed = []
+        for part in STEPS:
+            order = (y + jnp.array(part, jnp.int32)) % chips
+            packed.append(partial_scores(core, order, head_here, here, came))
 
     mine = lax.dynamic_index_in_dim(told_lists, number, 1, keepdims=False).reshape(members)
     offset = mine % 512 - 1
     sent = lax.dynamic_index_in_dim(lists, number, 1, keepdims=False).reshape(members)
     token = jnp.where(sent > 0, sent // 512 - 1, -1)
-    packed, offset, token = lax.optimization_barrier((packed, offset, token))
-    parts = exchange(packed, "y")
-    scores = unpack(jnp.sum(parts.astype(jnp.float32), axis=0))[:VB] / sharpness_divisor
+    total = 0.0
+    for part, scores in zip(STEPS, packed):
+        for i, step in enumerate(part):
+            if step == 0:
+                total += scores[i]
+            else:
+                sent_part = scores[i].astype(jnp.float16)
+                total += lax.ppermute(sent_part, "y", [(k, (k + step) % 8) for k in range(8)]).astype(jnp.float32)
+    scores = unpack(total)[:VB] / sharpness_divisor
 
     with jax.named_scope("softmax"):
         peak = jnp.max(scores, axis=0)

time: 252 us -> 237 us (0.940)
  blocking collectives: 73.7 us -> 35 us
  starting transfers between devices: 60.7 us -> 83.6 us
  waiting for transfers between devices: 48.2 us -> 58.5 us
  local copies, waits for them, and re-layouts: 17 us -> 9.57 us
  other arithmetic: 9.02 us -> 4.87 us
    all_to_all x3 -> x2, blocking collectives: 73.7 us -> 35 us  [exchange(): return lax.all_to_all(value, axis, split_axis=0, concat_axis=0, tiled=True)]
    ppermute x0 -> x7, starting transfers between devices: none -> 22.8 us  [per_device(): lax.ppermute(sent_part, 'y', [(k, (k + step) % 8) for k in range(8)])]
    ppermute x0 -> x7, waiting for transfers between devices: none -> 9.84 us  [per_device(): lax.ppermute(sent_part, 'y', [(k, (k + step) % 8) for k in range(8)])]
    all_gather x1, waiting for transfers between devices: 23.9 us -> 32.7 us  [per_device(): everyone = lax.all_gather(both, SEQ, axis=0, tiled=True)]
    all_to_all x2, waiting for transfers between devices: 18.1 us -> 9.79 us  [exchange(): return lax.all_to_all(value, axis, split_axis=0, concat_axis=0, tiled=True)]
    rsqrt x1, local copies, waits for them, and re-layouts: 3.41 us -> 0.67 us  [per_device(): scale = lax.rsqrt(row_squares / D + epsilon)]
    pallas_call x1 -> x2, Pallas kernels: 9.3 us -> 9.29 us  [partial_scores(): pl.pallas_call(partial_kernel, grid_spec=pltpu.PrefetchScalarGridSpec(num...]
  transfers between devices with their start and end apart: 14 -> 21, of which waited for: 6 -> 9; matrix products, arithmetic and copies ran while one was open for 7% -> 4% of each run, Pallas kernels for 7% -> 10%
where the time goes in v4:
time: 237 us; the launch traced here: 236 us
  starting transfers between devices  83.6 us (35%)
  waiting for transfers between devices  58.5 us (25%)
  blocking collectives  35 us (15%)
  Pallas kernels  30.2 us (13%)
  between operations  14.1 us (6%)
  local copies, waits for them, and re-layouts  9.57 us (4%)
  other arithmetic  4.87 us (2%)
    ppermute x10, starting transfers between devices, by_steps(): lax.ppermute(turned[step], axis, [(i, (i + step) % count) for i in range(...  40.9 us
    all_to_all x2, blocking collectives, exchange(): return lax.all_to_all(value, axis, split_axis=0, concat_axis=0, tiled=True)  35 us
    all_gather x1, waiting for transfers between devices, per_device(): everyone = lax.all_gather(both, SEQ, axis=0, tiled=True)  32.7 us
    ppermute x7, starting transfers between devices, per_device(): lax.ppermute(sent_part, 'y', [(k, (k + step) % 8) for k in range(8)])  22.8 us
    all_to_all x2, starting transfers between devices, exchange(): return lax.all_to_all(value, axis, split_axis=0, concat_axis=0, tiled=True)  16.9 us
    pallas_call x1, Pallas kernels, pick_rows(): pl.pallas_call(rows_kernel, grid_spec=pltpu.PrefetchScalarGridSpec(num_sc...  12.2 us
    ppermute x7, waiting for transfers between devices, per_device(): lax.ppermute(sent_part, 'y', [(k, (k + step) % 8) for k in range(8)])  9.84 us
    all_to_all x2, waiting for transfers between devices, exchange(): return lax.all_to_all(value, axis, split_axis=0, concat_axis=0, tiled=True)  9.79 us
  transfers between devices with their start and end apart: 21, of which 9 were waited for; matrix products, arithmetic and copies ran while one was open for 4% of the time, Pallas kernels for 10%

profile of v4, /device:TPU:1, one launch (start us, length us, event | category | flops | bytes accessed | tf_op | source)
XLA Modules:
  0.0 236.1 jit_solution(5500182360650387706)
XLA Ops:
  8.3 10.1 %all-to-all-start = ((f32[16,2,128]{2,1,0:T(2,128)}), f32[16,2,128]{2,1,0:T(2,128)S(1)}, u32[]{:S(2)}, u32[]{:S(2)}) async-start(f32[16,2,128]{2,1,0:T(2,128)} %get-tuple-element.13), calls=%async_computation | async-start | bytes 32768 | tf_op jit(solution)/shard_map/all_to_all | solution.py:28
  19.3 7.1 %split_head.1 = bf16[8,304,1024]{2,1,0:T(8,128)(2,1)} custom-call(bf16[297,8192]{1,0:T(8,128)(2,1)} %head_ref.1), custom_call_target="tpu_custom_call" | custom-call | tf_op jit(solution)/shard_map/split_head/pallas_call | solution.py:80
  26.4 6.7 %all-to-all-start.1 = ((bf16[8,304,1024]{2,1,0:T(8,128)(2,1)}), bf16[8,304,1024]{2,1,0:T(8,128)(2,1)}, u32[]{:S(2)}, u32[]{:S(2)}) async-start(bf16[8,304,1024]{2,1,0:T(8,128)(2,1)} %split_head.1), calls=%async_computation.1 | async-start | bytes 9961472 | tf_op jit(solution)/shard_map/all_to_all | solution.py:28
  35.9 9.2 %collective-permute-start = (f32[4,418]{1,0:T(4,128)S(1)}, f32[4,418]{1,0:T(4,128)S(1)}, u32[]{:S(2)}, u32[]{:S(2)}) collective-permute-start(f32[4,418]{1,0:T(4,128)S(1)} %get-tuple-element.46), channel_id=1, source_target_pairs={{0,112},{16,0},{32,16},{48,32},{64,48},{80,64},{96,80},{112,96},{1... | collective-permute-start | bytes 20072 | tf_op jit(solution)/shard_map/ppermute | solution.py:41
  48.9 4.5 %collective-permute-start.4 = (f32[4,418]{1,0:T(4,128)S(1)}, f32[4,418]{1,0:T(4,128)S(1)}, u32[]{:S(2)}, u32[]{:S(2)}) collective-permute-start(f32[4,418]{1,0:T(4,128)S(1)} %get-tuple-element.42), channel_id=1, source_target_pairs={{0,48},{16,64},{32,80},{48,96},{64,112},{80,0},{96,16},{112,32},{1... | collective-permute-start | bytes 20072 | tf_op jit(solution)/shard_map/ppermute | solution.py:41
  53.4 5.0 %collective-permute-start.3 = (f32[4,418]{1,0:T(4,128)S(1)}, f32[4,418]{1,0:T(4,128)S(1)}, u32[]{:S(2)}, u32[]{:S(2)}) collective-permute-start(f32[4,418]{1,0:T(4,128)S(1)} %get-tuple-element.43), channel_id=1, source_target_pairs={{0,64},{16,80},{32,96},{48,112},{64,0},{80,16},{96,32},{112,48},{1... | collective-permute-start | bytes 20072 | tf_op jit(solution)/shard_map/ppermute | solution.py:41
  58.4 5.5 %collective-permute-start.1 = (f32[4,418]{1,0:T(4,128)S(1)}, f32[4,418]{1,0:T(4,128)S(1)}, u32[]{:S(2)}, u32[]{:S(2)}) collective-permute-start(f32[4,418]{1,0:T(4,128)S(1)} %get-tuple-element.45), channel_id=1, source_target_pairs={{0,96},{16,112},{32,0},{48,16},{64,32},{80,48},{96,64},{112,80},{1... | collective-permute-start | bytes 20072 | tf_op jit(solution)/shard_map/ppermute | solution.py:41
  64.7 3.7 %collective-permute-start.2 = (f32[4,418]{1,0:T(4,128)S(1)}, f32[4,418]{1,0:T(4,128)S(1)}, u32[]{:S(2)}, u32[]{:S(2)}) collective-permute-start(f32[4,418]{1,0:T(4,128)S(1)} %get-tuple-element.44), channel_id=1, source_target_pairs={{0,80},{16,96},{32,112},{48,0},{64,16},{80,32},{96,48},{112,64},{1... | collective-permute-start | bytes 20072 | tf_op jit(solution)/shard_map/ppermute | solution.py:41
  68.4 2.9 %collective-permute-done.2 = f32[4,418]{1,0:T(4,128)S(1)} collective-permute-done((f32[4,418]{1,0:T(4,128)S(1)}, f32[4,418]{1,0:T(4,128)S(1)}, u32[]{:S(2)}, u32[]{:S(2)}) %collective-permute-start.2) | collective-permute-done | bytes 6720 | tf_op jit(solution)/shard_map/ppermute | solution.py:41
  71.6 4.4 %collective-permute-start.7 = (f32[8,418]{1,0:T(8,128)S(1)}, f32[8,418]{1,0:T(8,128)S(1)}, u32[]{:S(2)}, u32[]{:S(2)}) collective-permute-start(f32[8,418]{1,0:T(8,128)S(1)} %bitcast.119), channel_id=1, source_target_pairs={{0,384},{128,0},{256,128},{384,256},{1,385},{129,1},{257,129},{385... | collective-permute-start | bytes 40136 | tf_op jit(solution)/shard_map/ppermute | solution.py:41
  88.3 32.7 %all-gather.2.cloned.1.call-done.refs_0_.refs_1_.refs_2_.refs_3_.refs_4_.refs_5_.refs_6_.refs_7_.refs_8_.refs_9_.refs_10_.refs_11_.refs_12_.refs_13_.refs_14_.refs_15_ = bf16[8192,512]{1,0:T(8,128)(2,1)} async-done(((bf16[256,512]{1,0:T(8,128)(2,1)}), bf16[8192,512]{1,0:T(8,128)(2,1)}) %all-gather.2.cloned.1.call-update) | async-done | bytes 8388624 | tf_op jit(solution)/shard_map/all_gather | solution.py:206
  121.0 12.2 %pick_rows.1 = (bf16[8,320,512]{2,1,0:T(8,128)(2,1)}, bf16[8,320,512]{2,1,0:T(8,128)(2,1)}) custom-call(s32[64]{0:T(128)} %copy-done.2, bf16[8192,512]{1,0:T(8,128)(2,1)} %all-gather.2.cloned.1.call-done.refs_0_.refs_1_.refs_2_.refs_3_.refs_4_.refs_5_.refs_6_.refs_7_.refs_8_.refs_9_.refs_10_.refs_11_.refs_12_.refs_13_.refs_14_.refs_15_, ...), custom_call_target="tpu_custom_call" | custom-call | tf_op jit(solution)/shard_map/partial/pick_rows/pallas_call | solution.py:128
  133.1 3.0 %collective-permute-start.10 = (bf16[8,320,512]{2,1,0:T(8,128)(2,1)}, bf16[8,320,512]{2,1,0:T(8,128)(2,1)S(1)}, u32[]{:S(2)}, u32[]{:S(2)}) collective-permute-start(bf16[8,320,512]{2,1,0:T(8,128)(2,1)} %get-tuple-element.20), channel_id=1, source_target_pairs={{0,1},{1,0},{2,3},{3,2},{4,5},{5,4},{6,7},{7,6},{8,9},{9,8},{10,11... | collective-permute-start | bytes 7864328 | tf_op jit(solution)/shard_map/partial/ppermute | solution.py:259
  137.1 9.8 %all-to-all-done.1.head_here_ref.head_away_ref = bf16[8,304,1024]{2,1,0:T(8,128)(2,1)} async-done(((bf16[8,304,1024]{2,1,0:T(8,128)(2,1)}), bf16[8,304,1024]{2,1,0:T(8,128)(2,1)}, u32[]{:S(2)}, u32[]{:S(2)}) %all-to-all-start.1) | async-done | bytes 4980768 | tf_op jit(solution)/shard_map/all_to_all | solution.py:28
  148.7 3.8 %partial_scores.2 = f32[3,760,128]{2,1,0:T(8,128)S(1)} custom-call(s32[4]{0:T(128)S(1)} %pad_add_fusion.order_ref, bf16[8,304,1024]{2,1,0:T(8,128)(2,1)} %all-to-all-done.1.head_here_ref.head_away_ref, bf16[8,304,1024]{2,1,0:T(8,128)(2,1)} %all-to-all-done.1.head_here_ref.head_away_ref, bf16[8,320,512]{2,1,0:T(8,128)(2,1)S(1)} %copy-done, ...), custom_call_target="tpu_custom_call" | custom-call | tf_op jit(solution)/shard_map/partial/partial_scores/pallas_call | solution.py:167
  154.6 5.1 %collective-permute-start.13 = (f16[760,128]{1,0:T(8,128)(2,1)S(1)}, f16[760,128]{1,0:T(8,128)(2,1)S(1)}, u32[]{:S(2)}, u32[]{:S(2)}) collective-permute-start(f16[760,128]{1,0:T(8,128)(2,1)S(1)} %get-tuple-element.30), channel_id=1, source_target_pairs={{0,10},{2,12},{4,14},{6,0},{8,2},{10,4},{12,6},{14,8},{1,11},{3,13... | collective-permute-start | bytes 583688 | tf_op jit(solution)/shard_map/ppermute | solution.py:276
  161.7 5.5 %partial_scores.3 = f32[5,760,128]{2,1,0:T(8,128)S(1)} custom-call(s32[6]{0:T(128)S(1)} %pad_add_fusion.1.order_ref, bf16[8,304,1024]{2,1,0:T(8,128)(2,1)} %all-to-all-done.1.head_here_ref.head_away_ref, bf16[8,304,1024]{2,1,0:T(8,128)(2,1)} %all-to-all-done.1.head_here_ref.head_away_ref, bf16[8,320,512]{2,1,0:T(8,128)(2,1)S(1)} %copy-done, ...), custom_call_target="tpu_custom_call" | custom-call | tf_op jit(solution)/shard_map/partial/partial_scores/pallas_call | solution.py:167
  167.5 5.2 %collective-permute-start.14 = (f16[760,128]{1,0:T(8,128)(2,1)S(1)}, f16[760,128]{1,0:T(8,128)(2,1)S(1)}, u32[]{:S(2)}, u32[]{:S(2)}) collective-permute-start(f16[760,128]{1,0:T(8,128)(2,1)S(1)} %get-tuple-element.25), channel_id=1, source_target_pairs={{0,4},{2,6},{4,8},{6,10},{8,12},{10,14},{12,0},{14,2},{1,5},{3,7},... | collective-permute-start | bytes 583688 | tf_op jit(solution)/shard_map/ppermute | solution.py:276
  172.7 3.4 %collective-permute-start.17 = (f16[760,128]{1,0:T(8,128)(2,1)S(1)}, f16[760,128]{1,0:T(8,128)(2,1)S(1)}, u32[]{:S(2)}, u32[]{:S(2)}) collective-permute-start(f16[760,128]{1,0:T(8,128)(2,1)S(1)} %get-tuple-element.26), channel_id=1, source_target_pairs={{0,14},{2,0},{4,2},{6,4},{8,6},{10,8},{12,10},{14,12},{1,15},{3,1}... | collective-permute-start | bytes 583688 | tf_op jit(solution)/shard_map/ppermute | solution.py:276
  178.1 3.3 %collective-permute-start.15 = (f16[760,128]{1,0:T(8,128)(2,1)S(1)}, f16[760,128]{1,0:T(8,128)(2,1)S(1)}, u32[]{:S(2)}, u32[]{:S(2)}) collective-permute-start(f16[760,128]{1,0:T(8,128)(2,1)S(1)} %get-tuple-element.28), channel_id=1, source_target_pairs={{0,12},{2,14},{4,0},{6,2},{8,4},{10,6},{12,8},{14,10},{1,13},{3,15... | collective-permute-start | bytes 583688 | tf_op jit(solution)/shard_map/ppermute | solution.py:276
  182.0 3.8 %collective-permute-done.14 = f16[760,128]{1,0:T(8,128)(2,1)S(1)} collective-permute-done((f16[760,128]{1,0:T(8,128)(2,1)S(1)}, f16[760,128]{1,0:T(8,128)(2,1)S(1)}, u32[]{:S(2)}, u32[]{:S(2)}) %collective-permute-start.14) | collective-permute-done | bytes 194592 | tf_op jit(solution)/shard_map/ppermute | solution.py:276
  185.8 5.4 %collective-permute-done.16 = f16[760,128]{1,0:T(8,128)(2,1)S(1)} collective-permute-done((f16[760,128]{1,0:T(8,128)(2,1)S(1)}, f16[760,128]{1,0:T(8,128)(2,1)S(1)}, u32[]{:S(2)}, u32[]{:S(2)}) %collective-permute-start.16) | collective-permute-done | bytes 194592 | tf_op jit(solution)/shard_map/ppermute | solution.py:276
  192.5 19.8 %all_to_all.24 = f32[32,1,30]{2,1,0:T(1,128)S(1)} all-to-all(f32[32,1,30]{2,1,0:T(1,128)S(1)} %copy.158), channel_id=1, replica_groups=mesh['x'=4,'z'=8,'y'=8,'core'=2] {'x','z'}, dimensions={0} | all-to-all | bytes 7680 | tf_op jit(solution)/shard_map/all_to_all | solution.py:28
  213.4 15.2 %all_to_all.25 = f32[16,3,128]{2,1,0:T(4,128)S(1)} all-to-all(f32[16,3,128]{2,1,0:T(4,128)S(1)} %broadcast_in_dim.146), channel_id=1, replica_groups=mesh['x'=4,'z'=8,'y'=8,'core'=2] {'core','y'}, dimensions={0} | all-to-all | bytes 49152 | tf_op jit(solution)/shard_map/all_to_all | solution.py:28
  (156 shorter events, 34.9 us)
Async XLA Ops:
  6.5 114.4 %all-gather.2.cloned.1.call-start = ((), (), s32[]{:S(2)}) async-start(), calls=%async_computation.4 | async-start | bytes 8650752 | tf_op jit(solution)/shard_map/all_gather | solution.py:206
  8.3 18.1 %all-to-all-start = ((f32[16,2,128]{2,1,0:T(2,128)}), f32[16,2,128]{2,1,0:T(2,128)S(1)}, u32[]{:S(2)}, u32[]{:S(2)}) async-start(f32[16,2,128]{2,1,0:T(2,128)} %get-tuple-element.13), calls=%async_computation | async-start | bytes 32768 | tf_op jit(solution)/shard_map/all_to_all | solution.py:28
  26.4 120.5 %all-to-all-start.1 = ((bf16[8,304,1024]{2,1,0:T(8,128)(2,1)}), bf16[8,304,1024]{2,1,0:T(8,128)(2,1)}, u32[]{:S(2)}, u32[]{:S(2)}) async-start(bf16[8,304,1024]{2,1,0:T(8,128)(2,1)} %split_head.1), calls=%async_computation.1 | async-start | bytes 9961472 | tf_op jit(solution)/shard_map/all_to_all | solution.py:28
  35.9 22.5 %collective-permute-start = (f32[4,418]{1,0:T(4,128)S(1)}, f32[4,418]{1,0:T(4,128)S(1)}, u32[]{:S(2)}, u32[]{:S(2)}) collective-permute-start(f32[4,418]{1,0:T(4,128)S(1)} %get-tuple-element.46), channel_id=1, source_target_pairs={{0,112},{16,0},{32,16},{48,32},{64,48},{80,64},{96,80},{112,96},{1... | collective-permute-start | bytes 20072 | tf_op jit(solution)/shard_map/ppermute | solution.py:41
  45.1 26.2 %collective-permute-start.6 = (f32[4,418]{1,0:T(4,128)S(1)}, f32[4,418]{1,0:T(4,128)S(1)}, u32[]{:S(2)}, u32[]{:S(2)}) collective-permute-start(f32[4,418]{1,0:T(4,128)S(1)} %get-tuple-element.40), channel_id=1, source_target_pairs={{0,16},{16,32},{32,48},{48,64},{64,80},{80,96},{96,112},{112,0},{1... | collective-permute-start | bytes 20072 | tf_op jit(solution)/shard_map/ppermute | solution.py:41
  47.0 24.3 %collective-permute-start.5 = (f32[4,418]{1,0:T(4,128)S(1)}, f32[4,418]{1,0:T(4,128)S(1)}, u32[]{:S(2)}, u32[]{:S(2)}) collective-permute-start(f32[4,418]{1,0:T(4,128)S(1)} %get-tuple-element.41), channel_id=1, source_target_pairs={{0,32},{16,48},{32,64},{48,80},{64,96},{80,112},{96,0},{112,16},{1... | collective-permute-start | bytes 20072 | tf_op jit(solution)/shard_map/ppermute | solution.py:41
  48.9 22.3 %collective-permute-start.4 = (f32[4,418]{1,0:T(4,128)S(1)}, f32[4,418]{1,0:T(4,128)S(1)}, u32[]{:S(2)}, u32[]{:S(2)}) collective-permute-start(f32[4,418]{1,0:T(4,128)S(1)} %get-tuple-element.42), channel_id=1, source_target_pairs={{0,48},{16,64},{32,80},{48,96},{64,112},{80,0},{96,16},{112,32},{1... | collective-permute-start | bytes 20072 | tf_op jit(solution)/shard_map/ppermute | solution.py:41
  53.4 17.8 %collective-permute-start.3 = (f32[4,418]{1,0:T(4,128)S(1)}, f32[4,418]{1,0:T(4,128)S(1)}, u32[]{:S(2)}, u32[]{:S(2)}) collective-permute-start(f32[4,418]{1,0:T(4,128)S(1)} %get-tuple-element.43), channel_id=1, source_target_pairs={{0,64},{16,80},{32,96},{48,112},{64,0},{80,16},{96,32},{112,48},{1... | collective-permute-start | bytes 20072 | tf_op jit(solution)/shard_map/ppermute | solution.py:41
  58.4 6.3 %collective-permute-start.1 = (f32[4,418]{1,0:T(4,128)S(1)}, f32[4,418]{1,0:T(4,128)S(1)}, u32[]{:S(2)}, u32[]{:S(2)}) collective-permute-start(f32[4,418]{1,0:T(4,128)S(1)} %get-tuple-element.45), channel_id=1, source_target_pairs={{0,96},{16,112},{32,0},{48,16},{64,32},{80,48},{96,64},{112,80},{1... | collective-permute-start | bytes 20072 | tf_op jit(solution)/shard_map/ppermute | solution.py:41
  64.7 6.6 %collective-permute-start.2 = (f32[4,418]{1,0:T(4,128)S(1)}, f32[4,418]{1,0:T(4,128)S(1)}, u32[]{:S(2)}, u32[]{:S(2)}) collective-permute-start(f32[4,418]{1,0:T(4,128)S(1)} %get-tuple-element.44), channel_id=1, source_target_pairs={{0,80},{16,96},{32,112},{48,0},{64,16},{80,32},{96,48},{112,64},{1... | collective-permute-start | bytes 20072 | tf_op jit(solution)/shard_map/ppermute | solution.py:41
  71.6 10.7 %collective-permute-start.7 = (f32[8,418]{1,0:T(8,128)S(1)}, f32[8,418]{1,0:T(8,128)S(1)}, u32[]{:S(2)}, u32[]{:S(2)}) collective-permute-start(f32[8,418]{1,0:T(8,128)S(1)} %bitcast.119), channel_id=1, source_target_pairs={{0,384},{128,0},{256,128},{384,256},{1,385},{129,1},{257,129},{385... | collective-permute-start | bytes 40136 | tf_op jit(solution)/shard_map/ppermute | solution.py:41
  76.0 6.7 %collective-permute-start.8 = (f32[8,418]{1,0:T(8,128)S(1)}, f32[8,418]{1,0:T(8,128)S(1)}, u32[]{:S(2)}, u32[]{:S(2)}) collective-permute-start(f32[8,418]{1,0:T(8,128)S(1)} %bitcast.118), channel_id=1, source_target_pairs={{0,256},{128,384},{256,0},{384,128},{1,257},{129,385},{257,1},{385... | collective-permute-start | bytes 40136 | tf_op jit(solution)/shard_map/ppermute | solution.py:41
  78.4 6.4 %collective-permute-start.9 = (f32[8,418]{1,0:T(8,128)S(1)}, f32[8,418]{1,0:T(8,128)S(1)}, u32[]{:S(2)}, u32[]{:S(2)}) collective-permute-start(f32[8,418]{1,0:T(8,128)S(1)} %bitcast.117), channel_id=1, source_target_pairs={{0,128},{128,256},{256,384},{384,0},{1,129},{129,257},{257,385},{3... | collective-permute-start | bytes 40136 | tf_op jit(solution)/shard_map/ppermute | solution.py:41
  85.4 35.5 %copy-start.2 = (s32[64]{0:T(128)}, s32[64]{0:T(128)S(1)}, u32[]{:S(2)}) copy-start(s32[64]{0:T(128)S(1)} %reshape.256.unit_ref) | copy-start | bytes 772
  121.0 15.2 %copy-start.5 = (s32[5]{0:T(128)S(1)}, s32[5]{0:T(128)}, u32[]{:S(2)}) copy-start(s32[5]{0:T(128)} %constant.196.clone) | copy-start | bytes 64
  121.0 15.3 %copy-start.4 = (s32[3]{0:T(128)S(1)}, s32[3]{0:T(128)}, u32[]{:S(2)}) copy-start(s32[3]{0:T(128)} %constant.195.clone) | copy-start | bytes 40
  133.1 13.8 %collective-permute-start.10 = (bf16[8,320,512]{2,1,0:T(8,128)(2,1)}, bf16[8,320,512]{2,1,0:T(8,128)(2,1)S(1)}, u32[]{:S(2)}, u32[]{:S(2)}) collective-permute-start(bf16[8,320,512]{2,1,0:T(8,128)(2,1)} %get-tuple-element.20), channel_id=1, source_target_pairs={{0,1},{1,0},{2,3},{3,2},{4,5},{5,4},{6,7},{7,6},{8,9},{9,8},{10,11... | collective-permute-start | bytes 7864328 | tf_op jit(solution)/shard_map/partial/ppermute | solution.py:259
  152.7 23.4 %collective-permute-start.11 = (f16[760,128]{1,0:T(8,128)(2,1)S(1)}, f16[760,128]{1,0:T(8,128)(2,1)S(1)}, u32[]{:S(2)}, u32[]{:S(2)}) collective-permute-start(f16[760,128]{1,0:T(8,128)(2,1)S(1)} %get-tuple-element.29), channel_id=1, source_target_pairs={{0,8},{2,10},{4,12},{6,14},{8,0},{10,2},{12,4},{14,6},{1,9},{3,11}... | collective-permute-start | bytes 583688 | tf_op jit(solution)/shard_map/ppermute | solution.py:276
  154.6 23.4 %collective-permute-start.13 = (f16[760,128]{1,0:T(8,128)(2,1)S(1)}, f16[760,128]{1,0:T(8,128)(2,1)S(1)}, u32[]{:S(2)}, u32[]{:S(2)}) collective-permute-start(f16[760,128]{1,0:T(8,128)(2,1)S(1)} %get-tuple-element.30), channel_id=1, source_target_pairs={{0,10},{2,12},{4,14},{6,0},{8,2},{10,4},{12,6},{14,8},{1,11},{3,13... | collective-permute-start | bytes 583688 | tf_op jit(solution)/shard_map/ppermute | solution.py:276
  159.8 22.3 %collective-permute-start.12 = (f16[760,128]{1,0:T(8,128)(2,1)S(1)}, f16[760,128]{1,0:T(8,128)(2,1)S(1)}, u32[]{:S(2)}, u32[]{:S(2)}) collective-permute-start(f16[760,128]{1,0:T(8,128)(2,1)S(1)} %get-tuple-element.31), channel_id=1, source_target_pairs={{0,6},{2,8},{4,10},{6,12},{8,14},{10,0},{12,2},{14,4},{1,7},{3,9},... | collective-permute-start | bytes 583688 | tf_op jit(solution)/shard_map/ppermute | solution.py:276
  167.5 18.3 %collective-permute-start.14 = (f16[760,128]{1,0:T(8,128)(2,1)S(1)}, f16[760,128]{1,0:T(8,128)(2,1)S(1)}, u32[]{:S(2)}, u32[]{:S(2)}) collective-permute-start(f16[760,128]{1,0:T(8,128)(2,1)S(1)} %get-tuple-element.25), channel_id=1, source_target_pairs={{0,4},{2,6},{4,8},{6,10},{8,12},{10,14},{12,0},{14,2},{1,5},{3,7},... | collective-permute-start | bytes 583688 | tf_op jit(solution)/shard_map/ppermute | solution.py:276
  172.7 13.2 %collective-permute-start.17 = (f16[760,128]{1,0:T(8,128)(2,1)S(1)}, f16[760,128]{1,0:T(8,128)(2,1)S(1)}, u32[]{:S(2)}, u32[]{:S(2)}) collective-permute-start(f16[760,128]{1,0:T(8,128)(2,1)S(1)} %get-tuple-element.26), channel_id=1, source_target_pairs={{0,14},{2,0},{4,2},{6,4},{8,6},{10,8},{12,10},{14,12},{1,15},{3,1}... | collective-permute-start | bytes 583688 | tf_op jit(solution)/shard_map/ppermute | solution.py:276
  176.1 15.1 %collective-permute-start.16 = (f16[760,128]{1,0:T(8,128)(2,1)S(1)}, f16[760,128]{1,0:T(8,128)(2,1)S(1)}, u32[]{:S(2)}, u32[]{:S(2)}) collective-permute-start(f16[760,128]{1,0:T(8,128)(2,1)S(1)} %get-tuple-element.27), channel_id=1, source_target_pairs={{0,2},{2,4},{4,6},{6,8},{8,10},{10,12},{12,14},{14,0},{1,3},{3,5},... | collective-permute-start | bytes 583688 | tf_op jit(solution)/shard_map/ppermute | solution.py:276
  178.1 13.1 %collective-permute-start.15 = (f16[760,128]{1,0:T(8,128)(2,1)S(1)}, f16[760,128]{1,0:T(8,128)(2,1)S(1)}, u32[]{:S(2)}, u32[]{:S(2)}) collective-permute-start(f16[760,128]{1,0:T(8,128)(2,1)S(1)} %get-tuple-element.28), channel_id=1, source_target_pairs={{0,12},{2,14},{4,0},{6,2},{8,4},{10,6},{12,8},{14,10},{1,13},{3,15... | collective-permute-start | bytes 583688 | tf_op jit(solution)/shard_map/ppermute | solution.py:276
  (3 other events, 15.3 us)
Sparse Core Ops, SparseCore 0:
  10.5 110.3 all-gather.1

commit v5 on v4

--- a/solution.py
+++ b/solution.py
@@ -13,7 +13,7 @@
 CAP = 10
 GROUP = 8
 TALL = 760
-STEPS = ((4, 3, 5), (2, 6, 1, 7, 0))
+STEPS = ((4,), (3, 5), (2, 6, 1, 7, 0))
 VMEM = 60 * 2**20
 
 sharpness_divisor = 0.7
@@ -71,8 +71,8 @@
     whole = VP - 16
     out_ref[0, :whole] = head_ref[:whole]
     last = head_ref[whole:].astype(jnp.float32)
-    rows = lax.broadcasted_iota(jnp.int32, last.shape, 0) + whole
-    out_ref[0, whole:] = jnp.where(rows < VB, last, 0.0).astype(jnp.bfloat16)
+    blank = jnp.zeros((VP - VB, last.shape[1]), jnp.float32)
+    out_ref[0, whole:] = jnp.concatenate([last, blank], axis=0).astype(jnp.bfloat16)
 
 
 def split_head(head, chips):
@@ -80,7 +80,7 @@
     return pl.pallas_call(
         split_kernel,
         grid=(chips,),
-        in_specs=[pl.BlockSpec((VP, part), lambda i: (0, i))],
+        in_specs=[pl.BlockSpec((VB, part), lambda i: (0, i))],
         out_specs=pl.BlockSpec((1, VP, part), lambda i: (i, 0, 0)),
         out_shape=jax.ShapeDtypeStruct((chips, VP, part), jnp.bfloat16),
         compiler_params=pltpu.CompilerParams(vmem_limit_bytes=VMEM),
@@ -143,7 +143,7 @@
             ],
         ),
         out_shape=[jax.ShapeDtypeStruct((chips, groups * each, width), jnp.bfloat16)] * 2,
-        compiler_params=pltpu.CompilerParams(vmem_limit_bytes=56 * 2**20),
+        compiler_params=pltpu.CompilerParams(vmem_limit_bytes=32 * 2**20),
         name="pick_rows",
     )(unit, *([everyone] * units), scale, gain, token_of)
 

time: 237 us -> 238 us (level)
    pallas_call x1, Pallas kernels: 12.2 us -> 9.64 us  [pick_rows(): pl.pallas_call(rows_kernel, grid_spec=pltpu.PrefetchScalarGridSpec(num_sc...]
    pallas_call x2 -> x3, Pallas kernels: 9.29 us -> 10.9 us  [partial_scores(): pl.pallas_call(partial_kernel, grid_spec=pltpu.PrefetchScalarGridSpec(num...]
  transfers between devices with their start and end apart: 21 -> 21, of which waited for: 9 -> 9; matrix products, arithmetic and copies ran while one was open for 4% -> 3% of each run, Pallas kernels for 10% -> 11%
where the time goes in v5:
time: 238 us; the launch traced here: 236 us
  starting transfers between devices  83.8 us (35%)
  waiting for transfers between devices  58 us (24%)
  blocking collectives  36.6 us (15%)
  Pallas kernels  29.3 us (12%)
  between operations  14.1 us (6%)
  local copies, waits for them, and re-layouts  9.4 us (4%)
  other arithmetic  4.94 us (2%)
    ppermute x10, starting transfers between devices, by_steps(): lax.ppermute(turned[step], axis, [(i, (i + step) % count) for i in range(...  40.9 us
    all_to_all x2, blocking collectives, exchange(): return lax.all_to_all(value, axis, split_axis=0, concat_axis=0, tiled=True)  36.6 us
    all_gather x1, waiting for transfers between devices, per_device(): everyone = lax.all_gather(both, SEQ, axis=0, tiled=True)  33.9 us
    ppermute x7, starting transfers between devices, per_device(): lax.ppermute(sent_part, 'y', [(k, (k + step) % 8) for k in range(8)])  23 us
    all_to_all x2, starting transfers between devices, exchange(): return lax.all_to_all(value, axis, split_axis=0, concat_axis=0, tiled=True)  16.9 us
    pallas_call x3, Pallas kernels, partial_scores(): pl.pallas_call(partial_kernel, grid_spec=pltpu.PrefetchScalarGridSpec(num...  10.9 us
    pallas_call x1, Pallas kernels, pick_rows(): pl.pallas_call(rows_kernel, grid_spec=pltpu.PrefetchScalarGridSpec(num_sc...  9.64 us
    all_to_all x2, waiting for transfers between devices, exchange(): return lax.all_to_all(value, axis, split_axis=0, concat_axis=0, tiled=True)  8.88 us
  transfers between devices with their start and end apart: 21, of which 9 were waited for; matrix products, arithmetic and copies ran while one was open for 3% of the time, Pallas kernels for 11%

profile of v5, /device:TPU:1, one launch (start us, length us, event | category | flops | bytes accessed | tf_op | source)
XLA Modules:
  0.0 236.5 jit_solution(14814288570180732984)
XLA Ops:
  8.3 10.1 %all-to-all-start = ((f32[16,2,128]{2,1,0:T(2,128)}), f32[16,2,128]{2,1,0:T(2,128)S(1)}, u32[]{:S(2)}, u32[]{:S(2)}) async-start(f32[16,2,128]{2,1,0:T(2,128)} %get-tuple-element.13), calls=%async_computation | async-start | bytes 32768 | tf_op jit(solution)/shard_map/all_to_all | solution.py:28
  19.3 7.1 %split_head.1 = bf16[8,304,1024]{2,1,0:T(8,128)(2,1)} custom-call(bf16[297,8192]{1,0:T(8,128)(2,1)} %head_ref.1), custom_call_target="tpu_custom_call" | custom-call | tf_op jit(solution)/shard_map/split_head/pallas_call | solution.py:80
  26.4 6.7 %all-to-all-start.1 = ((bf16[8,304,1024]{2,1,0:T(8,128)(2,1)}), bf16[8,304,1024]{2,1,0:T(8,128)(2,1)}, u32[]{:S(2)}, u32[]{:S(2)}) async-start(bf16[8,304,1024]{2,1,0:T(8,128)(2,1)} %split_head.1), calls=%async_computation.1 | async-start | bytes 9961472 | tf_op jit(solution)/shard_map/all_to_all | solution.py:28
  35.9 9.2 %collective-permute-start = (f32[4,418]{1,0:T(4,128)S(1)}, f32[4,418]{1,0:T(4,128)S(1)}, u32[]{:S(2)}, u32[]{:S(2)}) collective-permute-start(f32[4,418]{1,0:T(4,128)S(1)} %get-tuple-element.45), channel_id=1, source_target_pairs={{0,112},{16,0},{32,16},{48,32},{64,48},{80,64},{96,80},{112,96},{1... | collective-permute-start | bytes 20072 | tf_op jit(solution)/shard_map/ppermute | solution.py:41
  48.9 4.5 %collective-permute-start.4 = (f32[4,418]{1,0:T(4,128)S(1)}, f32[4,418]{1,0:T(4,128)S(1)}, u32[]{:S(2)}, u32[]{:S(2)}) collective-permute-start(f32[4,418]{1,0:T(4,128)S(1)} %get-tuple-element.41), channel_id=1, source_target_pairs={{0,48},{16,64},{32,80},{48,96},{64,112},{80,0},{96,16},{112,32},{1... | collective-permute-start | bytes 20072 | tf_op jit(solution)/shard_map/ppermute | solution.py:41
  53.4 5.0 %collective-permute-start.3 = (f32[4,418]{1,0:T(4,128)S(1)}, f32[4,418]{1,0:T(4,128)S(1)}, u32[]{:S(2)}, u32[]{:S(2)}) collective-permute-start(f32[4,418]{1,0:T(4,128)S(1)} %get-tuple-element.42), channel_id=1, source_target_pairs={{0,64},{16,80},{32,96},{48,112},{64,0},{80,16},{96,32},{112,48},{1... | collective-permute-start | bytes 20072 | tf_op jit(solution)/shard_map/ppermute | solution.py:41
  58.4 5.5 %collective-permute-start.1 = (f32[4,418]{1,0:T(4,128)S(1)}, f32[4,418]{1,0:T(4,128)S(1)}, u32[]{:S(2)}, u32[]{:S(2)}) collective-permute-start(f32[4,418]{1,0:T(4,128)S(1)} %get-tuple-element.44), channel_id=1, source_target_pairs={{0,96},{16,112},{32,0},{48,16},{64,32},{80,48},{96,64},{112,80},{1... | collective-permute-start | bytes 20072 | tf_op jit(solution)/shard_map/ppermute | solution.py:41
  64.7 3.7 %collective-permute-start.2 = (f32[4,418]{1,0:T(4,128)S(1)}, f32[4,418]{1,0:T(4,128)S(1)}, u32[]{:S(2)}, u32[]{:S(2)}) collective-permute-start(f32[4,418]{1,0:T(4,128)S(1)} %get-tuple-element.43), channel_id=1, source_target_pairs={{0,80},{16,96},{32,112},{48,0},{64,16},{80,32},{96,48},{112,64},{1... | collective-permute-start | bytes 20072 | tf_op jit(solution)/shard_map/ppermute | solution.py:41
  68.4 2.9 %collective-permute-done.2 = f32[4,418]{1,0:T(4,128)S(1)} collective-permute-done((f32[4,418]{1,0:T(4,128)S(1)}, f32[4,418]{1,0:T(4,128)S(1)}, u32[]{:S(2)}, u32[]{:S(2)}) %collective-permute-start.2) | collective-permute-done | bytes 6720 | tf_op jit(solution)/shard_map/ppermute | solution.py:41
  71.6 4.4 %collective-permute-start.7 = (f32[8,418]{1,0:T(8,128)S(1)}, f32[8,418]{1,0:T(8,128)S(1)}, u32[]{:S(2)}, u32[]{:S(2)}) collective-permute-start(f32[8,418]{1,0:T(8,128)S(1)} %bitcast.121), channel_id=1, source_target_pairs={{0,384},{128,0},{256,128},{384,256},{1,385},{129,1},{257,129},{385... | collective-permute-start | bytes 40136 | tf_op jit(solution)/shard_map/ppermute | solution.py:41
  87.1 33.9 %all-gather.2.cloned.1.call-done.refs_0_.refs_1_.refs_2_.refs_3_.refs_4_.refs_5_.refs_6_.refs_7_.refs_8_.refs_9_.refs_10_.refs_11_.refs_12_.refs_13_.refs_14_.refs_15_ = bf16[8192,512]{1,0:T(8,128)(2,1)} async-done(((bf16[256,512]{1,0:T(8,128)(2,1)}), bf16[8192,512]{1,0:T(8,128)(2,1)}) %all-gather.2.cloned.1.call-update) | async-done | bytes 8388624 | tf_op jit(solution)/shard_map/all_gather | solution.py:206
  121.0 3.4 %copy-done = bf16[8192,512]{1,0:T(8,128)(2,1)S(1)} copy-done((bf16[8192,512]{1,0:T(8,128)(2,1)S(1)}, bf16[8192,512]{1,0:T(8,128)(2,1)}, u32[]{:S(2)}) %copy-start) | copy-done | bytes 8388632
  124.4 9.6 %pick_rows.1 = (bf16[8,320,512]{2,1,0:T(8,128)(2,1)}, bf16[8,320,512]{2,1,0:T(8,128)(2,1)S(1)}) custom-call(s32[64]{0:T(128)S(1)} %reshape.260.unit_ref, bf16[8192,512]{1,0:T(8,128)(2,1)S(1)} %copy-done, bf16[8192,512]{1,0:T(8,128)(2,1)S(1)} %copy-done, bf16[8192,512]{1,0:T(8,128)(2,1)S(1)} %copy-done, bf16[8192,512]{1,0:T(8,128)(2,1)S(1)} %copy-done, ...), custom_call_target="tpu_custom_call" | custom-call | tf_op jit(solution)/shard_map/partial/pick_rows/pallas_call | solution.py:128
  134.0 3.0 %collective-permute-start.10 = (bf16[8,320,512]{2,1,0:T(8,128)(2,1)}, bf16[8,320,512]{2,1,0:T(8,128)(2,1)}, u32[]{:S(2)}, u32[]{:S(2)}) collective-permute-start(bf16[8,320,512]{2,1,0:T(8,128)(2,1)} %get-tuple-element.20), channel_id=1, source_target_pairs={{0,1},{1,0},{2,3},{3,2},{4,5},{5,4},{6,7},{7,6},{8,9},{9,8},{10,11... | collective-permute-start | bytes 7864328 | tf_op jit(solution)/shard_map/partial/ppermute | solution.py:259
  138.0 8.9 %all-to-all-done.1.head_here_ref.head_away_ref = bf16[8,304,1024]{2,1,0:T(8,128)(2,1)} async-done(((bf16[8,304,1024]{2,1,0:T(8,128)(2,1)}), bf16[8,304,1024]{2,1,0:T(8,128)(2,1)}, u32[]{:S(2)}, u32[]{:S(2)}) %all-to-all-start.1) | async-done | bytes 4980768 | tf_op jit(solution)/shard_map/all_to_all | solution.py:28
  151.3 2.9 %partial_scores.4 = f32[2,760,128]{2,1,0:T(8,128)S(1)} custom-call(s32[3]{0:T(128)S(1)} %pad_add_fusion.1.order_ref, bf16[8,304,1024]{2,1,0:T(8,128)(2,1)} %all-to-all-done.1.head_here_ref.head_away_ref, bf16[8,304,1024]{2,1,0:T(8,128)(2,1)} %all-to-all-done.1.head_here_ref.head_away_ref, bf16[8,320,512]{2,1,0:T(8,128)(2,1)S(1)} %get-tuple-element.19.here_ref, ...), custom_call_target="tpu_custom_call" | custom-call | tf_op jit(solution)/shard_map/partial/partial_scores/pallas_call | solution.py:167
  156.6 6.0 %collective-permute-start.13 = (f16[760,128]{1,0:T(8,128)(2,1)S(1)}, f16[760,128]{1,0:T(8,128)(2,1)S(1)}, u32[]{:S(2)}, u32[]{:S(2)}) collective-permute-start(f16[760,128]{1,0:T(8,128)(2,1)S(1)} %get-tuple-element.34), channel_id=1, source_target_pairs={{0,10},{2,12},{4,14},{6,0},{8,2},{10,4},{12,6},{14,8},{1,11},{3,13... | collective-permute-start | bytes 583688 | tf_op jit(solution)/shard_map/ppermute | solution.py:276
  162.6 5.8 %partial_scores.5 = f32[5,760,128]{2,1,0:T(8,128)S(1)} custom-call(s32[6]{0:T(128)S(1)} %pad_add_fusion.2.order_ref, bf16[8,304,1024]{2,1,0:T(8,128)(2,1)} %all-to-all-done.1.head_here_ref.head_away_ref, bf16[8,304,1024]{2,1,0:T(8,128)(2,1)} %all-to-all-done.1.head_here_ref.head_away_ref, bf16[8,320,512]{2,1,0:T(8,128)(2,1)S(1)} %get-tuple-element.19.here_ref, ...), custom_call_target="tpu_custom_call" | custom-call | tf_op jit(solution)/shard_map/partial/partial_scores/pallas_call | solution.py:167
  168.7 3.8 %collective-permute-start.14 = (f16[760,128]{1,0:T(8,128)(2,1)S(1)}, f16[760,128]{1,0:T(8,128)(2,1)S(1)}, u32[]{:S(2)}, u32[]{:S(2)}) collective-permute-start(f16[760,128]{1,0:T(8,128)(2,1)S(1)} %get-tuple-element.25), channel_id=1, source_target_pairs={{0,4},{2,6},{4,8},{6,10},{8,12},{10,14},{12,0},{14,2},{1,5},{3,7},... | collective-permute-start | bytes 583688 | tf_op jit(solution)/shard_map/ppermute | solution.py:276
  172.6 3.4 %collective-permute-start.17 = (f16[760,128]{1,0:T(8,128)(2,1)S(1)}, f16[760,128]{1,0:T(8,128)(2,1)S(1)}, u32[]{:S(2)}, u32[]{:S(2)}) collective-permute-start(f16[760,128]{1,0:T(8,128)(2,1)S(1)} %get-tuple-element.26), channel_id=1, source_target_pairs={{0,14},{2,0},{4,2},{6,4},{8,6},{10,8},{12,10},{14,12},{1,15},{3,1}... | collective-permute-start | bytes 583688 | tf_op jit(solution)/shard_map/ppermute | solution.py:276
  177.9 3.5 %collective-permute-start.15 = (f16[760,128]{1,0:T(8,128)(2,1)S(1)}, f16[760,128]{1,0:T(8,128)(2,1)S(1)}, u32[]{:S(2)}, u32[]{:S(2)}) collective-permute-start(f16[760,128]{1,0:T(8,128)(2,1)S(1)} %get-tuple-element.28), channel_id=1, source_target_pairs={{0,12},{2,14},{4,0},{6,2},{8,4},{10,6},{12,8},{14,10},{1,13},{3,15... | collective-permute-start | bytes 583688 | tf_op jit(solution)/shard_map/ppermute | solution.py:276
  183.6 5.4 %collective-permute-done.16 = f16[760,128]{1,0:T(8,128)(2,1)S(1)} collective-permute-done((f16[760,128]{1,0:T(8,128)(2,1)S(1)}, f16[760,128]{1,0:T(8,128)(2,1)S(1)}, u32[]{:S(2)}, u32[]{:S(2)}) %collective-permute-start.16) | collective-permute-done | bytes 194592 | tf_op jit(solution)/shard_map/ppermute | solution.py:276
  191.3 19.7 %all_to_all.24 = f32[32,1,30]{2,1,0:T(1,128)S(1)} all-to-all(f32[32,1,30]{2,1,0:T(1,128)S(1)} %copy.159), channel_id=1, replica_groups=mesh['x'=4,'z'=8,'y'=8,'core'=2] {'x','z'}, dimensions={0} | all-to-all | bytes 7680 | tf_op jit(solution)/shard_map/all_to_all | solution.py:28
  212.1 16.9 %all_to_all.25 = f32[16,3,128]{2,1,0:T(4,128)S(1)} all-to-all(f32[16,3,128]{2,1,0:T(4,128)S(1)} %broadcast_in_dim.146), channel_id=1, replica_groups=mesh['x'=4,'z'=8,'y'=8,'core'=2] {'core','y'}, dimensions={0} | all-to-all | bytes 49152 | tf_op jit(solution)/shard_map/all_to_all | solution.py:28
  (156 shorter events, 37.1 us)
Async XLA Ops:
  6.5 114.4 %all-gather.2.cloned.1.call-start = ((), (), s32[]{:S(2)}) async-start(), calls=%async_computation.4 | async-start | bytes 8650752 | tf_op jit(solution)/shard_map/all_gather | solution.py:206
  8.3 18.1 %all-to-all-start = ((f32[16,2,128]{2,1,0:T(2,128)}), f32[16,2,128]{2,1,0:T(2,128)S(1)}, u32[]{:S(2)}, u32[]{:S(2)}) async-start(f32[16,2,128]{2,1,0:T(2,128)} %get-tuple-element.13), calls=%async_computation | async-start | bytes 32768 | tf_op jit(solution)/shard_map/all_to_all | solution.py:28
  26.4 6.8 %copy-start.3 = (s32[128]{0:T(128)S(1)}, s32[128]{0:T(128)}, u32[]{:S(2)}) copy-start(s32[128]{0:T(128)} %param.17) | copy-start | bytes 1540
  26.4 120.5 %all-to-all-start.1 = ((bf16[8,304,1024]{2,1,0:T(8,128)(2,1)}), bf16[8,304,1024]{2,1,0:T(8,128)(2,1)}, u32[]{:S(2)}, u32[]{:S(2)}) async-start(bf16[8,304,1024]{2,1,0:T(8,128)(2,1)} %split_head.1), calls=%async_computation.1 | async-start | bytes 9961472 | tf_op jit(solution)/shard_map/all_to_all | solution.py:28
  35.9 22.5 %collective-permute-start = (f32[4,418]{1,0:T(4,128)S(1)}, f32[4,418]{1,0:T(4,128)S(1)}, u32[]{:S(2)}, u32[]{:S(2)}) collective-permute-start(f32[4,418]{1,0:T(4,128)S(1)} %get-tuple-element.45), channel_id=1, source_target_pairs={{0,112},{16,0},{32,16},{48,32},{64,48},{80,64},{96,80},{112,96},{1... | collective-permute-start | bytes 20072 | tf_op jit(solution)/shard_map/ppermute | solution.py:41
  45.1 26.2 %collective-permute-start.6 = (f32[4,418]{1,0:T(4,128)S(1)}, f32[4,418]{1,0:T(4,128)S(1)}, u32[]{:S(2)}, u32[]{:S(2)}) collective-permute-start(f32[4,418]{1,0:T(4,128)S(1)} %get-tuple-element.39), channel_id=1, source_target_pairs={{0,16},{16,32},{32,48},{48,64},{64,80},{80,96},{96,112},{112,0},{1... | collective-permute-start | bytes 20072 | tf_op jit(solution)/shard_map/ppermute | solution.py:41
  47.0 24.3 %collective-permute-start.5 = (f32[4,418]{1,0:T(4,128)S(1)}, f32[4,418]{1,0:T(4,128)S(1)}, u32[]{:S(2)}, u32[]{:S(2)}) collective-permute-start(f32[4,418]{1,0:T(4,128)S(1)} %get-tuple-element.40), channel_id=1, source_target_pairs={{0,32},{16,48},{32,64},{48,80},{64,96},{80,112},{96,0},{112,16},{1... | collective-permute-start | bytes 20072 | tf_op jit(solution)/shard_map/ppermute | solution.py:41
  48.9 22.3 %collective-permute-start.4 = (f32[4,418]{1,0:T(4,128)S(1)}, f32[4,418]{1,0:T(4,128)S(1)}, u32[]{:S(2)}, u32[]{:S(2)}) collective-permute-start(f32[4,418]{1,0:T(4,128)S(1)} %get-tuple-element.41), channel_id=1, source_target_pairs={{0,48},{16,64},{32,80},{48,96},{64,112},{80,0},{96,16},{112,32},{1... | collective-permute-start | bytes 20072 | tf_op jit(solution)/shard_map/ppermute | solution.py:41
  53.4 17.8 %collective-permute-start.3 = (f32[4,418]{1,0:T(4,128)S(1)}, f32[4,418]{1,0:T(4,128)S(1)}, u32[]{:S(2)}, u32[]{:S(2)}) collective-permute-start(f32[4,418]{1,0:T(4,128)S(1)} %get-tuple-element.42), channel_id=1, source_target_pairs={{0,64},{16,80},{32,96},{48,112},{64,0},{80,16},{96,32},{112,48},{1... | collective-permute-start | bytes 20072 | tf_op jit(solution)/shard_map/ppermute | solution.py:41
  58.4 6.3 %collective-permute-start.1 = (f32[4,418]{1,0:T(4,128)S(1)}, f32[4,418]{1,0:T(4,128)S(1)}, u32[]{:S(2)}, u32[]{:S(2)}) collective-permute-start(f32[4,418]{1,0:T(4,128)S(1)} %get-tuple-element.44), channel_id=1, source_target_pairs={{0,96},{16,112},{32,0},{48,16},{64,32},{80,48},{96,64},{112,80},{1... | collective-permute-start | bytes 20072 | tf_op jit(solution)/shard_map/ppermute | solution.py:41
  64.7 6.6 %collective-permute-start.2 = (f32[4,418]{1,0:T(4,128)S(1)}, f32[4,418]{1,0:T(4,128)S(1)}, u32[]{:S(2)}, u32[]{:S(2)}) collective-permute-start(f32[4,418]{1,0:T(4,128)S(1)} %get-tuple-element.43), channel_id=1, source_target_pairs={{0,80},{16,96},{32,112},{48,0},{64,16},{80,32},{96,48},{112,64},{1... | collective-permute-start | bytes 20072 | tf_op jit(solution)/shard_map/ppermute | solution.py:41
  71.6 10.1 %collective-permute-start.7 = (f32[8,418]{1,0:T(8,128)S(1)}, f32[8,418]{1,0:T(8,128)S(1)}, u32[]{:S(2)}, u32[]{:S(2)}) collective-permute-start(f32[8,418]{1,0:T(8,128)S(1)} %bitcast.121), channel_id=1, source_target_pairs={{0,384},{128,0},{256,128},{384,256},{1,385},{129,1},{257,129},{385... | collective-permute-start | bytes 40136 | tf_op jit(solution)/shard_map/ppermute | solution.py:41
  76.0 6.7 %collective-permute-start.8 = (f32[8,418]{1,0:T(8,128)S(1)}, f32[8,418]{1,0:T(8,128)S(1)}, u32[]{:S(2)}, u32[]{:S(2)}) collective-permute-start(f32[8,418]{1,0:T(8,128)S(1)} %bitcast.120), channel_id=1, source_target_pairs={{0,256},{128,384},{256,0},{384,128},{1,257},{129,385},{257,1},{385... | collective-permute-start | bytes 40136 | tf_op jit(solution)/shard_map/ppermute | solution.py:41
  78.4 6.4 %collective-permute-start.9 = (f32[8,418]{1,0:T(8,128)S(1)}, f32[8,418]{1,0:T(8,128)S(1)}, u32[]{:S(2)}, u32[]{:S(2)}) collective-permute-start(f32[8,418]{1,0:T(8,128)S(1)} %bitcast.119), channel_id=1, source_target_pairs={{0,128},{128,256},{256,384},{384,0},{1,129},{129,257},{257,385},{3... | collective-permute-start | bytes 40136 | tf_op jit(solution)/shard_map/ppermute | solution.py:41
  124.3 12.7 %copy-start.4 = (s32[5]{0:T(128)S(1)}, s32[5]{0:T(128)}, u32[]{:S(2)}) copy-start(s32[5]{0:T(128)} %constant.214.clone) | copy-start | bytes 64
  124.3 12.8 %copy-start.2 = (s32[2]{0:T(128)S(1)}, s32[2]{0:T(128)}, u32[]{:S(2)}) copy-start(s32[2]{0:T(128)} %constant.213.clone) | copy-start | bytes 28
  134.0 12.9 %collective-permute-start.10 = (bf16[8,320,512]{2,1,0:T(8,128)(2,1)}, bf16[8,320,512]{2,1,0:T(8,128)(2,1)}, u32[]{:S(2)}, u32[]{:S(2)}) collective-permute-start(bf16[8,320,512]{2,1,0:T(8,128)(2,1)} %get-tuple-element.20), channel_id=1, source_target_pairs={{0,1},{1,0},{2,3},{3,2},{4,5},{5,4},{6,7},{7,6},{8,9},{9,8},{10,11... | collective-permute-start | bytes 7864328 | tf_op jit(solution)/shard_map/partial/ppermute | solution.py:259
  149.2 26.8 %collective-permute-start.11 = (f16[760,128]{1,0:T(8,128)(2,1)S(1)}, f16[760,128]{1,0:T(8,128)(2,1)S(1)}, u32[]{:S(2)}, u32[]{:S(2)}) collective-permute-start(f16[760,128]{1,0:T(8,128)(2,1)S(1)} %convert_bitcast_fusion), channel_id=1, source_target_pairs={{0,8},{2,10},{4,12},{6,14},{8,0},{10,2},{12,4},{14,6},{1,9},{3,11}... | collective-permute-start | bytes 583688 | tf_op jit(solution)/shard_map/ppermute | solution.py:276
  154.3 23.6 %collective-permute-start.12 = (f16[760,128]{1,0:T(8,128)(2,1)S(1)}, f16[760,128]{1,0:T(8,128)(2,1)S(1)}, u32[]{:S(2)}, u32[]{:S(2)}) collective-permute-start(f16[760,128]{1,0:T(8,128)(2,1)S(1)} %get-tuple-element.33), channel_id=1, source_target_pairs={{0,6},{2,8},{4,10},{6,12},{8,14},{10,0},{12,2},{14,4},{1,7},{3,9},... | collective-permute-start | bytes 583688 | tf_op jit(solution)/shard_map/ppermute | solution.py:276
  156.6 24.9 %collective-permute-start.13 = (f16[760,128]{1,0:T(8,128)(2,1)S(1)}, f16[760,128]{1,0:T(8,128)(2,1)S(1)}, u32[]{:S(2)}, u32[]{:S(2)}) collective-permute-start(f16[760,128]{1,0:T(8,128)(2,1)S(1)} %get-tuple-element.34), channel_id=1, source_target_pairs={{0,10},{2,12},{4,14},{6,0},{8,2},{10,4},{12,6},{14,8},{1,11},{3,13... | collective-permute-start | bytes 583688 | tf_op jit(solution)/shard_map/ppermute | solution.py:276
  168.7 14.9 %collective-permute-start.14 = (f16[760,128]{1,0:T(8,128)(2,1)S(1)}, f16[760,128]{1,0:T(8,128)(2,1)S(1)}, u32[]{:S(2)}, u32[]{:S(2)}) collective-permute-start(f16[760,128]{1,0:T(8,128)(2,1)S(1)} %get-tuple-element.25), channel_id=1, source_target_pairs={{0,4},{2,6},{4,8},{6,10},{8,12},{10,14},{12,0},{14,2},{1,5},{3,7},... | collective-permute-start | bytes 583688 | tf_op jit(solution)/shard_map/ppermute | solution.py:276
  172.6 11.0 %collective-permute-start.17 = (f16[760,128]{1,0:T(8,128)(2,1)S(1)}, f16[760,128]{1,0:T(8,128)(2,1)S(1)}, u32[]{:S(2)}, u32[]{:S(2)}) collective-permute-start(f16[760,128]{1,0:T(8,128)(2,1)S(1)} %get-tuple-element.26), channel_id=1, source_target_pairs={{0,14},{2,0},{4,2},{6,4},{8,6},{10,8},{12,10},{14,12},{1,15},{3,1}... | collective-permute-start | bytes 583688 | tf_op jit(solution)/shard_map/ppermute | solution.py:276
  176.0 13.0 %collective-permute-start.16 = (f16[760,128]{1,0:T(8,128)(2,1)S(1)}, f16[760,128]{1,0:T(8,128)(2,1)S(1)}, u32[]{:S(2)}, u32[]{:S(2)}) collective-permute-start(f16[760,128]{1,0:T(8,128)(2,1)S(1)} %get-tuple-element.27), channel_id=1, source_target_pairs={{0,2},{2,4},{4,6},{6,8},{8,10},{10,12},{12,14},{14,0},{1,3},{3,5},... | collective-permute-start | bytes 583688 | tf_op jit(solution)/shard_map/ppermute | solution.py:276
  177.9 12.0 %collective-permute-start.15 = (f16[760,128]{1,0:T(8,128)(2,1)S(1)}, f16[760,128]{1,0:T(8,128)(2,1)S(1)}, u32[]{:S(2)}, u32[]{:S(2)}) collective-permute-start(f16[760,128]{1,0:T(8,128)(2,1)S(1)} %get-tuple-element.28), channel_id=1, source_target_pairs={{0,12},{2,14},{4,0},{6,2},{8,4},{10,6},{12,8},{14,10},{1,13},{3,15... | collective-permute-start | bytes 583688 | tf_op jit(solution)/shard_map/ppermute | solution.py:276
  (2 other events, 10.1 us)
Sparse Core Ops, SparseCore 0:
  10.5 110.3 all-gather.1

commit v6 on v5

--- a/solution.py
+++ b/solution.py
@@ -13,7 +13,7 @@
 CAP = 10
 GROUP = 8
 TALL = 760
-STEPS = ((4,), (3, 5), (2, 6, 1, 7, 0))
+STEPS = ((4, 3, 5), (2, 6, 1, 7, 0))
 VMEM = 60 * 2**20
 
 sharpness_divisor = 0.7

time: 238 us -> 236 us (level)
    pallas_call x3 -> x2, Pallas kernels: 10.9 us -> 9.81 us  [partial_scores(): pl.pallas_call(partial_kernel, grid_spec=pltpu.PrefetchScalarGridSpec(num...]
  transfers between devices with their start and end apart: 21 -> 21, of which waited for: 9 -> 8; matrix products, arithmetic and copies ran while one was open for 3% -> 3% of each run, Pallas kernels for 11% -> 10%
where the time goes in v6:
time: 236 us; the launch traced here: 235 us
  starting transfers between devices  84.2 us (36%)
  waiting for transfers between devices  58.5 us (25%)
  blocking collectives  35.3 us (15%)
  Pallas kernels  28.2 us (12%)
  between operations  14.1 us (6%)
  local copies, waits for them, and re-layouts  9.44 us (4%)
  other arithmetic  4.87 us (2%)
    ppermute x10, starting transfers between devices, by_steps(): lax.ppermute(turned[step], axis, [(i, (i + step) % count) for i in range(...  40.9 us
    all_to_all x2, blocking collectives, exchange(): return lax.all_to_all(value, axis, split_axis=0, concat_axis=0, tiled=True)  35.3 us
    all_gather x1, waiting for transfers between devices, per_device(): everyone = lax.all_gather(both, SEQ, axis=0, tiled=True)  33.9 us
    ppermute x7, starting transfers between devices, per_device(): lax.ppermute(sent_part, 'y', [(k, (k + step) % 8) for k in range(8)])  23.4 us
    all_to_all x2, starting transfers between devices, exchange(): return lax.all_to_all(value, axis, split_axis=0, concat_axis=0, tiled=True)  16.9 us
    pallas_call x2, Pallas kernels, partial_scores(): pl.pallas_call(partial_kernel, grid_spec=pltpu.PrefetchScalarGridSpec(num...  9.81 us
    pallas_call x1, Pallas kernels, pick_rows(): pl.pallas_call(rows_kernel, grid_spec=pltpu.PrefetchScalarGridSpec(num_sc...  9.64 us
    all_to_all x2, waiting for transfers between devices, exchange(): return lax.all_to_all(value, axis, split_axis=0, concat_axis=0, tiled=True)  8.96 us
  transfers between devices with their start and end apart: 21, of which 8 were waited for; matrix products, arithmetic and copies ran while one was open for 3% of the time, Pallas kernels for 10%

profile of v6, /device:TPU:1, one launch (start us, length us, event | category | flops | bytes accessed | tf_op | source)
XLA Modules:
  0.0 234.9 jit_solution(1882268880709679260)
XLA Ops:
  8.3 10.1 %all-to-all-start = ((f32[16,2,128]{2,1,0:T(2,128)}), f32[16,2,128]{2,1,0:T(2,128)S(1)}, u32[]{:S(2)}, u32[]{:S(2)}) async-start(f32[16,2,128]{2,1,0:T(2,128)} %get-tuple-element.13), calls=%async_computation | async-start | bytes 32768 | tf_op jit(solution)/shard_map/all_to_all | solution.py:28
  19.3 7.1 %split_head.1 = bf16[8,304,1024]{2,1,0:T(8,128)(2,1)} custom-call(bf16[297,8192]{1,0:T(8,128)(2,1)} %head_ref.1), custom_call_target="tpu_custom_call" | custom-call | tf_op jit(solution)/shard_map/split_head/pallas_call | solution.py:80
  26.4 6.7 %all-to-all-start.1 = ((bf16[8,304,1024]{2,1,0:T(8,128)(2,1)}), bf16[8,304,1024]{2,1,0:T(8,128)(2,1)}, u32[]{:S(2)}, u32[]{:S(2)}) async-start(bf16[8,304,1024]{2,1,0:T(8,128)(2,1)} %split_head.1), calls=%async_computation.1 | async-start | bytes 9961472 | tf_op jit(solution)/shard_map/all_to_all | solution.py:28
  35.9 9.2 %collective-permute-start = (f32[4,418]{1,0:T(4,128)S(1)}, f32[4,418]{1,0:T(4,128)S(1)}, u32[]{:S(2)}, u32[]{:S(2)}) collective-permute-start(f32[4,418]{1,0:T(4,128)S(1)} %get-tuple-element.46), channel_id=1, source_target_pairs={{0,112},{16,0},{32,16},{48,32},{64,48},{80,64},{96,80},{112,96},{1... | collective-permute-start | bytes 20072 | tf_op jit(solution)/shard_map/ppermute | solution.py:41
  48.9 4.5 %collective-permute-start.4 = (f32[4,418]{1,0:T(4,128)S(1)}, f32[4,418]{1,0:T(4,128)S(1)}, u32[]{:S(2)}, u32[]{:S(2)}) collective-permute-start(f32[4,418]{1,0:T(4,128)S(1)} %get-tuple-element.42), channel_id=1, source_target_pairs={{0,48},{16,64},{32,80},{48,96},{64,112},{80,0},{96,16},{112,32},{1... | collective-permute-start | bytes 20072 | tf_op jit(solution)/shard_map/ppermute | solution.py:41
  53.5 5.0 %collective-permute-start.3 = (f32[4,418]{1,0:T(4,128)S(1)}, f32[4,418]{1,0:T(4,128)S(1)}, u32[]{:S(2)}, u32[]{:S(2)}) collective-permute-start(f32[4,418]{1,0:T(4,128)S(1)} %get-tuple-element.43), channel_id=1, source_target_pairs={{0,64},{16,80},{32,96},{48,112},{64,0},{80,16},{96,32},{112,48},{1... | collective-permute-start | bytes 20072 | tf_op jit(solution)/shard_map/ppermute | solution.py:41
  58.4 5.5 %collective-permute-start.1 = (f32[4,418]{1,0:T(4,128)S(1)}, f32[4,418]{1,0:T(4,128)S(1)}, u32[]{:S(2)}, u32[]{:S(2)}) collective-permute-start(f32[4,418]{1,0:T(4,128)S(1)} %get-tuple-element.45), channel_id=1, source_target_pairs={{0,96},{16,112},{32,0},{48,16},{64,32},{80,48},{96,64},{112,80},{1... | collective-permute-start | bytes 20072 | tf_op jit(solution)/shard_map/ppermute | solution.py:41
  64.7 3.7 %collective-permute-start.2 = (f32[4,418]{1,0:T(4,128)S(1)}, f32[4,418]{1,0:T(4,128)S(1)}, u32[]{:S(2)}, u32[]{:S(2)}) collective-permute-start(f32[4,418]{1,0:T(4,128)S(1)} %get-tuple-element.44), channel_id=1, source_target_pairs={{0,80},{16,96},{32,112},{48,0},{64,16},{80,32},{96,48},{112,64},{1... | collective-permute-start | bytes 20072 | tf_op jit(solution)/shard_map/ppermute | solution.py:41
  71.6 4.4 %collective-permute-start.7 = (f32[8,418]{1,0:T(8,128)S(1)}, f32[8,418]{1,0:T(8,128)S(1)}, u32[]{:S(2)}, u32[]{:S(2)}) collective-permute-start(f32[8,418]{1,0:T(8,128)S(1)} %bitcast.120), channel_id=1, source_target_pairs={{0,384},{128,0},{256,128},{384,256},{1,385},{129,1},{257,129},{385... | collective-permute-start | bytes 40136 | tf_op jit(solution)/shard_map/ppermute | solution.py:41
  87.1 33.9 %all-gather.2.cloned.1.call-done.refs_0_.refs_1_.refs_2_.refs_3_.refs_4_.refs_5_.refs_6_.refs_7_.refs_8_.refs_9_.refs_10_.refs_11_.refs_12_.refs_13_.refs_14_.refs_15_ = bf16[8192,512]{1,0:T(8,128)(2,1)} async-done(((bf16[256,512]{1,0:T(8,128)(2,1)}), bf16[8192,512]{1,0:T(8,128)(2,1)}) %all-gather.2.cloned.1.call-update) | async-done | bytes 8388624 | tf_op jit(solution)/shard_map/all_gather | solution.py:206
  121.0 3.4 %copy-done = bf16[8192,512]{1,0:T(8,128)(2,1)S(1)} copy-done((bf16[8192,512]{1,0:T(8,128)(2,1)S(1)}, bf16[8192,512]{1,0:T(8,128)(2,1)}, u32[]{:S(2)}) %copy-start) | copy-done | bytes 8388632
  124.4 9.6 %pick_rows.1 = (bf16[8,320,512]{2,1,0:T(8,128)(2,1)}, bf16[8,320,512]{2,1,0:T(8,128)(2,1)S(1)}) custom-call(s32[64]{0:T(128)S(1)} %reshape.256.unit_ref, bf16[8192,512]{1,0:T(8,128)(2,1)S(1)} %copy-done, bf16[8192,512]{1,0:T(8,128)(2,1)S(1)} %copy-done, bf16[8192,512]{1,0:T(8,128)(2,1)S(1)} %copy-done, bf16[8192,512]{1,0:T(8,128)(2,1)S(1)} %copy-done, ...), custom_call_target="tpu_custom_call" | custom-call | tf_op jit(solution)/shard_map/partial/pick_rows/pallas_call | solution.py:128
  134.0 3.0 %collective-permute-start.10 = (bf16[8,320,512]{2,1,0:T(8,128)(2,1)}, bf16[8,320,512]{2,1,0:T(8,128)(2,1)}, u32[]{:S(2)}, u32[]{:S(2)}) collective-permute-start(bf16[8,320,512]{2,1,0:T(8,128)(2,1)} %get-tuple-element.20), channel_id=1, source_target_pairs={{0,1},{1,0},{2,3},{3,2},{4,5},{5,4},{6,7},{7,6},{8,9},{9,8},{10,11... | collective-permute-start | bytes 7864328 | tf_op jit(solution)/shard_map/partial/ppermute | solution.py:259
  138.0 9.0 %all-to-all-done.1.head_here_ref.head_away_ref = bf16[8,304,1024]{2,1,0:T(8,128)(2,1)} async-done(((bf16[8,304,1024]{2,1,0:T(8,128)(2,1)}), bf16[8,304,1024]{2,1,0:T(8,128)(2,1)}, u32[]{:S(2)}, u32[]{:S(2)}) %all-to-all-start.1) | async-done | bytes 4980768 | tf_op jit(solution)/shard_map/all_to_all | solution.py:28
  146.9 4.0 %partial_scores.2 = f32[3,760,128]{2,1,0:T(8,128)S(1)} custom-call(s32[4]{0:T(128)S(1)} %pad_add_fusion.order_ref, bf16[8,304,1024]{2,1,0:T(8,128)(2,1)} %all-to-all-done.1.head_here_ref.head_away_ref, bf16[8,304,1024]{2,1,0:T(8,128)(2,1)} %all-to-all-done.1.head_here_ref.head_away_ref, bf16[8,320,512]{2,1,0:T(8,128)(2,1)S(1)} %get-tuple-element.19.here_ref, ...), custom_call_target="tpu_custom_call" | custom-call | tf_op jit(solution)/shard_map/partial/partial_scores/pallas_call | solution.py:167
  153.2 5.0 %collective-permute-start.13 = (f16[760,128]{1,0:T(8,128)(2,1)S(1)}, f16[760,128]{1,0:T(8,128)(2,1)S(1)}, u32[]{:S(2)}, u32[]{:S(2)}) collective-permute-start(f16[760,128]{1,0:T(8,128)(2,1)S(1)} %get-tuple-element.30), channel_id=1, source_target_pairs={{0,10},{2,12},{4,14},{6,0},{8,2},{10,4},{12,6},{14,8},{1,11},{3,13... | collective-permute-start | bytes 583688 | tf_op jit(solution)/shard_map/ppermute | solution.py:276
  160.3 5.8 %partial_scores.3 = f32[5,760,128]{2,1,0:T(8,128)S(1)} custom-call(s32[6]{0:T(128)S(1)} %pad_add_fusion.1.order_ref, bf16[8,304,1024]{2,1,0:T(8,128)(2,1)} %all-to-all-done.1.head_here_ref.head_away_ref, bf16[8,304,1024]{2,1,0:T(8,128)(2,1)} %all-to-all-done.1.head_here_ref.head_away_ref, bf16[8,320,512]{2,1,0:T(8,128)(2,1)S(1)} %get-tuple-element.19.here_ref, ...), custom_call_target="tpu_custom_call" | custom-call | tf_op jit(solution)/shard_map/partial/partial_scores/pallas_call | solution.py:167
  166.4 5.0 %collective-permute-start.14 = (f16[760,128]{1,0:T(8,128)(2,1)S(1)}, f16[760,128]{1,0:T(8,128)(2,1)S(1)}, u32[]{:S(2)}, u32[]{:S(2)}) collective-permute-start(f16[760,128]{1,0:T(8,128)(2,1)S(1)} %get-tuple-element.25), channel_id=1, source_target_pairs={{0,4},{2,6},{4,8},{6,10},{8,12},{10,14},{12,0},{14,2},{1,5},{3,7},... | collective-permute-start | bytes 583688 | tf_op jit(solution)/shard_map/ppermute | solution.py:276
  171.5 3.4 %collective-permute-start.17 = (f16[760,128]{1,0:T(8,128)(2,1)S(1)}, f16[760,128]{1,0:T(8,128)(2,1)S(1)}, u32[]{:S(2)}, u32[]{:S(2)}) collective-permute-start(f16[760,128]{1,0:T(8,128)(2,1)S(1)} %get-tuple-element.26), channel_id=1, source_target_pairs={{0,14},{2,0},{4,2},{6,4},{8,6},{10,8},{12,10},{14,12},{1,15},{3,1}... | collective-permute-start | bytes 583688 | tf_op jit(solution)/shard_map/ppermute | solution.py:276
  176.9 3.9 %collective-permute-start.15 = (f16[760,128]{1,0:T(8,128)(2,1)S(1)}, f16[760,128]{1,0:T(8,128)(2,1)S(1)}, u32[]{:S(2)}, u32[]{:S(2)}) collective-permute-start(f16[760,128]{1,0:T(8,128)(2,1)S(1)} %get-tuple-element.28), channel_id=1, source_target_pairs={{0,12},{2,14},{4,0},{6,2},{8,4},{10,6},{12,8},{14,10},{1,13},{3,15... | collective-permute-start | bytes 583688 | tf_op jit(solution)/shard_map/ppermute | solution.py:276
  180.8 3.3 %collective-permute-done.14 = f16[760,128]{1,0:T(8,128)(2,1)S(1)} collective-permute-done((f16[760,128]{1,0:T(8,128)(2,1)S(1)}, f16[760,128]{1,0:T(8,128)(2,1)S(1)}, u32[]{:S(2)}, u32[]{:S(2)}) %collective-permute-start.14) | collective-permute-done | bytes 194592 | tf_op jit(solution)/shard_map/ppermute | solution.py:276
  184.0 5.6 %collective-permute-done.16 = f16[760,128]{1,0:T(8,128)(2,1)S(1)} collective-permute-done((f16[760,128]{1,0:T(8,128)(2,1)S(1)}, f16[760,128]{1,0:T(8,128)(2,1)S(1)}, u32[]{:S(2)}, u32[]{:S(2)}) %collective-permute-start.16) | collective-permute-done | bytes 194592 | tf_op jit(solution)/shard_map/ppermute | solution.py:276
  191.0 20.1 %all_to_all.24 = f32[32,1,30]{2,1,0:T(1,128)S(1)} all-to-all(f32[32,1,30]{2,1,0:T(1,128)S(1)} %copy.158), channel_id=1, replica_groups=mesh['x'=4,'z'=8,'y'=8,'core'=2] {'x','z'}, dimensions={0} | all-to-all | bytes 7680 | tf_op jit(solution)/shard_map/all_to_all | solution.py:28
  212.2 15.2 %all_to_all.25 = f32[16,3,128]{2,1,0:T(4,128)S(1)} all-to-all(f32[16,3,128]{2,1,0:T(4,128)S(1)} %broadcast_in_dim.146), channel_id=1, replica_groups=mesh['x'=4,'z'=8,'y'=8,'core'=2] {'core','y'}, dimensions={0} | all-to-all | bytes 49152 | tf_op jit(solution)/shard_map/all_to_all | solution.py:28
  (154 shorter events, 34.5 us)
Async XLA Ops:
  6.5 114.4 %all-gather.2.cloned.1.call-start = ((), (), s32[]{:S(2)}) async-start(), calls=%async_computation.4 | async-start | bytes 8650752 | tf_op jit(solution)/shard_map/all_gather | solution.py:206
  8.3 18.1 %all-to-all-start = ((f32[16,2,128]{2,1,0:T(2,128)}), f32[16,2,128]{2,1,0:T(2,128)S(1)}, u32[]{:S(2)}, u32[]{:S(2)}) async-start(f32[16,2,128]{2,1,0:T(2,128)} %get-tuple-element.13), calls=%async_computation | async-start | bytes 32768 | tf_op jit(solution)/shard_map/all_to_all | solution.py:28
  26.4 6.8 %copy-start.2 = (s32[128]{0:T(128)S(1)}, s32[128]{0:T(128)}, u32[]{:S(2)}) copy-start(s32[128]{0:T(128)} %param.16) | copy-start | bytes 1540
  26.4 120.5 %all-to-all-start.1 = ((bf16[8,304,1024]{2,1,0:T(8,128)(2,1)}), bf16[8,304,1024]{2,1,0:T(8,128)(2,1)}, u32[]{:S(2)}, u32[]{:S(2)}) async-start(bf16[8,304,1024]{2,1,0:T(8,128)(2,1)} %split_head.1), calls=%async_computation.1 | async-start | bytes 9961472 | tf_op jit(solution)/shard_map/all_to_all | solution.py:28
  35.9 22.5 %collective-permute-start = (f32[4,418]{1,0:T(4,128)S(1)}, f32[4,418]{1,0:T(4,128)S(1)}, u32[]{:S(2)}, u32[]{:S(2)}) collective-permute-start(f32[4,418]{1,0:T(4,128)S(1)} %get-tuple-element.46), channel_id=1, source_target_pairs={{0,112},{16,0},{32,16},{48,32},{64,48},{80,64},{96,80},{112,96},{1... | collective-permute-start | bytes 20072 | tf_op jit(solution)/shard_map/ppermute | solution.py:41
  45.1 26.2 %collective-permute-start.6 = (f32[4,418]{1,0:T(4,128)S(1)}, f32[4,418]{1,0:T(4,128)S(1)}, u32[]{:S(2)}, u32[]{:S(2)}) collective-permute-start(f32[4,418]{1,0:T(4,128)S(1)} %get-tuple-element.40), channel_id=1, source_target_pairs={{0,16},{16,32},{32,48},{48,64},{64,80},{80,96},{96,112},{112,0},{1... | collective-permute-start | bytes 20072 | tf_op jit(solution)/shard_map/ppermute | solution.py:41
  47.0 24.3 %collective-permute-start.5 = (f32[4,418]{1,0:T(4,128)S(1)}, f32[4,418]{1,0:T(4,128)S(1)}, u32[]{:S(2)}, u32[]{:S(2)}) collective-permute-start(f32[4,418]{1,0:T(4,128)S(1)} %get-tuple-element.41), channel_id=1, source_target_pairs={{0,32},{16,48},{32,64},{48,80},{64,96},{80,112},{96,0},{112,16},{1... | collective-permute-start | bytes 20072 | tf_op jit(solution)/shard_map/ppermute | solution.py:41
  48.9 22.3 %collective-permute-start.4 = (f32[4,418]{1,0:T(4,128)S(1)}, f32[4,418]{1,0:T(4,128)S(1)}, u32[]{:S(2)}, u32[]{:S(2)}) collective-permute-start(f32[4,418]{1,0:T(4,128)S(1)} %get-tuple-element.42), channel_id=1, source_target_pairs={{0,48},{16,64},{32,80},{48,96},{64,112},{80,0},{96,16},{112,32},{1... | collective-permute-start | bytes 20072 | tf_op jit(solution)/shard_map/ppermute | solution.py:41
  53.5 17.8 %collective-permute-start.3 = (f32[4,418]{1,0:T(4,128)S(1)}, f32[4,418]{1,0:T(4,128)S(1)}, u32[]{:S(2)}, u32[]{:S(2)}) collective-permute-start(f32[4,418]{1,0:T(4,128)S(1)} %get-tuple-element.43), channel_id=1, source_target_pairs={{0,64},{16,80},{32,96},{48,112},{64,0},{80,16},{96,32},{112,48},{1... | collective-permute-start | bytes 20072 | tf_op jit(solution)/shard_map/ppermute | solution.py:41
  58.4 6.3 %collective-permute-start.1 = (f32[4,418]{1,0:T(4,128)S(1)}, f32[4,418]{1,0:T(4,128)S(1)}, u32[]{:S(2)}, u32[]{:S(2)}) collective-permute-start(f32[4,418]{1,0:T(4,128)S(1)} %get-tuple-element.45), channel_id=1, source_target_pairs={{0,96},{16,112},{32,0},{48,16},{64,32},{80,48},{96,64},{112,80},{1... | collective-permute-start | bytes 20072 | tf_op jit(solution)/shard_map/ppermute | solution.py:41
  64.7 6.6 %collective-permute-start.2 = (f32[4,418]{1,0:T(4,128)S(1)}, f32[4,418]{1,0:T(4,128)S(1)}, u32[]{:S(2)}, u32[]{:S(2)}) collective-permute-start(f32[4,418]{1,0:T(4,128)S(1)} %get-tuple-element.44), channel_id=1, source_target_pairs={{0,80},{16,96},{32,112},{48,0},{64,16},{80,32},{96,48},{112,64},{1... | collective-permute-start | bytes 20072 | tf_op jit(solution)/shard_map/ppermute | solution.py:41
  71.6 10.1 %collective-permute-start.7 = (f32[8,418]{1,0:T(8,128)S(1)}, f32[8,418]{1,0:T(8,128)S(1)}, u32[]{:S(2)}, u32[]{:S(2)}) collective-permute-start(f32[8,418]{1,0:T(8,128)S(1)} %bitcast.120), channel_id=1, source_target_pairs={{0,384},{128,0},{256,128},{384,256},{1,385},{129,1},{257,129},{385... | collective-permute-start | bytes 40136 | tf_op jit(solution)/shard_map/ppermute | solution.py:41
  76.0 6.7 %collective-permute-start.8 = (f32[8,418]{1,0:T(8,128)S(1)}, f32[8,418]{1,0:T(8,128)S(1)}, u32[]{:S(2)}, u32[]{:S(2)}) collective-permute-start(f32[8,418]{1,0:T(8,128)S(1)} %bitcast.119), channel_id=1, source_target_pairs={{0,256},{128,384},{256,0},{384,128},{1,257},{129,385},{257,1},{385... | collective-permute-start | bytes 40136 | tf_op jit(solution)/shard_map/ppermute | solution.py:41
  78.5 6.4 %collective-permute-start.9 = (f32[8,418]{1,0:T(8,128)S(1)}, f32[8,418]{1,0:T(8,128)S(1)}, u32[]{:S(2)}, u32[]{:S(2)}) collective-permute-start(f32[8,418]{1,0:T(8,128)S(1)} %bitcast.118), channel_id=1, source_target_pairs={{0,128},{128,256},{256,384},{384,0},{1,129},{129,257},{257,385},{3... | collective-permute-start | bytes 40136 | tf_op jit(solution)/shard_map/ppermute | solution.py:41
  124.4 12.7 %copy-start.4 = (s32[5]{0:T(128)S(1)}, s32[5]{0:T(128)}, u32[]{:S(2)}) copy-start(s32[5]{0:T(128)} %constant.196.clone) | copy-start | bytes 64
  124.4 12.8 %copy-start.3 = (s32[3]{0:T(128)S(1)}, s32[3]{0:T(128)}, u32[]{:S(2)}) copy-start(s32[3]{0:T(128)} %constant.195.clone) | copy-start | bytes 40
  134.0 12.9 %collective-permute-start.10 = (bf16[8,320,512]{2,1,0:T(8,128)(2,1)}, bf16[8,320,512]{2,1,0:T(8,128)(2,1)}, u32[]{:S(2)}, u32[]{:S(2)}) collective-permute-start(bf16[8,320,512]{2,1,0:T(8,128)(2,1)} %get-tuple-element.20), channel_id=1, source_target_pairs={{0,1},{1,0},{2,3},{3,2},{4,5},{5,4},{6,7},{7,6},{8,9},{9,8},{10,11... | collective-permute-start | bytes 7864328 | tf_op jit(solution)/shard_map/partial/ppermute | solution.py:259
  151.2 23.7 %collective-permute-start.11 = (f16[760,128]{1,0:T(8,128)(2,1)S(1)}, f16[760,128]{1,0:T(8,128)(2,1)S(1)}, u32[]{:S(2)}, u32[]{:S(2)}) collective-permute-start(f16[760,128]{1,0:T(8,128)(2,1)S(1)} %get-tuple-element.29), channel_id=1, source_target_pairs={{0,8},{2,10},{4,12},{6,14},{8,0},{10,2},{12,4},{14,6},{1,9},{3,11}... | collective-permute-start | bytes 583688 | tf_op jit(solution)/shard_map/ppermute | solution.py:276
  153.2 23.6 %collective-permute-start.13 = (f16[760,128]{1,0:T(8,128)(2,1)S(1)}, f16[760,128]{1,0:T(8,128)(2,1)S(1)}, u32[]{:S(2)}, u32[]{:S(2)}) collective-permute-start(f16[760,128]{1,0:T(8,128)(2,1)S(1)} %get-tuple-element.30), channel_id=1, source_target_pairs={{0,10},{2,12},{4,14},{6,0},{8,2},{10,4},{12,6},{14,8},{1,11},{3,13... | collective-permute-start | bytes 583688 | tf_op jit(solution)/shard_map/ppermute | solution.py:276
  158.3 22.5 %collective-permute-start.12 = (f16[760,128]{1,0:T(8,128)(2,1)S(1)}, f16[760,128]{1,0:T(8,128)(2,1)S(1)}, u32[]{:S(2)}, u32[]{:S(2)}) collective-permute-start(f16[760,128]{1,0:T(8,128)(2,1)S(1)} %get-tuple-element.31), channel_id=1, source_target_pairs={{0,6},{2,8},{4,10},{6,12},{8,14},{10,0},{12,2},{14,4},{1,7},{3,9},... | collective-permute-start | bytes 583688 | tf_op jit(solution)/shard_map/ppermute | solution.py:276
  166.4 17.6 %collective-permute-start.14 = (f16[760,128]{1,0:T(8,128)(2,1)S(1)}, f16[760,128]{1,0:T(8,128)(2,1)S(1)}, u32[]{:S(2)}, u32[]{:S(2)}) collective-permute-start(f16[760,128]{1,0:T(8,128)(2,1)S(1)} %get-tuple-element.25), channel_id=1, source_target_pairs={{0,4},{2,6},{4,8},{6,10},{8,12},{10,14},{12,0},{14,2},{1,5},{3,7},... | collective-permute-start | bytes 583688 | tf_op jit(solution)/shard_map/ppermute | solution.py:276
  171.5 12.6 %collective-permute-start.17 = (f16[760,128]{1,0:T(8,128)(2,1)S(1)}, f16[760,128]{1,0:T(8,128)(2,1)S(1)}, u32[]{:S(2)}, u32[]{:S(2)}) collective-permute-start(f16[760,128]{1,0:T(8,128)(2,1)S(1)} %get-tuple-element.26), channel_id=1, source_target_pairs={{0,14},{2,0},{4,2},{6,4},{8,6},{10,8},{12,10},{14,12},{1,15},{3,1}... | collective-permute-start | bytes 583688 | tf_op jit(solution)/shard_map/ppermute | solution.py:276
  174.9 14.7 %collective-permute-start.16 = (f16[760,128]{1,0:T(8,128)(2,1)S(1)}, f16[760,128]{1,0:T(8,128)(2,1)S(1)}, u32[]{:S(2)}, u32[]{:S(2)}) collective-permute-start(f16[760,128]{1,0:T(8,128)(2,1)S(1)} %get-tuple-element.27), channel_id=1, source_target_pairs={{0,2},{2,4},{4,6},{6,8},{8,10},{10,12},{12,14},{14,0},{1,3},{3,5},... | collective-permute-start | bytes 583688 | tf_op jit(solution)/shard_map/ppermute | solution.py:276
  176.9 12.8 %collective-permute-start.15 = (f16[760,128]{1,0:T(8,128)(2,1)S(1)}, f16[760,128]{1,0:T(8,128)(2,1)S(1)}, u32[]{:S(2)}, u32[]{:S(2)}) collective-permute-start(f16[760,128]{1,0:T(8,128)(2,1)S(1)} %get-tuple-element.28), channel_id=1, source_target_pairs={{0,12},{2,14},{4,0},{6,2},{8,4},{10,6},{12,8},{14,10},{1,13},{3,15... | collective-permute-start | bytes 583688 | tf_op jit(solution)/shard_map/ppermute | solution.py:276
  (2 other events, 10.1 us)
Sparse Core Ops, SparseCore 0:
  10.5 110.3 all-gather.1
